TPU v7x, 256 devices: a whole 4x4x8 slice. The times are simulated.
256 devices in a mesh: pipe: 8 (over x, core), tensor: 32 (over y, z).
Axes of the slice: x: 4, y: 4, z: 8, core: 2. Of those that a mesh axis runs over, the one named last changes fastest.
Arguments:
- x_in: bfloat16 [4, 64, 7168], P(None, None, 'tensor'), may hold values from -6 to 6
- cotangent: bfloat16 [4, 64, 7168], P(None, None, 'tensor'), may hold values from -6 to 6
- w_in: bfloat16 [8, 6, 224, 28672], P('pipe', None, None, 'tensor'), may hold values from -0.15625 to 0.15625
- w_out: bfloat16 [8, 6, 896, 7168], P('pipe', None, None, 'tensor'), may hold values from -0.078125 to 0.078125
Outputs:
- grad_acts: bfloat16 [8, 4, 64, 7168], P('pipe', None, None, 'tensor')
- grad_w_in: bfloat16 [8, 6, 224, 28672], P('pipe', None, None, 'tensor')
- grad_w_out: bfloat16 [8, 6, 896, 7168], P('pipe', None, None, 'tensor')
All inputs are finite; a program needn't handle non-finite values.
Results may differ from a plain program's by a relative error of at most 0.04.
Values may be sent and summed in bfloat16 or wider, within the bound.
No kernel may reach another device: no remote copies, remote signals or barrier semaphores. Data moves between devices by JAX's collectives and lax.ppermute only.
A program may use at most 64 MiB of HBM per device.

v0:
```python
import jax
import jax.numpy as jnp
from jax import lax
from jax.sharding import PartitionSpec as P


def from_partner(value, axis, apart):
    return lax.ppermute(value, axis, [(i, i ^ 1 << apart) for i in range(lax.axis_size(axis))])


def from_behind(block, axis, distance):
    devices = range(lax.axis_size(axis))
    route = [(i - distance, i) for i in devices if i - distance in devices]
    return lax.ppermute(block, axis, route)


def gelu_value(values):
    return jax.nn.gelu(values, approximate=True)


def gelu_slope(preact):
    result, pullback = jax.vjp(gelu_value, preact)
    return pullback(jnp.ones_like(preact))[0]


def store_slot(buffer, update, slot_no, active):
    previous = lax.dynamic_index_in_dim(buffer, slot_no, 0, keepdims=False)
    chosen = jnp.where(active, update, previous)
    return lax.dynamic_update_index_in_dim(buffer, chosen, slot_no, 0)


def body(x_in, cotangent, w_in, w_out):
    levels = lax.axis_size("tensor").bit_length() - 1
    sections = lax.axis_size("pipe")
    my_section = lax.axis_index("pipe")
    batches, tok_rows, in_slab = x_in.shape
    w_first = w_in[0]
    w_second = w_out[0]
    n_terms = levels + 1
    hid_slab = w_first.shape[2]
    n_steps = batches + sections - 1
    hidden_start = jnp.zeros((batches, n_terms, tok_rows, hid_slab), jnp.bfloat16)

    def forward_step(moment, carried):
        incoming, near_store, hidden_store, preact_store = carried
        micro_idx = moment - my_section
        active = (micro_idx >= 0) & (micro_idx < batches)
        slot_no = jnp.clip(micro_idx, 0, batches - 1)
        loaded = lax.dynamic_index_in_dim(x_in, slot_no, 0, keepdims=False)
        inputs = jnp.where(my_section == 0, loaded, incoming)
        nearby = [inputs]
        for level in range(levels):
            nearby.append(from_partner(inputs, "tensor", level))
        nearby = jnp.stack(nearby)
        preact = jnp.einsum("ktd,kdf->tf", nearby, w_first, preferred_element_type=jnp.float32)
        hidden = gelu_value(preact).astype(jnp.bfloat16)
        hid_near = [hidden]
        for level in range(levels):
            hid_near.append(from_partner(hidden, "tensor", level))
        hid_near = jnp.stack(hid_near)
        mixing = jnp.einsum("ktf,kfd->td", hid_near, w_second, preferred_element_type=jnp.float32)
        layer_out = (inputs.astype(jnp.float32) + mixing).astype(jnp.bfloat16)
        near_store = store_slot(near_store, nearby, slot_no, active)
        hidden_store = store_slot(hidden_store, hid_near, slot_no, active)
        preact_store = store_slot(preact_store, preact, slot_no, active)
        incoming = from_behind(layer_out, "pipe", 1)
        return (incoming, near_store, hidden_store, preact_store)

    start_fwd = (
        jnp.zeros((tok_rows, in_slab), jnp.bfloat16),
        jnp.zeros((batches, n_terms, tok_rows, in_slab), jnp.bfloat16),
        hidden_start,
        jnp.zeros((batches, tok_rows, hid_slab), jnp.float32),
    )
    incoming, near_store, hidden_store, preact_store = lax.fori_loop(
        0, n_steps, forward_step, start_fwd
    )

    def backward_step(moment, carried):
        incoming, grad_store, dpre_store, input_store = carried
        micro_idx = moment - (sections - 1 - my_section)
        active = (micro_idx >= 0) & (micro_idx < batches)
        slot_no = jnp.clip(micro_idx, 0, batches - 1)
        loaded = lax.dynamic_index_in_dim(cotangent, slot_no, 0, keepdims=False)
        gradient = jnp.where(my_section == sections - 1, loaded, incoming)
        preact = lax.dynamic_index_in_dim(preact_store, slot_no, 0, keepdims=False)
        pieces = jnp.einsum(
            "td,kfd->ktf", gradient, w_second, preferred_element_type=jnp.float32
        ).astype(jnp.bfloat16)
        hid_grad = pieces[0].astype(jnp.float32)
        for level in range(levels):
            hid_grad = hid_grad + from_partner(pieces[level + 1], "tensor", level).astype(
                jnp.float32
            )
        dpre = (hid_grad * gelu_slope(preact)).astype(jnp.bfloat16)
        returned = jnp.einsum(
            "tf,kdf->ktd", dpre, w_first, preferred_element_type=jnp.float32
        ).astype(jnp.bfloat16)
        input_grad = gradient.astype(jnp.float32) + returned[0].astype(jnp.float32)
        for level in range(levels):
            input_grad = input_grad + from_partner(returned[level + 1], "tensor", level).astype(
                jnp.float32
            )
        input_grad = input_grad.astype(jnp.bfloat16)
        grad_store = store_slot(grad_store, gradient, slot_no, active)
        dpre_store = store_slot(dpre_store, dpre, slot_no, active)
        input_store = store_slot(input_store, input_grad, slot_no, active)
        incoming = from_behind(input_grad, "pipe", -1)
        return (incoming, grad_store, dpre_store, input_store)

    start_bwd = (
        jnp.zeros((tok_rows, in_slab), jnp.bfloat16),
        jnp.zeros((batches, tok_rows, in_slab), jnp.bfloat16),
        jnp.zeros((batches, tok_rows, hid_slab), jnp.bfloat16),
        jnp.zeros((batches, tok_rows, in_slab), jnp.bfloat16),
    )
    incoming, grad_store, dpre_store, input_store = lax.fori_loop(
        0, n_steps, backward_step, start_bwd
    )
    grad_first = jnp.einsum(
        "mktd,mtf->kdf", near_store, dpre_store, preferred_element_type=jnp.float32
    ).astype(jnp.bfloat16)
    grad_second = jnp.einsum(
        "mktf,mtd->kfd", hidden_store, grad_store, preferred_element_type=jnp.float32
    ).astype(jnp.bfloat16)
    return (input_store[None], grad_first[None], grad_second[None])


def solution(mesh):
    placed = (
        P(None, None, "tensor"),
        P(None, None, "tensor"),
        P("pipe", None, None, "tensor"),
        P("pipe", None, None, "tensor"),
    )
    return jax.shard_map(
        body,
        mesh=mesh,
        in_specs=placed,
        out_specs=(
            P("pipe", None, None, "tensor"),
            P("pipe", None, None, "tensor"),
            P("pipe", None, None, "tensor"),
        ),
        check_vma=False,
    )
```

profile of v0, /device:TPU:1, one launch (start us, length us, event | category | flops | bytes accessed | tf_op | source)
XLA Modules:
  0.0 883.9 jit_solution(4119657938313284446)
XLA Ops:
  3.6 464.8 %while.41 = (s32[]{:T(128)}, bf16[64,224]{1,0:T(8,128)(2,1)S(1)}, bf16[4,6,64,224]{3,2,1,0:T(8,128)(2,1)}, bf16[4,6,64,896]{3,2,1,0:T(8,128)(2,1)}, f32[4,64,896...) while((s32[]{:T(128)}, bf16[64,224]{1,0:T(8,128)(2,1)S(1)}, ...), condition=%wide.region_1.2_spmd, body=%wide.region_0.1_spmd.sunk | while | flops 309342208 | bytes 16982696 | solution.py:75
  41.3 6.8 collective-permute-start.10
  85.4 5.0 collective-permute-start.10
  169.4 4.4 collective-permute-start.10
  210.4 5.2 collective-permute-start.10
  252.8 4.6 collective-permute-start.10
  294.8 4.4 collective-permute-start.10
  336.3 4.5 collective-permute-start.10
  377.6 5.0 collective-permute-start.10
  419.9 4.4 collective-permute-start.10
  461.7 4.3 collective-permute-start.10
  469.9 407.6 %while.42 = (s32[]{:T(128)}, bf16[64,224]{1,0:T(8,128)(2,1)S(1)}, bf16[4,64,224]{2,1,0:T(8,128)(2,1)S(1)}, bf16[4,64,896]{2,1,0:T(8,128)(2,1)}, bf16[4,64,224]{2...) while((s32[]{:T(128)}, bf16[64,224]{1,0:T(8,128)(2,1)S(1)}, ...), condition=%wide.region_3.4_spmd, body=%wide.region_2.3_spmd.sunk | while | flops 310732800 | bytes 21926580 | solution.py:117
  472.6 4.9 collective-permute-start.13
  498.9 4.4 collective-permute-start.21
  540.3 4.8 collective-permute-done.21
  591.8 4.3 collective-permute-done.13
  628.9 4.9 collective-permute-done.13
  666.4 5.3 collective-permute-done.13
  703.5 4.9 collective-permute-done.13
  740.3 4.5 collective-permute-done.13
  744.8 5.2 collective-permute-done.14
  781.5 5.4 collective-permute-done.14
  817.6 6.6 collective-permute-done.14
  853.7 7.0 collective-permute-done.14
  (951 shorter events, 770.0 us)
Async XLA Ops:
  5.0 15.0 %collective-permute-start = (bf16[64,224]{1,0:T(8,128)(2,1)}, bf16[64,224]{1,0:T(8,128)(2,1)}, u32[]{:S(2)}, u32[]{:S(2)}) collective-permute-start(bf16[64,224]{1,0:T(8,128)(2,1)} %get-tuple-element.658), channel_id=1, source_target_pairs={{0,1},{1,0},{2,3},{3,2},{4,5},{5,4},{6,7},{7,6},{8,9},{9,8},{10,11... | collective-permute-start | bytes 86024 | tf_op jit(solution)/shard_map/while/body/eval_jaxpr/ppermute | solution.py:8
  7.4 14.0 %collective-permute-start.1 = (bf16[64,224]{1,0:T(8,128)(2,1)}, bf16[64,224]{1,0:T(8,128)(2,1)}, u32[]{:S(2)}, u32[]{:S(2)}) collective-permute-start(bf16[64,224]{1,0:T(8,128)(2,1)} %get-tuple-element.658), channel_id=1, source_target_pairs={{0,2},{1,3},{2,0},{3,1},{4,6},{5,7},{6,4},{7,5},{8,10},{9,11},{10,... | collective-permute-start | bytes 86024 | tf_op jit(solution)/shard_map/while/body/eval_jaxpr/ppermute | solution.py:8
  10.4 12.3 %collective-permute-start.2 = (bf16[64,224]{1,0:T(8,128)(2,1)}, bf16[64,224]{1,0:T(8,128)(2,1)}, u32[]{:S(2)}, u32[]{:S(2)}) collective-permute-start(bf16[64,224]{1,0:T(8,128)(2,1)} %get-tuple-element.658), channel_id=1, source_target_pairs={{0,4},{1,5},{2,6},{3,7},{4,0},{5,1},{6,2},{7,3},{8,12},{9,13},{10,... | collective-permute-start | bytes 86024 | tf_op jit(solution)/shard_map/while/body/eval_jaxpr/ppermute | solution.py:8
  113.4 11.2 %collective-permute-start.5 = (bf16[64,896]{1,0:T(8,128)(2,1)S(1)}, bf16[64,896]{1,0:T(8,128)(2,1)S(1)}, u32[]{:S(2)}, u32[]{:S(2)}) collective-permute-start(bf16[64,896]{1,0:T(8,128)(2,1)S(1)} %get-tuple-element.659), channel_id=1, source_target_pairs={{0,1},{1,0},{2,3},{3,2},{4,5},{5,4},{6,7},{7,6},{8,9},{9,8},{10,11... | collective-permute-start | bytes 344072 | tf_op jit(solution)/shard_map/while/body/eval_jaxpr/ppermute | solution.py:8
  114.3 11.9 %collective-permute-start.6 = (bf16[64,896]{1,0:T(8,128)(2,1)S(1)}, bf16[64,896]{1,0:T(8,128)(2,1)S(1)}, u32[]{:S(2)}, u32[]{:S(2)}) collective-permute-start(bf16[64,896]{1,0:T(8,128)(2,1)S(1)} %get-tuple-element.659), channel_id=1, source_target_pairs={{0,2},{1,3},{2,0},{3,1},{4,6},{5,7},{6,4},{7,5},{8,10},{9,11},{10,... | collective-permute-start | bytes 344072 | tf_op jit(solution)/shard_map/while/body/eval_jaxpr/ppermute | solution.py:8
  155.2 11.2 %collective-permute-start.5 = (bf16[64,896]{1,0:T(8,128)(2,1)S(1)}, bf16[64,896]{1,0:T(8,128)(2,1)S(1)}, u32[]{:S(2)}, u32[]{:S(2)}) collective-permute-start(bf16[64,896]{1,0:T(8,128)(2,1)S(1)} %get-tuple-element.659), channel_id=1, source_target_pairs={{0,1},{1,0},{2,3},{3,2},{4,5},{5,4},{6,7},{7,6},{8,9},{9,8},{10,11... | collective-permute-start | bytes 344072 | tf_op jit(solution)/shard_map/while/body/eval_jaxpr/ppermute | solution.py:8
  156.0 11.7 %collective-permute-start.6 = (bf16[64,896]{1,0:T(8,128)(2,1)S(1)}, bf16[64,896]{1,0:T(8,128)(2,1)S(1)}, u32[]{:S(2)}, u32[]{:S(2)}) collective-permute-start(bf16[64,896]{1,0:T(8,128)(2,1)S(1)} %get-tuple-element.659), channel_id=1, source_target_pairs={{0,2},{1,3},{2,0},{3,1},{4,6},{5,7},{6,4},{7,5},{8,10},{9,11},{10,... | collective-permute-start | bytes 344072 | tf_op jit(solution)/shard_map/while/body/eval_jaxpr/ppermute | solution.py:8
  196.9 11.1 %collective-permute-start.5 = (bf16[64,896]{1,0:T(8,128)(2,1)S(1)}, bf16[64,896]{1,0:T(8,128)(2,1)S(1)}, u32[]{:S(2)}, u32[]{:S(2)}) collective-permute-start(bf16[64,896]{1,0:T(8,128)(2,1)S(1)} %get-tuple-element.659), channel_id=1, source_target_pairs={{0,1},{1,0},{2,3},{3,2},{4,5},{5,4},{6,7},{7,6},{8,9},{9,8},{10,11... | collective-permute-start | bytes 344072 | tf_op jit(solution)/shard_map/while/body/eval_jaxpr/ppermute | solution.py:8
  238.7 11.1 %collective-permute-start.5 = (bf16[64,896]{1,0:T(8,128)(2,1)S(1)}, bf16[64,896]{1,0:T(8,128)(2,1)S(1)}, u32[]{:S(2)}, u32[]{:S(2)}) collective-permute-start(bf16[64,896]{1,0:T(8,128)(2,1)S(1)} %get-tuple-element.659), channel_id=1, source_target_pairs={{0,1},{1,0},{2,3},{3,2},{4,5},{5,4},{6,7},{7,6},{8,9},{9,8},{10,11... | collective-permute-start | bytes 344072 | tf_op jit(solution)/shard_map/while/body/eval_jaxpr/ppermute | solution.py:8
  239.5 11.6 %collective-permute-start.6 = (bf16[64,896]{1,0:T(8,128)(2,1)S(1)}, bf16[64,896]{1,0:T(8,128)(2,1)S(1)}, u32[]{:S(2)}, u32[]{:S(2)}) collective-permute-start(bf16[64,896]{1,0:T(8,128)(2,1)S(1)} %get-tuple-element.659), channel_id=1, source_target_pairs={{0,2},{1,3},{2,0},{3,1},{4,6},{5,7},{6,4},{7,5},{8,10},{9,11},{10,... | collective-permute-start | bytes 344072 | tf_op jit(solution)/shard_map/while/body/eval_jaxpr/ppermute | solution.py:8
  280.4 11.2 %collective-permute-start.5 = (bf16[64,896]{1,0:T(8,128)(2,1)S(1)}, bf16[64,896]{1,0:T(8,128)(2,1)S(1)}, u32[]{:S(2)}, u32[]{:S(2)}) collective-permute-start(bf16[64,896]{1,0:T(8,128)(2,1)S(1)} %get-tuple-element.659), channel_id=1, source_target_pairs={{0,1},{1,0},{2,3},{3,2},{4,5},{5,4},{6,7},{7,6},{8,9},{9,8},{10,11... | collective-permute-start | bytes 344072 | tf_op jit(solution)/shard_map/while/body/eval_jaxpr/ppermute | solution.py:8
  281.2 11.8 %collective-permute-start.6 = (bf16[64,896]{1,0:T(8,128)(2,1)S(1)}, bf16[64,896]{1,0:T(8,128)(2,1)S(1)}, u32[]{:S(2)}, u32[]{:S(2)}) collective-permute-start(bf16[64,896]{1,0:T(8,128)(2,1)S(1)} %get-tuple-element.659), channel_id=1, source_target_pairs={{0,2},{1,3},{2,0},{3,1},{4,6},{5,7},{6,4},{7,5},{8,10},{9,11},{10,... | collective-permute-start | bytes 344072 | tf_op jit(solution)/shard_map/while/body/eval_jaxpr/ppermute | solution.py:8
  322.2 11.1 %collective-permute-start.5 = (bf16[64,896]{1,0:T(8,128)(2,1)S(1)}, bf16[64,896]{1,0:T(8,128)(2,1)S(1)}, u32[]{:S(2)}, u32[]{:S(2)}) collective-permute-start(bf16[64,896]{1,0:T(8,128)(2,1)S(1)} %get-tuple-element.659), channel_id=1, source_target_pairs={{0,1},{1,0},{2,3},{3,2},{4,5},{5,4},{6,7},{7,6},{8,9},{9,8},{10,11... | collective-permute-start | bytes 344072 | tf_op jit(solution)/shard_map/while/body/eval_jaxpr/ppermute | solution.py:8
  323.0 11.6 %collective-permute-start.6 = (bf16[64,896]{1,0:T(8,128)(2,1)S(1)}, bf16[64,896]{1,0:T(8,128)(2,1)S(1)}, u32[]{:S(2)}, u32[]{:S(2)}) collective-permute-start(bf16[64,896]{1,0:T(8,128)(2,1)S(1)} %get-tuple-element.659), channel_id=1, source_target_pairs={{0,2},{1,3},{2,0},{3,1},{4,6},{5,7},{6,4},{7,5},{8,10},{9,11},{10,... | collective-permute-start | bytes 344072 | tf_op jit(solution)/shard_map/while/body/eval_jaxpr/ppermute | solution.py:8
  405.6 11.1 %collective-permute-start.5 = (bf16[64,896]{1,0:T(8,128)(2,1)S(1)}, bf16[64,896]{1,0:T(8,128)(2,1)S(1)}, u32[]{:S(2)}, u32[]{:S(2)}) collective-permute-start(bf16[64,896]{1,0:T(8,128)(2,1)S(1)} %get-tuple-element.659), channel_id=1, source_target_pairs={{0,1},{1,0},{2,3},{3,2},{4,5},{5,4},{6,7},{7,6},{8,9},{9,8},{10,11... | collective-permute-start | bytes 344072 | tf_op jit(solution)/shard_map/while/body/eval_jaxpr/ppermute | solution.py:8
  406.5 11.7 %collective-permute-start.6 = (bf16[64,896]{1,0:T(8,128)(2,1)S(1)}, bf16[64,896]{1,0:T(8,128)(2,1)S(1)}, u32[]{:S(2)}, u32[]{:S(2)}) collective-permute-start(bf16[64,896]{1,0:T(8,128)(2,1)S(1)} %get-tuple-element.659), channel_id=1, source_target_pairs={{0,2},{1,3},{2,0},{3,1},{4,6},{5,7},{6,4},{7,5},{8,10},{9,11},{10,... | collective-permute-start | bytes 344072 | tf_op jit(solution)/shard_map/while/body/eval_jaxpr/ppermute | solution.py:8
  448.2 11.8 %collective-permute-start.6 = (bf16[64,896]{1,0:T(8,128)(2,1)S(1)}, bf16[64,896]{1,0:T(8,128)(2,1)S(1)}, u32[]{:S(2)}, u32[]{:S(2)}) collective-permute-start(bf16[64,896]{1,0:T(8,128)(2,1)S(1)} %get-tuple-element.659), channel_id=1, source_target_pairs={{0,2},{1,3},{2,0},{3,1},{4,6},{5,7},{6,4},{7,5},{8,10},{9,11},{10,... | collective-permute-start | bytes 344072 | tf_op jit(solution)/shard_map/while/body/eval_jaxpr/ppermute | solution.py:8
  700.7 11.7 %collective-permute-start.14 = (bf16[64,896]{1,0:T(8,128)(2,1)S(1)}, bf16[64,896]{1,0:T(8,128)(2,1)S(1)}, u32[]{:S(2)}, u32[]{:S(2)}) collective-permute-start(bf16[64,896]{1,0:T(8,128)(2,1)S(1)} %get-tuple-element.678), channel_id=1, source_target_pairs={{0,2},{1,3},{2,0},{3,1},{4,6},{5,7},{6,4},{7,5},{8,10},{9,11},{10,... | collective-permute-start | bytes 344072 | tf_op jit(solution)/shard_map/while/body/eval_jaxpr/ppermute | solution.py:8
  737.5 12.5 %collective-permute-start.14 = (bf16[64,896]{1,0:T(8,128)(2,1)S(1)}, bf16[64,896]{1,0:T(8,128)(2,1)S(1)}, u32[]{:S(2)}, u32[]{:S(2)}) collective-permute-start(bf16[64,896]{1,0:T(8,128)(2,1)S(1)} %get-tuple-element.678), channel_id=1, source_target_pairs={{0,2},{1,3},{2,0},{3,1},{4,6},{5,7},{6,4},{7,5},{8,10},{9,11},{10,... | collective-permute-start | bytes 344072 | tf_op jit(solution)/shard_map/while/body/eval_jaxpr/ppermute | solution.py:8
  738.5 11.5 %collective-permute-start.15 = (bf16[64,896]{1,0:T(8,128)(2,1)S(1)}, bf16[64,896]{1,0:T(8,128)(2,1)S(1)}, u32[]{:S(2)}, u32[]{:S(2)}) collective-permute-start(bf16[64,896]{1,0:T(8,128)(2,1)S(1)} %get-tuple-element.679), channel_id=1, source_target_pairs={{0,1},{1,0},{2,3},{3,2},{4,5},{5,4},{6,7},{7,6},{8,9},{9,8},{10,11... | collective-permute-start | bytes 344072 | tf_op jit(solution)/shard_map/while/body/eval_jaxpr/ppermute | solution.py:8
  774.5 12.4 %collective-permute-start.14 = (bf16[64,896]{1,0:T(8,128)(2,1)S(1)}, bf16[64,896]{1,0:T(8,128)(2,1)S(1)}, u32[]{:S(2)}, u32[]{:S(2)}) collective-permute-start(bf16[64,896]{1,0:T(8,128)(2,1)S(1)} %get-tuple-element.678), channel_id=1, source_target_pairs={{0,2},{1,3},{2,0},{3,1},{4,6},{5,7},{6,4},{7,5},{8,10},{9,11},{10,... | collective-permute-start | bytes 344072 | tf_op jit(solution)/shard_map/while/body/eval_jaxpr/ppermute | solution.py:8
  811.2 13.0 %collective-permute-start.14 = (bf16[64,896]{1,0:T(8,128)(2,1)S(1)}, bf16[64,896]{1,0:T(8,128)(2,1)S(1)}, u32[]{:S(2)}, u32[]{:S(2)}) collective-permute-start(bf16[64,896]{1,0:T(8,128)(2,1)S(1)} %get-tuple-element.678), channel_id=1, source_target_pairs={{0,2},{1,3},{2,0},{3,1},{4,6},{5,7},{6,4},{7,5},{8,10},{9,11},{10,... | collective-permute-start | bytes 344072 | tf_op jit(solution)/shard_map/while/body/eval_jaxpr/ppermute | solution.py:8
  812.2 12.0 %collective-permute-start.15 = (bf16[64,896]{1,0:T(8,128)(2,1)S(1)}, bf16[64,896]{1,0:T(8,128)(2,1)S(1)}, u32[]{:S(2)}, u32[]{:S(2)}) collective-permute-start(bf16[64,896]{1,0:T(8,128)(2,1)S(1)} %get-tuple-element.679), channel_id=1, source_target_pairs={{0,1},{1,0},{2,3},{3,2},{4,5},{5,4},{6,7},{7,6},{8,9},{9,8},{10,11... | collective-permute-start | bytes 344072 | tf_op jit(solution)/shard_map/while/body/eval_jaxpr/ppermute | solution.py:8
  847.9 12.7 %collective-permute-start.14 = (bf16[64,896]{1,0:T(8,128)(2,1)S(1)}, bf16[64,896]{1,0:T(8,128)(2,1)S(1)}, u32[]{:S(2)}, u32[]{:S(2)}) collective-permute-start(bf16[64,896]{1,0:T(8,128)(2,1)S(1)} %get-tuple-element.678), channel_id=1, source_target_pairs={{0,2},{1,3},{2,0},{3,1},{4,6},{5,7},{6,4},{7,5},{8,10},{9,11},{10,... | collective-permute-start | bytes 344072 | tf_op jit(solution)/shard_map/while/body/eval_jaxpr/ppermute | solution.py:8
  (243 other events, 2202.9 us)
where the time goes:
time: 897 us; the launch traced here: 884 us
  starting transfers between devices  414 us (46%)
  waiting for transfers between devices  159 us (18%)
  local copies, waits for them, and re-layouts  158 us (18%)
  other arithmetic  83 us (9%)
  matrix products  66.9 us (7%)
    ppermute x220, starting transfers between devices, from_partner(): lax.ppermute(value, axis, [(i, i ^ 1 << apart) for i in range(lax.axis_si...  326 us
    ppermute x220, waiting for transfers between devices, from_partner(): lax.ppermute(value, axis, [(i, i ^ 1 << apart) for i in range(lax.axis_si...  130 us
    while x242, local copies, waits for them, and re-layouts  111 us
    ppermute x22, starting transfers between devices, from_behind(): return lax.ppermute(block, axis, route)  88.2 us
    dynamic_update_slice x66, other arithmetic, store_slot(): return lax.dynamic_update_index_in_dim(buffer, chosen, slot_no, 0)  67.6 us
    ppermute x22, waiting for transfers between devices, from_behind(): return lax.ppermute(block, axis, route)  29 us
    dot_general x11, matrix products, forward_step(): jnp.einsum('ktd,kdf->tf', nearby, w_first, preferred_element_type=jnp.flo...  25.8 us
    another operation x22, local copies, waits for them, and re-layouts, forward_step(): nearby = jnp.stack(nearby)  23.3 us
  transfers between devices with their start and end apart: 242, of which 66 were waited for; matrix products, arithmetic and copies ran while one was open for 20% of the time, Pallas kernels for 0%

commit v1 on v0

v1 whole, which is shorter than its diff:
```python
import functools

import jax
import jax.numpy as jnp
from jax import lax
from jax.experimental import pallas as pl
from jax.experimental.pallas import tpu as pltpu
from jax.sharding import PartitionSpec as P

AXES = ("pipe", "tensor")
GELU_C = 0.7978845608028654
GELU_A = 0.044715
VMEM = pl.BlockSpec(memory_space=pltpu.VMEM)
SMEM = pl.BlockSpec(memory_space=pltpu.SMEM)
F32 = jnp.float32
BF16 = jnp.bfloat16


def partner(index, term):
    return index if term == 0 else index ^ (1 << (term - 1))


def send(value, term, routes):
    width = lax.axis_size("tensor")
    pairs = [
        (a * width + i, b * width + partner(i, term)) for a, b in routes for i in range(width)
    ]
    return lax.ppermute(value, AXES, pairs)


def column_chunks(width):
    return [(start, min(256, width - start)) for start in range(0, width, 256)]


def dot_nn(a, b):
    return lax.dot_general(a, b, (((1,), (0,)), ((), ())), preferred_element_type=F32)


def dot_nt(a, b):
    return lax.dot_general(a, b, (((1,), (1,)), ((), ())), preferred_element_type=F32)


def dot_tn(a, b):
    return lax.dot_general(a, b, (((0,), (0,)), ((), ())), preferred_element_type=F32)


def forward_kernel(n, last, *refs):
    active = refs[0]
    ins = refs[1 : 1 + n]
    first = refs[1 + n]
    second = refs[2 + n : 2 + 2 * n]
    preact, hidden = refs[2 + 2 * n : 4 + 2 * n]
    outs = refs[4 + 2 * n :]

    @pl.when(active[0] == 1)
    def _():
        for start, size in column_chunks(preact.shape[1]):
            cols = slice(start, start + size)
            total = dot_nn(ins[0][...], first[0, :, cols])
            for k in range(1, n):
                total = total + dot_nn(ins[k][...], first[k, :, cols])
            preact[:, cols] = total
            inner = GELU_C * (total + GELU_A * (total * total * total))
            hidden[:, cols] = (0.5 * total * (1.0 + jnp.tanh(inner))).astype(BF16)
        if not last:
            outs[0][...] = ins[0][...].astype(F32) + dot_nt(hidden[...], second[0][...])
            for k in range(1, n):
                outs[k][...] = dot_nt(hidden[...], second[k][...]).astype(BF16)


def backward_kernel(n, *refs):
    active = refs[0]
    ins = refs[1 : 1 + n]
    first = refs[1 + n]
    second = refs[2 + n : 2 + 2 * n]
    preact = refs[2 + 2 * n]
    dpre = refs[3 + 2 * n]
    outs = refs[4 + 2 * n :]

    @pl.when(active[0] == 1)
    def _():
        for start, size in column_chunks(preact.shape[1]):
            cols = slice(start, start + size)
            total = dot_nn(ins[0][...], second[0][:, cols])
            for k in range(1, n):
                total = total + dot_nn(ins[k][...], second[k][:, cols])
            x = preact[:, cols]
            square = x * x
            bent = jnp.tanh(GELU_C * (x + GELU_A * (square * x)))
            slope = 0.5 * (1.0 + bent) + 0.5 * x * (1.0 - bent * bent) * (
                GELU_C * (1.0 + 3.0 * GELU_A * square)
            )
            dpre[:, cols] = (total * slope).astype(BF16)
        outs[0][...] = ins[0][...].astype(F32) + dot_nt(dpre[...], first[0])
        for k in range(1, n):
            outs[k][...] = dot_nt(dpre[...], first[k]).astype(BF16)


def grad_kernel(n, *refs):
    ins = refs[:n]
    dpre = refs[n]
    hiddens = refs[n + 1 : 2 * n + 1]
    grad = refs[2 * n + 1]
    out_first, out_second = refs[2 * n + 2 :]
    for k in range(n):
        out_first[k] = dot_tn(ins[k][...], dpre[...]).astype(BF16)
        out_second[k] = dot_tn(grad[...], hiddens[k][...]).astype(BF16)


def call(kernel, out_shapes, args, flops, touched, flagged=True):
    return pl.pallas_call(
        kernel,
        out_shape=out_shapes,
        in_specs=([SMEM] if flagged else []) + [VMEM] * (len(args) - flagged),
        out_specs=[VMEM] * len(out_shapes),
        cost_estimate=pl.CostEstimate(flops=flops, bytes_accessed=touched, transcendentals=0),
        compiler_params=pltpu.CompilerParams(vmem_limit_bytes=24 * 1024 * 1024),
    )(*args)


def body(x_in, cotangent, w_in, w_out):
    sections = lax.axis_size("pipe")
    n = lax.axis_size("tensor").bit_length()
    me = lax.axis_index("pipe")
    batches, tok_rows, slab = x_in.shape
    tokens = batches * tok_rows
    first = w_in[0]
    owned = jnp.swapaxes(w_out[0], 1, 2)
    hid = first.shape[2]
    shape = jax.ShapeDtypeStruct
    flops = 4 * tokens * n * slab * hid
    touched = 4 * n * slab * hid

    x = x_in.reshape(tokens, slab)
    cot = cotangent.reshape(tokens, slab)
    everyone = [(s, s) for s in range(sections)]
    order = [k for k in (3, 5, 2, 4, 1) if k < n]

    def exchange(values, routes):
        got = {k: send(values[k], k, routes) for k in order}
        return [got[k] for k in range(1, n)]

    ins = [x] + exchange([x] * n, everyone)
    second_0 = [owned[0]] + exchange(owned, [(0, 0)])
    second_r = [owned[0]] + exchange(owned, everyone[1:])
    grads_in = [cot] + exchange([cot] * n, everyone)

    saved_ins = list(ins)
    saved_pre = saved_hid = None
    for layer in range(sections):
        last = layer == sections - 1
        active = (me == layer).astype(jnp.int32).reshape(1)
        second = second_0 if layer == 0 else second_r
        shapes = [shape((tokens, hid), F32), shape((tokens, hid), BF16)]
        if not last:
            shapes += [shape((tokens, slab), F32)] + [shape((tokens, slab), BF16)] * (n - 1)
        preact, hidden, *terms = call(
            functools.partial(forward_kernel, n, last),
            shapes,
            [active] + ins + [first] + second,
            flops // (2 if last else 1),
            touched,
        )
        if layer == 0:
            saved_pre, saved_hid = preact, hidden
        else:
            mine = me == layer
            saved_ins = [jnp.where(mine, a, b) for a, b in zip(ins, saved_ins)]
            saved_pre = jnp.where(mine, preact, saved_pre)
            saved_hid = jnp.where(mine, hidden, saved_hid)
        if last:
            break
        total = terms[0]
        for got in exchange(terms, everyone):
            total = total + got.astype(F32)
        out = total.astype(BF16)
        route = [(layer, layer + 1)]
        ins = exchange([out] * n, route)
        ins = [send(out, 0, route)] + ins

    hiddens = [saved_hid] + exchange([saved_hid] * n, everyone)

    saved_grad = cot
    saved_dpre = saved_out = None
    for layer in reversed(range(sections)):
        active = (me == layer).astype(jnp.int32).reshape(1)
        second = second_0 if layer == 0 else second_r
        dpre, *terms = call(
            functools.partial(backward_kernel, n),
            [shape((tokens, hid), BF16), shape((tokens, slab), F32)]
            + [shape((tokens, slab), BF16)] * (n - 1),
            [active] + grads_in + [first] + second + [saved_pre],
            flops,
            touched,
        )
        total = terms[0]
        for got in exchange(terms, everyone):
            total = total + got.astype(F32)
        out = total.astype(BF16)
        if layer == sections - 1:
            saved_dpre, saved_out = dpre, out
        else:
            mine = me == layer
            saved_grad = jnp.where(mine, grads_in[0], saved_grad)
            saved_dpre = jnp.where(mine, dpre, saved_dpre)
            saved_out = jnp.where(mine, out, saved_out)
        if layer > 0:
            route = [(layer, layer - 1)]
            grads_in = exchange([out] * n, route)
            grads_in = [send(out, 0, route)] + grads_in

    grad_first, grad_second = call(
        functools.partial(grad_kernel, n),
        [shape((n, slab, hid), BF16)] * 2,
        saved_ins + [saved_dpre] + hiddens + [saved_grad],
        flops,
        touched,
        flagged=False,
    )
    acts = saved_out.reshape(batches, tok_rows, slab)
    return acts[None], grad_first[None], jnp.swapaxes(grad_second, 1, 2)[None]


def solution(mesh):
    placed = (
        P(None, None, "tensor"),
        P(None, None, "tensor"),
        P("pipe", None, None, "tensor"),
        P("pipe", None, None, "tensor"),
    )
    return jax.shard_map(
        body,
        mesh=mesh,
        in_specs=placed,
        out_specs=(P("pipe", None, None, "tensor"),) * 3,
        check_vma=False,
    )
```

time: 897 us -> 1320 us (1.47)
  the two profiles are of different devices: /device:TPU:1 before, /device:TPU:5 now
where the time goes in v1:
time: 1320 us; the launch traced here: 1300 us
  starting transfers between devices  1100 us (83%)
  waiting for transfers between devices  108 us (8%)
  local copies, waits for them, and re-layouts  61.3 us (5%)
  Pallas kernels  18.7 us (1%)
    ppermute x184, starting transfers between devices, send(): return lax.ppermute(value, AXES, pairs)  1100 us
    ppermute x184, waiting for transfers between devices, send(): return lax.ppermute(value, AXES, pairs)  108 us
    unnamed x232, local copies, waits for them, and re-layouts  58.2 us
  transfers between devices with their start and end apart: 184, of which 38 were waited for; matrix products, arithmetic and copies ran while one was open for 1% of the time, Pallas kernels for 0%

profile of v1, /device:TPU:5, one launch (start us, length us, event | category | flops | bytes accessed | tf_op | source)
XLA Modules:
  0.0 1300.4 jit_solution(1088266007407500123)
XLA Ops:
  40.5 38.0 %collective-permute-start.9 = (bf16[224,896]{1,0:T(8,128)(2,1)}, bf16[224,896]{1,0:T(8,128)(2,1)S(1)}, u32[]{:S(2)}, u32[]{:S(2)}) collective-permute-start(bf16[224,896]{1,0:T(8,128)(2,1)} %get-tuple-element.235), channel_id=1, source_target_pairs={{32,48},{33,49},{34,50},{35,51},{36,52},{37,53},{38,54},{39,55},{4... | collective-permute-start | bytes 1204232 | tf_op jit(solution)/shard_map/ppermute | solution.py:28
  206.6 23.1 %collective-permute-start.52 = (bf16[256,224]{1,0:T(8,128)(2,1)}, bf16[256,224]{1,0:T(8,128)(2,1)S(1)}, u32[]{:S(2)}, u32[]{:S(2)}) collective-permute-start(bf16[256,224]{1,0:T(8,128)(2,1)} %add_convert_fusion.12), channel_id=1, source_target_pairs={{64,112},{65,113},{66,114},{67,115},{68,116},{69,117},{70,118},{71... | collective-permute-start | bytes 344072 | tf_op jit(solution)/shard_map/ppermute | solution.py:28
  229.8 13.1 %collective-permute-start.51 = (bf16[256,224]{1,0:T(8,128)(2,1)}, bf16[256,224]{1,0:T(8,128)(2,1)}, u32[]{:S(2)}, u32[]{:S(2)}) collective-permute-start(bf16[256,224]{1,0:T(8,128)(2,1)} %add_convert_fusion.12), channel_id=1, source_target_pairs={{64,104},{65,105},{66,106},{67,107},{68,108},{69,109},{70,110},{71... | collective-permute-start | bytes 344072 | tf_op jit(solution)/shard_map/ppermute | solution.py:28
  256.1 13.1 %collective-permute-start.49 = (bf16[256,224]{1,0:T(8,128)(2,1)}, bf16[256,224]{1,0:T(8,128)(2,1)}, u32[]{:S(2)}, u32[]{:S(2)}) collective-permute-start(bf16[256,224]{1,0:T(8,128)(2,1)} %add_convert_fusion.12), channel_id=1, source_target_pairs={{64,98},{65,99},{66,96},{67,97},{68,102},{69,103},{70,100},{71,101... | collective-permute-start | bytes 344072 | tf_op jit(solution)/shard_map/ppermute | solution.py:28
  296.1 14.1 %collective-permute-start.63 = (bf16[256,224]{1,0:T(8,128)(2,1)}, bf16[256,224]{1,0:T(8,128)(2,1)S(1)}, u32[]{:S(2)}, u32[]{:S(2)}) collective-permute-start(bf16[256,224]{1,0:T(8,128)(2,1)} %add_convert_fusion.11), channel_id=1, source_target_pairs={{96,144},{97,145},{98,146},{99,147},{100,148},{101,149},{102,150},... | collective-permute-start | bytes 344072 | tf_op jit(solution)/shard_map/ppermute | solution.py:28
  398.0 15.2 %collective-permute-start.74 = (bf16[256,224]{1,0:T(8,128)(2,1)}, bf16[256,224]{1,0:T(8,128)(2,1)S(1)}, u32[]{:S(2)}, u32[]{:S(2)}) collective-permute-start(bf16[256,224]{1,0:T(8,128)(2,1)} %add_convert_fusion.10), channel_id=1, source_target_pairs={{128,176},{129,177},{130,178},{131,179},{132,180},{133,181},{134,1... | collective-permute-start | bytes 344072 | tf_op jit(solution)/shard_map/ppermute | solution.py:28
  426.3 13.8 %collective-permute-start.72 = (bf16[256,224]{1,0:T(8,128)(2,1)}, bf16[256,224]{1,0:T(8,128)(2,1)}, u32[]{:S(2)}, u32[]{:S(2)}) collective-permute-start(bf16[256,224]{1,0:T(8,128)(2,1)} %add_convert_fusion.10), channel_id=1, source_target_pairs={{128,164},{129,165},{130,166},{131,167},{132,160},{133,161},{134,1... | collective-permute-start | bytes 344072 | tf_op jit(solution)/shard_map/ppermute | solution.py:28
  440.1 13.8 %collective-permute-start.71 = (bf16[256,224]{1,0:T(8,128)(2,1)}, bf16[256,224]{1,0:T(8,128)(2,1)}, u32[]{:S(2)}, u32[]{:S(2)}) collective-permute-start(bf16[256,224]{1,0:T(8,128)(2,1)} %add_convert_fusion.10), channel_id=1, source_target_pairs={{128,162},{129,163},{130,160},{131,161},{132,166},{133,167},{134,1... | collective-permute-start | bytes 344072 | tf_op jit(solution)/shard_map/ppermute | solution.py:28
  453.9 13.8 %collective-permute-start.70 = (bf16[256,224]{1,0:T(8,128)(2,1)}, bf16[256,224]{1,0:T(8,128)(2,1)}, u32[]{:S(2)}, u32[]{:S(2)}) collective-permute-start(bf16[256,224]{1,0:T(8,128)(2,1)} %add_convert_fusion.10), channel_id=1, source_target_pairs={{128,161},{129,160},{130,163},{131,162},{132,165},{133,164},{134,1... | collective-permute-start | bytes 344072 | tf_op jit(solution)/shard_map/ppermute | solution.py:28
  468.3 13.8 %collective-permute-start.69 = (bf16[256,224]{1,0:T(8,128)(2,1)}, bf16[256,224]{1,0:T(8,128)(2,1)S(1)}, u32[]{:S(2)}, u32[]{:S(2)}) collective-permute-start(bf16[256,224]{1,0:T(8,128)(2,1)} %add_convert_fusion.10), channel_id=1, source_target_pairs={{128,160},{129,161},{130,162},{131,163},{132,164},{133,165},{134,1... | collective-permute-start | bytes 344072 | tf_op jit(solution)/shard_map/ppermute | solution.py:28
  520.7 13.5 %collective-permute-start.84 = (bf16[256,224]{1,0:T(8,128)(2,1)}, bf16[256,224]{1,0:T(8,128)(2,1)}, u32[]{:S(2)}, u32[]{:S(2)}) collective-permute-start(bf16[256,224]{1,0:T(8,128)(2,1)} %add_convert_fusion.9), channel_id=1, source_target_pairs={{160,200},{161,201},{162,202},{163,203},{164,204},{165,205},{166,2... | collective-permute-start | bytes 344072 | tf_op jit(solution)/shard_map/ppermute | solution.py:28
  534.2 13.5 %collective-permute-start.83 = (bf16[256,224]{1,0:T(8,128)(2,1)}, bf16[256,224]{1,0:T(8,128)(2,1)}, u32[]{:S(2)}, u32[]{:S(2)}) collective-permute-start(bf16[256,224]{1,0:T(8,128)(2,1)} %add_convert_fusion.9), channel_id=1, source_target_pairs={{160,196},{161,197},{162,198},{163,199},{164,192},{165,193},{166,1... | collective-permute-start | bytes 344072 | tf_op jit(solution)/shard_map/ppermute | solution.py:28
  547.7 13.5 %collective-permute-start.82 = (bf16[256,224]{1,0:T(8,128)(2,1)}, bf16[256,224]{1,0:T(8,128)(2,1)}, u32[]{:S(2)}, u32[]{:S(2)}) collective-permute-start(bf16[256,224]{1,0:T(8,128)(2,1)} %add_convert_fusion.9), channel_id=1, source_target_pairs={{160,194},{161,195},{162,192},{163,193},{164,198},{165,199},{166,1... | collective-permute-start | bytes 344072 | tf_op jit(solution)/shard_map/ppermute | solution.py:28
  561.3 13.5 %collective-permute-start.81 = (bf16[256,224]{1,0:T(8,128)(2,1)}, bf16[256,224]{1,0:T(8,128)(2,1)}, u32[]{:S(2)}, u32[]{:S(2)}) collective-permute-start(bf16[256,224]{1,0:T(8,128)(2,1)} %add_convert_fusion.9), channel_id=1, source_target_pairs={{160,193},{161,192},{162,195},{163,194},{164,197},{165,196},{166,1... | collective-permute-start | bytes 344072 | tf_op jit(solution)/shard_map/ppermute | solution.py:28
  627.5 13.5 %collective-permute-start.95 = (bf16[256,224]{1,0:T(8,128)(2,1)}, bf16[256,224]{1,0:T(8,128)(2,1)}, u32[]{:S(2)}, u32[]{:S(2)}) collective-permute-start(bf16[256,224]{1,0:T(8,128)(2,1)} %add_convert_fusion.8), channel_id=1, source_target_pairs={{192,232},{193,233},{194,234},{195,235},{196,236},{197,237},{198,2... | collective-permute-start | bytes 344072 | tf_op jit(solution)/shard_map/ppermute | solution.py:28
  641.0 13.5 %collective-permute-start.94 = (bf16[256,224]{1,0:T(8,128)(2,1)}, bf16[256,224]{1,0:T(8,128)(2,1)}, u32[]{:S(2)}, u32[]{:S(2)}) collective-permute-start(bf16[256,224]{1,0:T(8,128)(2,1)} %add_convert_fusion.8), channel_id=1, source_target_pairs={{192,228},{193,229},{194,230},{195,231},{196,224},{197,225},{198,2... | collective-permute-start | bytes 344072 | tf_op jit(solution)/shard_map/ppermute | solution.py:28
  654.5 13.5 %collective-permute-start.93 = (bf16[256,224]{1,0:T(8,128)(2,1)}, bf16[256,224]{1,0:T(8,128)(2,1)}, u32[]{:S(2)}, u32[]{:S(2)}) collective-permute-start(bf16[256,224]{1,0:T(8,128)(2,1)} %add_convert_fusion.8), channel_id=1, source_target_pairs={{192,226},{193,227},{194,224},{195,225},{196,230},{197,231},{198,2... | collective-permute-start | bytes 344072 | tf_op jit(solution)/shard_map/ppermute | solution.py:28
  668.0 13.5 %collective-permute-start.92 = (bf16[256,224]{1,0:T(8,128)(2,1)}, bf16[256,224]{1,0:T(8,128)(2,1)}, u32[]{:S(2)}, u32[]{:S(2)}) collective-permute-start(bf16[256,224]{1,0:T(8,128)(2,1)} %add_convert_fusion.8), channel_id=1, source_target_pairs={{192,225},{193,224},{194,227},{195,226},{196,229},{197,228},{198,2... | collective-permute-start | bytes 344072 | tf_op jit(solution)/shard_map/ppermute | solution.py:28
  682.2 13.5 %collective-permute-start.91 = (bf16[256,224]{1,0:T(8,128)(2,1)}, bf16[256,224]{1,0:T(8,128)(2,1)}, u32[]{:S(2)}, u32[]{:S(2)}) collective-permute-start(bf16[256,224]{1,0:T(8,128)(2,1)} %add_convert_fusion.8), channel_id=1, source_target_pairs={{192,224},{193,225},{194,226},{195,227},{196,228},{197,229},{198,2... | collective-permute-start | bytes 344072 | tf_op jit(solution)/shard_map/ppermute | solution.py:28
  1010.2 13.1 %collective-permute-start.140 = (bf16[256,224]{1,0:T(8,128)(2,1)S(1)}, bf16[256,224]{1,0:T(8,128)(2,1)S(1)}, u32[]{:S(2)}, u32[]{:S(2)}) collective-permute-start(bf16[256,224]{1,0:T(8,128)(2,1)S(1)} %add_convert_fusion.4), channel_id=1, source_target_pairs={{128,112},{129,113},{130,114},{131,115},{132,116},{133,117},{134,1... | collective-permute-start | bytes 344072 | tf_op jit(solution)/shard_map/ppermute | solution.py:28
  1023.3 13.3 %collective-permute-start.139 = (bf16[256,224]{1,0:T(8,128)(2,1)S(1)}, bf16[256,224]{1,0:T(8,128)(2,1)S(1)}, u32[]{:S(2)}, u32[]{:S(2)}) collective-permute-start(bf16[256,224]{1,0:T(8,128)(2,1)S(1)} %add_convert_fusion.4), channel_id=1, source_target_pairs={{128,104},{129,105},{130,106},{131,107},{132,108},{133,109},{134,1... | collective-permute-start | bytes 344072 | tf_op jit(solution)/shard_map/ppermute | solution.py:28
  1036.6 13.1 %collective-permute-start.138 = (bf16[256,224]{1,0:T(8,128)(2,1)S(1)}, bf16[256,224]{1,0:T(8,128)(2,1)S(1)}, u32[]{:S(2)}, u32[]{:S(2)}) collective-permute-start(bf16[256,224]{1,0:T(8,128)(2,1)S(1)} %add_convert_fusion.4), channel_id=1, source_target_pairs={{128,100},{129,101},{130,102},{131,103},{132,96},{133,97},{134,98}... | collective-permute-start | bytes 344072 | tf_op jit(solution)/shard_map/ppermute | solution.py:28
  1230.3 24.2 %collective-permute-start.180 = (bf16[256,896]{1,0:T(8,128)(2,1)S(1)}, bf16[256,896]{1,0:T(8,128)(2,1)S(1)}, u32[]{:S(2)}, u32[]{:S(2)}) collective-permute-start(bf16[256,896]{1,0:T(8,128)(2,1)S(1)} %select_select_fusion.1.refs_7_), channel_id=1, source_target_pairs={{0,2},{1,3},{2,0},{3,1},{4,6},{5,7},{6,4},{7,5},{8,10},{9,11},{10,... | collective-permute-start | bytes 1376264 | tf_op jit(solution)/shard_map/ppermute | solution.py:28
  1278.8 13.7 %collective-permute-done.179.refs_8_ = bf16[256,896]{1,0:T(8,128)(2,1)S(1)} collective-permute-done((bf16[256,896]{1,0:T(8,128)(2,1)S(1)}, bf16[256,896]{1,0:T(8,128)(2,1)S(1)}, u32[]{:S(2)}, u32[]{:S(2)}) %collective-permute-start.179) | collective-permute-done | bytes 458784 | tf_op jit(solution)/shard_map/ppermute | solution.py:28
  (619 shorter events, 926.6 us)
Async XLA Ops:
  35.8 55.9 %collective-permute-start.22 = (bf16[256,224]{1,0:T(8,128)(2,1)S(1)}, bf16[256,224]{1,0:T(8,128)(2,1)S(1)}, u32[]{:S(2)}, u32[]{:S(2)}) collective-permute-start(bf16[256,224]{1,0:T(8,128)(2,1)S(1)} %get-tuple-element.122), channel_id=1, source_target_pairs={{0,4},{1,5},{2,6},{3,7},{4,0},{5,1},{6,2},{7,3},{8,12},{9,13},{10,... | collective-permute-start | bytes 344072 | tf_op jit(solution)/shard_map/ppermute | solution.py:28
  36.6 68.3 %collective-permute-start.23 = (bf16[256,224]{1,0:T(8,128)(2,1)S(1)}, bf16[256,224]{1,0:T(8,128)(2,1)S(1)}, u32[]{:S(2)}, u32[]{:S(2)}) collective-permute-start(bf16[256,224]{1,0:T(8,128)(2,1)S(1)} %get-tuple-element.123), channel_id=1, source_target_pairs={{0,8},{1,9},{2,10},{3,11},{4,12},{5,13},{6,14},{7,15},{8,0},{9,1},... | collective-permute-start | bytes 344072 | tf_op jit(solution)/shard_map/ppermute | solution.py:28
  37.7 80.3 %collective-permute-start.24 = (bf16[256,224]{1,0:T(8,128)(2,1)S(1)}, bf16[256,224]{1,0:T(8,128)(2,1)S(1)}, u32[]{:S(2)}, u32[]{:S(2)}) collective-permute-start(bf16[256,224]{1,0:T(8,128)(2,1)S(1)} %get-tuple-element.124), channel_id=1, source_target_pairs={{0,16},{1,17},{2,18},{3,19},{4,20},{5,21},{6,22},{7,23},{8,24},{9,... | collective-permute-start | bytes 344072 | tf_op jit(solution)/shard_map/ppermute | solution.py:28
  40.5 91.4 %collective-permute-start.9 = (bf16[224,896]{1,0:T(8,128)(2,1)}, bf16[224,896]{1,0:T(8,128)(2,1)S(1)}, u32[]{:S(2)}, u32[]{:S(2)}) collective-permute-start(bf16[224,896]{1,0:T(8,128)(2,1)} %get-tuple-element.235), channel_id=1, source_target_pairs={{32,48},{33,49},{34,50},{35,51},{36,52},{37,53},{38,54},{39,55},{4... | collective-permute-start | bytes 1204232 | tf_op jit(solution)/shard_map/ppermute | solution.py:28
  206.6 63.9 %collective-permute-start.52 = (bf16[256,224]{1,0:T(8,128)(2,1)}, bf16[256,224]{1,0:T(8,128)(2,1)S(1)}, u32[]{:S(2)}, u32[]{:S(2)}) collective-permute-start(bf16[256,224]{1,0:T(8,128)(2,1)} %add_convert_fusion.12), channel_id=1, source_target_pairs={{64,112},{65,113},{66,114},{67,115},{68,116},{69,117},{70,118},{71... | collective-permute-start | bytes 344072 | tf_op jit(solution)/shard_map/ppermute | solution.py:28
  296.1 65.8 %collective-permute-start.63 = (bf16[256,224]{1,0:T(8,128)(2,1)}, bf16[256,224]{1,0:T(8,128)(2,1)S(1)}, u32[]{:S(2)}, u32[]{:S(2)}) collective-permute-start(bf16[256,224]{1,0:T(8,128)(2,1)} %add_convert_fusion.11), channel_id=1, source_target_pairs={{96,144},{97,145},{98,146},{99,147},{100,148},{101,149},{102,150},... | collective-permute-start | bytes 344072 | tf_op jit(solution)/shard_map/ppermute | solution.py:28
  310.2 64.7 %collective-permute-start.62 = (bf16[256,224]{1,0:T(8,128)(2,1)}, bf16[256,224]{1,0:T(8,128)(2,1)}, u32[]{:S(2)}, u32[]{:S(2)}) collective-permute-start(bf16[256,224]{1,0:T(8,128)(2,1)} %add_convert_fusion.11), channel_id=1, source_target_pairs={{96,136},{97,137},{98,138},{99,139},{100,140},{101,141},{102,142},... | collective-permute-start | bytes 344072 | tf_op jit(solution)/shard_map/ppermute | solution.py:28
  398.0 69.6 %collective-permute-start.74 = (bf16[256,224]{1,0:T(8,128)(2,1)}, bf16[256,224]{1,0:T(8,128)(2,1)S(1)}, u32[]{:S(2)}, u32[]{:S(2)}) collective-permute-start(bf16[256,224]{1,0:T(8,128)(2,1)} %add_convert_fusion.10), channel_id=1, source_target_pairs={{128,176},{129,177},{130,178},{131,179},{132,180},{133,181},{134,1... | collective-permute-start | bytes 344072 | tf_op jit(solution)/shard_map/ppermute | solution.py:28
  413.2 68.9 %collective-permute-start.73 = (bf16[256,224]{1,0:T(8,128)(2,1)}, bf16[256,224]{1,0:T(8,128)(2,1)}, u32[]{:S(2)}, u32[]{:S(2)}) collective-permute-start(bf16[256,224]{1,0:T(8,128)(2,1)} %add_convert_fusion.10), channel_id=1, source_target_pairs={{128,168},{129,169},{130,170},{131,171},{132,172},{133,173},{134,1... | collective-permute-start | bytes 344072 | tf_op jit(solution)/shard_map/ppermute | solution.py:28
  511.0 63.8 %collective-permute-start.85 = (bf16[256,224]{1,0:T(8,128)(2,1)}, bf16[256,224]{1,0:T(8,128)(2,1)S(1)}, u32[]{:S(2)}, u32[]{:S(2)}) collective-permute-start(bf16[256,224]{1,0:T(8,128)(2,1)} %add_convert_fusion.9), channel_id=1, source_target_pairs={{160,208},{161,209},{162,210},{163,211},{164,212},{165,213},{166,2... | collective-permute-start | bytes 344072 | tf_op jit(solution)/shard_map/ppermute | solution.py:28
  520.7 67.7 %collective-permute-start.84 = (bf16[256,224]{1,0:T(8,128)(2,1)}, bf16[256,224]{1,0:T(8,128)(2,1)}, u32[]{:S(2)}, u32[]{:S(2)}) collective-permute-start(bf16[256,224]{1,0:T(8,128)(2,1)} %add_convert_fusion.9), channel_id=1, source_target_pairs={{160,200},{161,201},{162,202},{163,203},{164,204},{165,205},{166,2... | collective-permute-start | bytes 344072 | tf_op jit(solution)/shard_map/ppermute | solution.py:28
  616.7 64.8 %collective-permute-start.96 = (bf16[256,224]{1,0:T(8,128)(2,1)}, bf16[256,224]{1,0:T(8,128)(2,1)S(1)}, u32[]{:S(2)}, u32[]{:S(2)}) collective-permute-start(bf16[256,224]{1,0:T(8,128)(2,1)} %add_convert_fusion.8), channel_id=1, source_target_pairs={{192,240},{193,241},{194,242},{195,243},{196,244},{197,245},{198,2... | collective-permute-start | bytes 344072 | tf_op jit(solution)/shard_map/ppermute | solution.py:28
  627.5 68.2 %collective-permute-start.95 = (bf16[256,224]{1,0:T(8,128)(2,1)}, bf16[256,224]{1,0:T(8,128)(2,1)}, u32[]{:S(2)}, u32[]{:S(2)}) collective-permute-start(bf16[256,224]{1,0:T(8,128)(2,1)} %add_convert_fusion.8), channel_id=1, source_target_pairs={{192,232},{193,233},{194,234},{195,235},{196,236},{197,237},{198,2... | collective-permute-start | bytes 344072 | tf_op jit(solution)/shard_map/ppermute | solution.py:28
  641.0 57.4 %collective-permute-start.94 = (bf16[256,224]{1,0:T(8,128)(2,1)}, bf16[256,224]{1,0:T(8,128)(2,1)}, u32[]{:S(2)}, u32[]{:S(2)}) collective-permute-start(bf16[256,224]{1,0:T(8,128)(2,1)} %add_convert_fusion.8), channel_id=1, source_target_pairs={{192,228},{193,229},{194,230},{195,231},{196,224},{197,225},{198,2... | collective-permute-start | bytes 344072 | tf_op jit(solution)/shard_map/ppermute | solution.py:28
  729.3 63.4 %collective-permute-start.107 = (bf16[256,224]{1,0:T(8,128)(2,1)S(1)}, bf16[256,224]{1,0:T(8,128)(2,1)S(1)}, u32[]{:S(2)}, u32[]{:S(2)}) collective-permute-start(bf16[256,224]{1,0:T(8,128)(2,1)S(1)} %add_convert_fusion.7), channel_id=1, source_target_pairs={{224,208},{225,209},{226,210},{227,211},{228,212},{229,213},{230,2... | collective-permute-start | bytes 344072 | tf_op jit(solution)/shard_map/ppermute | solution.py:28
  742.3 63.1 %collective-permute-start.106 = (bf16[256,224]{1,0:T(8,128)(2,1)S(1)}, bf16[256,224]{1,0:T(8,128)(2,1)S(1)}, u32[]{:S(2)}, u32[]{:S(2)}) collective-permute-start(bf16[256,224]{1,0:T(8,128)(2,1)S(1)} %add_convert_fusion.7), channel_id=1, source_target_pairs={{224,200},{225,201},{226,202},{227,203},{228,204},{229,205},{230,2... | collective-permute-start | bytes 344072 | tf_op jit(solution)/shard_map/ppermute | solution.py:28
  822.4 64.3 %collective-permute-start.118 = (bf16[256,224]{1,0:T(8,128)(2,1)S(1)}, bf16[256,224]{1,0:T(8,128)(2,1)S(1)}, u32[]{:S(2)}, u32[]{:S(2)}) collective-permute-start(bf16[256,224]{1,0:T(8,128)(2,1)S(1)} %add_convert_fusion.6), channel_id=1, source_target_pairs={{192,176},{193,177},{194,178},{195,179},{196,180},{197,181},{198,1... | collective-permute-start | bytes 344072 | tf_op jit(solution)/shard_map/ppermute | solution.py:28
  835.2 64.3 %collective-permute-start.117 = (bf16[256,224]{1,0:T(8,128)(2,1)S(1)}, bf16[256,224]{1,0:T(8,128)(2,1)S(1)}, u32[]{:S(2)}, u32[]{:S(2)}) collective-permute-start(bf16[256,224]{1,0:T(8,128)(2,1)S(1)} %add_convert_fusion.6), channel_id=1, source_target_pairs={{192,168},{193,169},{194,170},{195,171},{196,172},{197,173},{198,1... | collective-permute-start | bytes 344072 | tf_op jit(solution)/shard_map/ppermute | solution.py:28
  921.4 59.8 %collective-permute-start.129 = (bf16[256,224]{1,0:T(8,128)(2,1)S(1)}, bf16[256,224]{1,0:T(8,128)(2,1)S(1)}, u32[]{:S(2)}, u32[]{:S(2)}) collective-permute-start(bf16[256,224]{1,0:T(8,128)(2,1)S(1)} %add_convert_fusion.5), channel_id=1, source_target_pairs={{160,144},{161,145},{162,146},{163,147},{164,148},{165,149},{166,1... | collective-permute-start | bytes 344072 | tf_op jit(solution)/shard_map/ppermute | solution.py:28
  929.6 64.4 %collective-permute-start.128 = (bf16[256,224]{1,0:T(8,128)(2,1)S(1)}, bf16[256,224]{1,0:T(8,128)(2,1)S(1)}, u32[]{:S(2)}, u32[]{:S(2)}) collective-permute-start(bf16[256,224]{1,0:T(8,128)(2,1)S(1)} %add_convert_fusion.5), channel_id=1, source_target_pairs={{160,136},{161,137},{162,138},{163,139},{164,140},{165,141},{166,1... | collective-permute-start | bytes 344072 | tf_op jit(solution)/shard_map/ppermute | solution.py:28
  1010.2 65.9 %collective-permute-start.140 = (bf16[256,224]{1,0:T(8,128)(2,1)S(1)}, bf16[256,224]{1,0:T(8,128)(2,1)S(1)}, u32[]{:S(2)}, u32[]{:S(2)}) collective-permute-start(bf16[256,224]{1,0:T(8,128)(2,1)S(1)} %add_convert_fusion.4), channel_id=1, source_target_pairs={{128,112},{129,113},{130,114},{131,115},{132,116},{133,117},{134,1... | collective-permute-start | bytes 344072 | tf_op jit(solution)/shard_map/ppermute | solution.py:28
  1023.3 65.8 %collective-permute-start.139 = (bf16[256,224]{1,0:T(8,128)(2,1)S(1)}, bf16[256,224]{1,0:T(8,128)(2,1)S(1)}, u32[]{:S(2)}, u32[]{:S(2)}) collective-permute-start(bf16[256,224]{1,0:T(8,128)(2,1)S(1)} %add_convert_fusion.4), channel_id=1, source_target_pairs={{128,104},{129,105},{130,106},{131,107},{132,108},{133,109},{134,1... | collective-permute-start | bytes 344072 | tf_op jit(solution)/shard_map/ppermute | solution.py:28
  1104.4 63.0 %collective-permute-start.151 = (bf16[256,224]{1,0:T(8,128)(2,1)S(1)}, bf16[256,224]{1,0:T(8,128)(2,1)S(1)}, u32[]{:S(2)}, u32[]{:S(2)}) collective-permute-start(bf16[256,224]{1,0:T(8,128)(2,1)S(1)} %add_convert_fusion.3), channel_id=1, source_target_pairs={{96,80},{97,81},{98,82},{99,83},{100,84},{101,85},{102,86},{103,87... | collective-permute-start | bytes 344072 | tf_op jit(solution)/shard_map/ppermute | solution.py:28
  1117.4 62.9 %collective-permute-start.150 = (bf16[256,224]{1,0:T(8,128)(2,1)S(1)}, bf16[256,224]{1,0:T(8,128)(2,1)S(1)}, u32[]{:S(2)}, u32[]{:S(2)}) collective-permute-start(bf16[256,224]{1,0:T(8,128)(2,1)S(1)} %add_convert_fusion.3), channel_id=1, source_target_pairs={{96,72},{97,73},{98,74},{99,75},{100,76},{101,77},{102,78},{103,79... | collective-permute-start | bytes 344072 | tf_op jit(solution)/shard_map/ppermute | solution.py:28
  (276 other events, 5152.6 us)

commit v2 on v1

v2 whole, which is shorter than its diff:
```python
import functools

import jax
import jax.numpy as jnp
from jax import lax
from jax.experimental import pallas as pl
from jax.experimental.pallas import tpu as pltpu
from jax.sharding import PartitionSpec as P

AXES = ("pipe", "tensor")
GELU_C = 0.7978845608028654
GELU_A = 0.044715
VMEM = pl.BlockSpec(memory_space=pltpu.VMEM)
SMEM = pl.BlockSpec(memory_space=pltpu.SMEM)
ANY = pl.BlockSpec(memory_space=pl.ANY)
F32 = jnp.float32
BF16 = jnp.bfloat16


def partner(index, term):
    return index if term == 0 else index ^ (1 << (term - 1))


def send(value, term, routes):
    width = lax.axis_size("tensor")
    pairs = [
        (a * width + i, b * width + partner(i, term)) for a, b in routes for i in range(width)
    ]
    return lax.ppermute(value, AXES, pairs)


def column_chunks(width):
    return [(start, min(256, width - start)) for start in range(0, width, 256)]


def dot_nn(a, b):
    return lax.dot_general(a, b, (((1,), (0,)), ((), ())), preferred_element_type=F32)


def dot_nt(a, b):
    return lax.dot_general(a, b, (((1,), (1,)), ((), ())), preferred_element_type=F32)


def dot_tn(a, b):
    return lax.dot_general(a, b, (((0,), (0,)), ((), ())), preferred_element_type=F32)


def copy_in(n, first, second, w_first, w_second, sems):
    copies = []
    for k in range(n):
        copies.append(pltpu.make_async_copy(first.at[k], w_first.at[k], sems.at[k]))
        copies.append(pltpu.make_async_copy(second[k], w_second.at[k], sems.at[n + k]))
    return copies[0::2], copies[1::2]


def forward_kernel(n, last, tokens, n_state, *refs):
    active, refs = refs[0], refs[1:]
    ins, refs = refs[:n], refs[n:]
    first, refs = refs[0], refs[1:]
    second, refs = refs[:n], refs[n:]
    refs = refs[n_state:]
    st_ins, st_pre, st_hid = refs[:3]
    outs, refs = (refs[3:3], refs[3:]) if last else (refs[3 : 3 + n], refs[3 + n :])
    w_first, w_second, preact, hidden, sems = refs
    rows = pl.ds(0, tokens)

    @pl.when(active[0] == 1)
    def _():
        from_first, from_second = copy_in(n, first, second, w_first, w_second, sems)
        for copy in from_first:
            copy.start()
        if not last:
            for copy in from_second:
                copy.start()
        saves = [
            pltpu.make_async_copy(ins[k].at[rows], st_ins.at[k], sems.at[2 * n + k])
            for k in range(n)
        ]
        for copy in saves:
            copy.start()
        for start, size in column_chunks(preact.shape[1]):
            cols = slice(start, start + size)
            total = None
            for k in range(n):
                if start == 0:
                    from_first[k].wait()
                part = dot_nn(ins[k][rows, :], w_first[k, :, cols])
                total = part if k == 0 else total + part
            preact[:, cols] = total
            inner = GELU_C * (total + GELU_A * (total * total * total))
            hidden[:, cols] = (0.5 * total * (1.0 + jnp.tanh(inner))).astype(BF16)
        saves.append(pltpu.make_async_copy(preact, st_pre, sems.at[3 * n]))
        saves.append(pltpu.make_async_copy(hidden, st_hid, sems.at[3 * n + 1]))
        saves[n].start()
        saves[n + 1].start()
        if not last:
            for k in range(n):
                from_second[k].wait()
                part = dot_nt(hidden[...], w_second[k])
                if k == 0:
                    outs[0][...] = ins[0][rows, :].astype(F32) + part
                else:
                    outs[k][...] = part.astype(BF16)
        for copy in saves:
            copy.wait()


def backward_kernel(n, tokens, offset, n_state, *refs):
    active, refs = refs[0], refs[1:]
    ins, refs = refs[:n], refs[n:]
    first, refs = refs[0], refs[1:]
    second, refs = refs[:n], refs[n:]
    st_pre, refs = refs[0], refs[1 + n_state :]
    st_dpre, st_grad = refs[:2]
    outs, refs = refs[2 : 2 + n], refs[2 + n :]
    w_first, w_second, preact, dpre, sems = refs
    rows = pl.ds(offset, tokens)

    @pl.when(active[0] == 1)
    def _():
        from_first, from_second = copy_in(n, first, second, w_first, w_second, sems)
        from_pre = pltpu.make_async_copy(st_pre, preact, sems.at[2 * n])
        for copy in from_second + [from_pre] + from_first:
            copy.start()
        save_grad = pltpu.make_async_copy(ins[0].at[rows], st_grad, sems.at[2 * n + 1])
        save_grad.start()
        for start, size in column_chunks(preact.shape[1]):
            cols = slice(start, start + size)
            total = None
            for k in range(n):
                if start == 0:
                    from_second[k].wait()
                part = dot_nn(ins[k][rows, :], w_second[k, :, cols])
                total = part if k == 0 else total + part
            if start == 0:
                from_pre.wait()
            x = preact[:, cols]
            square = x * x
            bent = jnp.tanh(GELU_C * (x + GELU_A * (square * x)))
            slope = 0.5 * (1.0 + bent) + 0.5 * x * (1.0 - bent * bent) * (
                GELU_C * (1.0 + 3.0 * GELU_A * square)
            )
            dpre[:, cols] = (total * slope).astype(BF16)
        save_dpre = pltpu.make_async_copy(dpre, st_dpre, sems.at[2 * n + 2])
        save_dpre.start()
        for k in range(n):
            from_first[k].wait()
            part = dot_nt(dpre[...], w_first[k])
            if k == 0:
                outs[0][...] = ins[0][rows, :].astype(F32) + part
            else:
                outs[k][...] = part.astype(BF16)
        save_grad.wait()
        save_dpre.wait()


def grad_kernel(n, *refs):
    ins, dpre, refs = refs[0], refs[1], refs[2:]
    hiddens, grad, refs = refs[:n], refs[n], refs[n + 1 :]
    out_first, out_second, v_first, v_second, sems = refs
    copies = []
    for k in range(n):
        v_first[k] = dot_tn(ins[k], dpre[...]).astype(BF16)
        v_second[k] = dot_tn(grad[...], hiddens[k][...]).astype(BF16)
        copies.append(pltpu.make_async_copy(v_first.at[k], out_first.at[k], sems.at[k]))
        copies.append(pltpu.make_async_copy(v_second.at[k], out_second.at[k], sems.at[n + k]))
        copies[-2].start()
        copies[-1].start()
    for copy in copies:
        copy.wait()


def body(x_in, cotangent, w_in, w_out):
    sections = lax.axis_size("pipe")
    n = lax.axis_size("tensor").bit_length()
    me = lax.axis_index("pipe")
    batches, tok_rows, slab = x_in.shape
    tokens = batches * tok_rows
    first = w_in[0]
    owned = jnp.swapaxes(w_out[0], 1, 2)
    hid = first.shape[2]
    shape = jax.ShapeDtypeStruct
    cost = pl.CostEstimate(
        flops=4 * tokens * n * slab * hid, bytes_accessed=4 * n * slab * hid, transcendentals=0
    )
    params = pltpu.CompilerParams(vmem_limit_bytes=52 * 1024 * 1024)
    weights = [pltpu.VMEM((n, slab, hid), BF16)] * 2
    work = [pltpu.VMEM((tokens, hid), F32), pltpu.VMEM((tokens, hid), BF16)]
    term_shapes = [shape((tokens, slab), F32)] + [shape((tokens, slab), BF16)] * (n - 1)

    everyone = [(s, s) for s in range(sections)]
    order = [k for k in (3, 5, 2, 4, 1) if k < n]

    def exchange(values, routes):
        got = {k: send(values[k], k, routes) for k in order}
        return [got[k] for k in range(1, n)]

    def neighbours(layer, step):
        return [
            (s, s + step)
            for s in range(layer % 2, sections, 2)
            if 0 <= s + step < sections
        ]

    def reduced(terms, got):
        total = terms[0]
        for k in order:
            total = total + got[k - 1].astype(F32)
        return total.astype(BF16)

    both = jnp.concatenate(
        [x_in.reshape(tokens, slab), cotangent.reshape(tokens, slab)], axis=0
    )
    ins = [both] + exchange([both] * n, everyone)
    first_grads = ins
    second_0 = [owned[0]] + exchange(owned, [(0, 0)])
    second_r = None

    state = []
    for layer in range(sections):
        last = layer == sections - 1
        active = (me == layer).astype(jnp.int32).reshape(1)
        second = second_0 if layer == 0 else second_r
        state_shapes = [
            shape((n, tokens, slab), BF16), shape((tokens, hid), F32), shape((tokens, hid), BF16)
        ]
        outs = [] if last else term_shapes
        *state, = pl.pallas_call(
            functools.partial(forward_kernel, n, last, tokens, len(state)),
            out_shape=state_shapes + outs,
            in_specs=[SMEM] + [VMEM] * n + [ANY] * (1 + n + len(state)),
            out_specs=[ANY] * 3 + [VMEM] * len(outs),
            scratch_shapes=weights + work + [pltpu.SemaphoreType.DMA((3 * n + 2,))],
            input_output_aliases={2 + 2 * n + i: i for i in range(len(state))},
            cost_estimate=cost,
            compiler_params=params,
        )(active, *ins, first, *second, *state)
        state, terms = state[:3], state[3:]
        if last:
            break
        out = reduced(terms, exchange(terms, everyone))
        if layer == 0:
            second_r = [owned[0]] + exchange(owned, everyone)
        route = neighbours(layer, 1)
        ins = exchange([out] * n, route)
        ins = [send(out, 0, route)] + ins

    st_ins, st_pre, st_hid = state
    hiddens = {0: st_hid}
    pending = list(order)
    state = []
    grads_in = first_grads
    saved_out = None
    for layer in reversed(range(sections)):
        active = (me == layer).astype(jnp.int32).reshape(1)
        second = second_0 if layer == 0 else second_r
        st_dpre, st_grad, *terms = pl.pallas_call(
            functools.partial(
                backward_kernel, n, tokens, tokens if layer == sections - 1 else 0, len(state)
            ),
            out_shape=[shape((tokens, hid), BF16), shape((tokens, slab), BF16)] + term_shapes,
            in_specs=[SMEM] + [VMEM] * n + [ANY] * (2 + n + len(state)),
            out_specs=[ANY] * 2 + [VMEM] * n,
            scratch_shapes=weights + work + [pltpu.SemaphoreType.DMA((2 * n + 3,))],
            input_output_aliases={3 + 2 * n + i: i for i in range(len(state))},
            cost_estimate=cost,
            compiler_params=params,
        )(active, *grads_in, first, *second, st_pre, *state)
        state = [st_dpre, st_grad]
        out = reduced(terms, exchange(terms, everyone))
        saved_out = out if saved_out is None else jnp.where(me == layer, out, saved_out)
        if layer > 0:
            route = neighbours(layer, -1)
            grads_in = exchange([out] * n, route)
            grads_in = [send(out, 0, route)] + grads_in
            if pending and layer <= sections - 2:
                k = pending.pop(0)
                block, _ = lax.optimization_barrier((st_hid, out))
                hiddens[k] = send(block, k, everyone)
            if layer <= sections - 4:
                done = [k for k in hiddens if k]
                tied = lax.optimization_barrier(tuple(grads_in) + tuple(hiddens[k] for k in done))
                grads_in = list(tied[:n])
                hiddens.update(zip(done, tied[n:]))

    grad_first, grad_second = pl.pallas_call(
        functools.partial(grad_kernel, n),
        out_shape=[shape((n, slab, hid), BF16)] * 2,
        in_specs=[VMEM] * (3 + n),
        out_specs=[ANY] * 2,
        scratch_shapes=weights + [pltpu.SemaphoreType.DMA((2 * n,))],
        cost_estimate=cost,
        compiler_params=params,
    )(st_ins, st_dpre, *[hiddens[k] for k in range(n)], st_grad)
    acts = saved_out.reshape(batches, tok_rows, slab)
    return acts[None], grad_first[None], jnp.swapaxes(grad_second, 1, 2)[None]


def solution(mesh):
    placed = (
        P(None, None, "tensor"),
        P(None, None, "tensor"),
        P("pipe", None, None, "tensor"),
        P("pipe", None, None, "tensor"),
    )
    return jax.shard_map(
        body,
        mesh=mesh,
        in_specs=placed,
        out_specs=(P("pipe", None, None, "tensor"),) * 3,
        check_vma=False,
    )
```

time: 1320 us -> 602 us (0.46)
  the two profiles are of different devices: /device:TPU:5 before, /device:TPU:8 now
where the time goes in v2:
time: 602 us; the launch traced here: 592 us
  starting transfers between devices  301 us (50%)
  waiting for transfers between devices  257 us (43%)
  Pallas kernels  21.7 us (4%)
  local copies, waits for them, and re-layouts  6.24 us (1%)
    ppermute x179, starting transfers between devices, send(): return lax.ppermute(value, AXES, pairs)  301 us
    ppermute x179, waiting for transfers between devices, send(): return lax.ppermute(value, AXES, pairs)  257 us
  transfers between devices with their start and end apart: 179, of which 61 were waited for; matrix products, arithmetic and copies ran while one was open for 1% of the time, Pallas kernels for 1%

profile of v2, /device:TPU:8, one launch (start us, length us, event | category | flops | bytes accessed | tf_op | source)
XLA Modules:
  0.0 592.1 jit_solution(16685585680026711560)
XLA Ops:
  5.4 7.2 %collective-permute-start.2 = (bf16[512,224]{1,0:T(8,128)(2,1)S(1)}, bf16[512,224]{1,0:T(8,128)(2,1)S(1)}, u32[]{:S(2)}, u32[]{:S(2)}) collective-permute-start(bf16[512,224]{1,0:T(8,128)(2,1)S(1)} %pad_maximum_fusion.refs_1_), channel_id=1, source_target_pairs={{0,4},{1,5},{2,6},{3,7},{4,0},{5,1},{6,2},{7,3},{8,12},{9,13},{10,... | collective-permute-start | bytes 688136 | tf_op jit(solution)/shard_map/ppermute | solution.py:29
  25.1 7.6 %collective-permute-start.12 = (bf16[224,896]{1,0:T(8,128)(2,1)}, bf16[224,896]{1,0:T(8,128)(2,1)S(1)}, u32[]{:S(2)}, u32[]{:S(2)}) collective-permute-start(bf16[224,896]{1,0:T(8,128)(2,1)} %get-tuple-element.361), channel_id=1, source_target_pairs={{0,4},{1,5},{2,6},{3,7},{4,0},{5,1},{6,2},{7,3},{8,12},{9,13},{10,... | collective-permute-start | bytes 1204232 | tf_op jit(solution)/shard_map/ppermute | solution.py:29
  42.6 17.3 %collective-permute-done.11.refs_10_ = bf16[224,896]{1,0:T(8,128)(2,1)S(1)} collective-permute-done((bf16[224,896]{1,0:T(8,128)(2,1)}, bf16[224,896]{1,0:T(8,128)(2,1)S(1)}, u32[]{:S(2)}, u32[]{:S(2)}) %collective-permute-start.11) | collective-permute-done | bytes 401440 | tf_op jit(solution)/shard_map/ppermute | solution.py:29
  60.8 6.8 %shard_map.67 = (bf16[6,256,224]{2,1,0:T(8,128)(2,1)}, f32[256,896]{1,0:T(8,128)}, bf16[256,896]{1,0:T(8,128)(2,1)}, f32[256,224]{1,0:T(8,128)S(1)}, bf16[256,22...) custom-call(s32[1]{0:T(128)} %bitcast.refs_0_, ...), custom_call_target="tpu_custom_call" | custom-call | flops 1233125376 | bytes 4816896 | tf_op jit(solution)/shard_map/pallas_call | solution.py:228
  73.9 5.2 collective-permute-done.15
  93.1 5.2 collective-permute-done.7.refs_11_
  99.6 6.9 %collective-permute-done.6.refs_10_ = bf16[224,896]{1,0:T(8,128)(2,1)S(1)} collective-permute-done((bf16[224,896]{1,0:T(8,128)(2,1)}, bf16[224,896]{1,0:T(8,128)(2,1)S(1)}, u32[]{:S(2)}, u32[]{:S(2)}) %collective-permute-start.6) | collective-permute-done | bytes 401440 | tf_op jit(solution)/shard_map/ppermute | solution.py:29
  148.7 11.7 %collective-permute-start.47 = (bf16[256,224]{1,0:T(8,128)(2,1)S(1)}, bf16[256,224]{1,0:T(8,128)(2,1)S(1)}, u32[]{:S(2)}, u32[]{:S(2)}) collective-permute-start(bf16[256,224]{1,0:T(8,128)(2,1)S(1)} %add_convert_fusion.12), channel_id=1, source_target_pairs={{0,48},{1,49},{2,50},{3,51},{4,52},{5,53},{6,54},{7,55},{8,56},{9,... | collective-permute-start | bytes 344072 | tf_op jit(solution)/shard_map/ppermute | solution.py:29
  182.2 7.4 %collective-permute-done.50 = bf16[256,224]{1,0:T(8,128)(2,1)S(1)} collective-permute-done((bf16[256,224]{1,0:T(8,128)(2,1)S(1)}, bf16[256,224]{1,0:T(8,128)(2,1)S(1)}, u32[]{:S(2)}, u32[]{:S(2)}) %collective-permute-start.50) | collective-permute-done | bytes 114720 | tf_op jit(solution)/shard_map/ppermute | solution.py:29
  204.5 7.3 %collective-permute-done.61 = bf16[256,224]{1,0:T(8,128)(2,1)S(1)} collective-permute-done((bf16[256,224]{1,0:T(8,128)(2,1)S(1)}, bf16[256,224]{1,0:T(8,128)(2,1)S(1)}, u32[]{:S(2)}, u32[]{:S(2)}) %collective-permute-start.61) | collective-permute-done | bytes 114720 | tf_op jit(solution)/shard_map/ppermute | solution.py:29
  211.9 14.0 %collective-permute-start.69 = (bf16[256,224]{1,0:T(8,128)(2,1)S(1)}, bf16[256,224]{1,0:T(8,128)(2,1)S(1)}, u32[]{:S(2)}, u32[]{:S(2)}) collective-permute-start(bf16[256,224]{1,0:T(8,128)(2,1)S(1)} %add_convert_fusion.10), channel_id=1, source_target_pairs={{0,48},{1,49},{2,50},{3,51},{4,52},{5,53},{6,54},{7,55},{8,56},{9,... | collective-permute-start | bytes 344072 | tf_op jit(solution)/shard_map/ppermute | solution.py:29
  247.7 7.0 %collective-permute-done.72 = bf16[256,224]{1,0:T(8,128)(2,1)S(1)} collective-permute-done((bf16[256,224]{1,0:T(8,128)(2,1)S(1)}, bf16[256,224]{1,0:T(8,128)(2,1)S(1)}, u32[]{:S(2)}, u32[]{:S(2)}) %collective-permute-start.72) | collective-permute-done | bytes 114720 | tf_op jit(solution)/shard_map/ppermute | solution.py:29
  269.7 7.3 %collective-permute-done.83 = bf16[256,224]{1,0:T(8,128)(2,1)S(1)} collective-permute-done((bf16[256,224]{1,0:T(8,128)(2,1)S(1)}, bf16[256,224]{1,0:T(8,128)(2,1)S(1)}, u32[]{:S(2)}, u32[]{:S(2)}) %collective-permute-start.83) | collective-permute-done | bytes 114720 | tf_op jit(solution)/shard_map/ppermute | solution.py:29
  277.2 12.5 %collective-permute-start.91 = (bf16[256,224]{1,0:T(8,128)(2,1)S(1)}, bf16[256,224]{1,0:T(8,128)(2,1)S(1)}, u32[]{:S(2)}, u32[]{:S(2)}) collective-permute-start(bf16[256,224]{1,0:T(8,128)(2,1)S(1)} %add_convert_fusion.8), channel_id=1, source_target_pairs={{0,48},{1,49},{2,50},{3,51},{4,52},{5,53},{6,54},{7,55},{8,56},{9,... | collective-permute-start | bytes 344072 | tf_op jit(solution)/shard_map/ppermute | solution.py:29
  313.7 6.9 %collective-permute-done.94 = bf16[256,224]{1,0:T(8,128)(2,1)S(1)} collective-permute-done((bf16[256,224]{1,0:T(8,128)(2,1)S(1)}, bf16[256,224]{1,0:T(8,128)(2,1)S(1)}, u32[]{:S(2)}, u32[]{:S(2)}) %collective-permute-start.94) | collective-permute-done | bytes 114720 | tf_op jit(solution)/shard_map/ppermute | solution.py:29
  329.8 5.1 collective-permute-done.100.refs_4_
  375.8 10.3 %collective-permute-done.124.refs_6_ = bf16[256,224]{1,0:T(8,128)(2,1)S(1)} collective-permute-done((bf16[256,224]{1,0:T(8,128)(2,1)S(1)}, bf16[256,224]{1,0:T(8,128)(2,1)S(1)}, u32[]{:S(2)}, u32[]{:S(2)}) %collective-permute-start.124) | collective-permute-done | bytes 114720 | tf_op jit(solution)/shard_map/ppermute | solution.py:29
  412.8 20.0 %collective-permute-done.136.refs_5_ = bf16[256,896]{1,0:T(8,128)(2,1)S(1)} collective-permute-done((bf16[256,896]{1,0:T(8,128)(2,1)S(1)}, bf16[256,896]{1,0:T(8,128)(2,1)S(1)}, u32[]{:S(2)}, u32[]{:S(2)}) %collective-permute-start.136) | collective-permute-done | bytes 458784 | tf_op jit(solution)/shard_map/ppermute | solution.py:29
  435.5 12.5 %collective-permute-done.138.refs_4_ = bf16[256,896]{1,0:T(8,128)(2,1)S(1)} collective-permute-done((bf16[256,896]{1,0:T(8,128)(2,1)S(1)}, bf16[256,896]{1,0:T(8,128)(2,1)S(1)}, u32[]{:S(2)}, u32[]{:S(2)}) %collective-permute-start.138) | collective-permute-done | bytes 458784 | tf_op jit(solution)/shard_map/ppermute | solution.py:29
  467.7 15.5 %collective-permute-done.149.refs_6_ = bf16[256,224]{1,0:T(8,128)(2,1)S(1)} collective-permute-done((bf16[256,224]{1,0:T(8,128)(2,1)S(1)}, bf16[256,224]{1,0:T(8,128)(2,1)S(1)}, u32[]{:S(2)}, u32[]{:S(2)}) %collective-permute-start.149) | collective-permute-done | bytes 114720 | tf_op jit(solution)/shard_map/ppermute | solution.py:29
  501.2 5.0 collective-permute-done.153
  510.9 8.0 %collective-permute-done.162.refs_3_ = bf16[256,896]{1,0:T(8,128)(2,1)S(1)} collective-permute-done((bf16[256,896]{1,0:T(8,128)(2,1)S(1)}, bf16[256,896]{1,0:T(8,128)(2,1)S(1)}, u32[]{:S(2)}, u32[]{:S(2)}) %collective-permute-start.162) | collective-permute-done | bytes 458784 | tf_op jit(solution)/shard_map/ppermute | solution.py:29
  538.6 25.2 %collective-permute-done.173.refs_6_ = bf16[256,224]{1,0:T(8,128)(2,1)S(1)} collective-permute-done((bf16[256,224]{1,0:T(8,128)(2,1)S(1)}, bf16[256,224]{1,0:T(8,128)(2,1)S(1)}, u32[]{:S(2)}, u32[]{:S(2)}) %collective-permute-start.173) | collective-permute-done | bytes 114720 | tf_op jit(solution)/shard_map/ppermute | solution.py:29
  571.6 5.9 shard_map.82
  (414 shorter events, 351.5 us)
Async XLA Ops:
  12.6 23.2 %collective-permute-start.1 = (bf16[512,224]{1,0:T(8,128)(2,1)S(1)}, bf16[512,224]{1,0:T(8,128)(2,1)S(1)}, u32[]{:S(2)}, u32[]{:S(2)}) collective-permute-start(bf16[512,224]{1,0:T(8,128)(2,1)S(1)} %pad_maximum_fusion.refs_1_), channel_id=1, source_target_pairs={{0,2},{1,3},{2,0},{3,1},{4,6},{5,7},{6,4},{7,5},{8,10},{9,11},{10,... | collective-permute-start | bytes 688136 | tf_op jit(solution)/shard_map/ppermute | solution.py:29
  14.0 23.6 %collective-permute-start = (bf16[512,224]{1,0:T(8,128)(2,1)S(1)}, bf16[512,224]{1,0:T(8,128)(2,1)S(1)}, u32[]{:S(2)}, u32[]{:S(2)}) collective-permute-start(bf16[512,224]{1,0:T(8,128)(2,1)S(1)} %pad_maximum_fusion.refs_1_), channel_id=1, source_target_pairs={{0,1},{1,0},{2,3},{3,2},{4,5},{5,4},{6,7},{7,6},{8,9},{9,8},{10,11... | collective-permute-start | bytes 688136 | tf_op jit(solution)/shard_map/ppermute | solution.py:29
  18.0 24.5 %collective-permute-start.14 = (bf16[224,896]{1,0:T(8,128)(2,1)}, bf16[224,896]{1,0:T(8,128)(2,1)S(1)}, u32[]{:S(2)}, u32[]{:S(2)}) collective-permute-start(bf16[224,896]{1,0:T(8,128)(2,1)} %get-tuple-element.359), channel_id=1, source_target_pairs={{0,16},{1,17},{2,18},{3,19},{4,20},{5,21},{6,22},{7,23},{8,24},{9,... | collective-permute-start | bytes 1204232 | tf_op jit(solution)/shard_map/ppermute | solution.py:29
  20.7 21.9 %collective-permute-start.13 = (bf16[224,896]{1,0:T(8,128)(2,1)}, bf16[224,896]{1,0:T(8,128)(2,1)S(1)}, u32[]{:S(2)}, u32[]{:S(2)}) collective-permute-start(bf16[224,896]{1,0:T(8,128)(2,1)} %get-tuple-element.360), channel_id=1, source_target_pairs={{0,8},{1,9},{2,10},{3,11},{4,12},{5,13},{6,14},{7,15},{8,0},{9,1},... | collective-permute-start | bytes 1204232 | tf_op jit(solution)/shard_map/ppermute | solution.py:29
  35.8 24.1 %collective-permute-start.11 = (bf16[224,896]{1,0:T(8,128)(2,1)}, bf16[224,896]{1,0:T(8,128)(2,1)S(1)}, u32[]{:S(2)}, u32[]{:S(2)}) collective-permute-start(bf16[224,896]{1,0:T(8,128)(2,1)} %get-tuple-element.362), channel_id=1, source_target_pairs={{0,2},{1,3},{2,0},{3,1},{4,6},{5,7},{6,4},{7,5},{8,10},{9,11},{10,... | collective-permute-start | bytes 1204232 | tf_op jit(solution)/shard_map/ppermute | solution.py:29
  37.7 22.2 %collective-permute-start.10 = (bf16[224,896]{1,0:T(8,128)(2,1)S(1)}, bf16[224,896]{1,0:T(8,128)(2,1)S(1)}, u32[]{:S(2)}, u32[]{:S(2)}) collective-permute-start(bf16[224,896]{1,0:T(8,128)(2,1)S(1)} %get-tuple-element.363), channel_id=1, source_target_pairs={{0,1},{1,0},{2,3},{3,2},{4,5},{5,4},{6,7},{7,6},{8,9},{9,8},{10,11... | collective-permute-start | bytes 1204232 | tf_op jit(solution)/shard_map/ppermute | solution.py:29
  85.2 21.3 %collective-permute-start.6 = (bf16[224,896]{1,0:T(8,128)(2,1)}, bf16[224,896]{1,0:T(8,128)(2,1)S(1)}, u32[]{:S(2)}, u32[]{:S(2)}) collective-permute-start(bf16[224,896]{1,0:T(8,128)(2,1)} %get-tuple-element.362), channel_id=1, source_target_pairs={{0,2},{1,3},{2,0},{3,1},{4,6},{5,7},{6,4},{7,5},{8,10},{9,11},{10,... | collective-permute-start | bytes 1204232 | tf_op jit(solution)/shard_map/ppermute | solution.py:29
  85.2 22.6 %collective-permute-start.5 = (bf16[224,896]{1,0:T(8,128)(2,1)S(1)}, bf16[224,896]{1,0:T(8,128)(2,1)S(1)}, u32[]{:S(2)}, u32[]{:S(2)}) collective-permute-start(bf16[224,896]{1,0:T(8,128)(2,1)S(1)} %copy-done.19), channel_id=1, source_target_pairs={{0,1},{1,0},{2,3},{3,2},{4,5},{5,4},{6,7},{7,6},{8,9},{9,8},{10,11... | collective-permute-start | bytes 1204232 | tf_op jit(solution)/shard_map/ppermute | solution.py:29
  88.7 20.5 %collective-permute-start.25 = (bf16[256,224]{1,0:T(8,128)(2,1)S(1)}, bf16[256,224]{1,0:T(8,128)(2,1)S(1)}, u32[]{:S(2)}, u32[]{:S(2)}) collective-permute-start(bf16[256,224]{1,0:T(8,128)(2,1)S(1)} %add_convert_fusion.14), channel_id=1, source_target_pairs={{0,48},{1,49},{2,50},{3,51},{4,52},{5,53},{6,54},{7,55},{8,56},{9,... | collective-permute-start | bytes 344072 | tf_op jit(solution)/shard_map/ppermute | solution.py:29
  211.9 20.7 %collective-permute-start.69 = (bf16[256,224]{1,0:T(8,128)(2,1)S(1)}, bf16[256,224]{1,0:T(8,128)(2,1)S(1)}, u32[]{:S(2)}, u32[]{:S(2)}) collective-permute-start(bf16[256,224]{1,0:T(8,128)(2,1)S(1)} %add_convert_fusion.10), channel_id=1, source_target_pairs={{0,48},{1,49},{2,50},{3,51},{4,52},{5,53},{6,54},{7,55},{8,56},{9,... | collective-permute-start | bytes 344072 | tf_op jit(solution)/shard_map/ppermute | solution.py:29
  406.0 26.8 %collective-permute-start.136 = (bf16[256,896]{1,0:T(8,128)(2,1)S(1)}, bf16[256,896]{1,0:T(8,128)(2,1)S(1)}, u32[]{:S(2)}, u32[]{:S(2)}) collective-permute-start(bf16[256,896]{1,0:T(8,128)(2,1)S(1)} %copy-done.6), channel_id=1, source_target_pairs={{0,4},{1,5},{2,6},{3,7},{4,0},{5,1},{6,2},{7,3},{8,12},{9,13},{10,... | collective-permute-start | bytes 1376264 | tf_op jit(solution)/shard_map/ppermute | solution.py:29
  408.9 26.6 %collective-permute-start.137 = (bf16[256,896]{1,0:T(8,128)(2,1)S(1)}, bf16[256,896]{1,0:T(8,128)(2,1)S(1)}, u32[]{:S(2)}, u32[]{:S(2)}) collective-permute-start(bf16[256,896]{1,0:T(8,128)(2,1)S(1)} %copy-done.6), channel_id=1, source_target_pairs={{0,16},{1,17},{2,18},{3,19},{4,20},{5,21},{6,22},{7,23},{8,24},{9,... | collective-permute-start | bytes 1376264 | tf_op jit(solution)/shard_map/ppermute | solution.py:29
  410.8 37.3 %collective-permute-start.138 = (bf16[256,896]{1,0:T(8,128)(2,1)S(1)}, bf16[256,896]{1,0:T(8,128)(2,1)S(1)}, u32[]{:S(2)}, u32[]{:S(2)}) collective-permute-start(bf16[256,896]{1,0:T(8,128)(2,1)S(1)} %copy-done.6), channel_id=1, source_target_pairs={{0,2},{1,3},{2,0},{3,1},{4,6},{5,7},{6,4},{7,5},{8,10},{9,11},{10,... | collective-permute-start | bytes 1376264 | tf_op jit(solution)/shard_map/ppermute | solution.py:29
  411.5 22.0 %collective-permute-start.135 = (bf16[256,224]{1,0:T(8,128)(2,1)S(1)}, bf16[256,224]{1,0:T(8,128)(2,1)S(1)}, u32[]{:S(2)}, u32[]{:S(2)}) collective-permute-start(bf16[256,224]{1,0:T(8,128)(2,1)S(1)} %add_convert_fusion.4), channel_id=1, source_target_pairs={{64,48},{65,49},{66,50},{67,51},{68,52},{69,53},{70,54},{71,55},{7... | collective-permute-start | bytes 344072 | tf_op jit(solution)/shard_map/ppermute | solution.py:29
  412.1 22.0 %collective-permute-start.134 = (bf16[256,224]{1,0:T(8,128)(2,1)S(1)}, bf16[256,224]{1,0:T(8,128)(2,1)S(1)}, u32[]{:S(2)}, u32[]{:S(2)}) collective-permute-start(bf16[256,224]{1,0:T(8,128)(2,1)S(1)} %add_convert_fusion.4), channel_id=1, source_target_pairs={{64,40},{65,41},{66,42},{67,43},{68,44},{69,45},{70,46},{71,47},{7... | collective-permute-start | bytes 344072 | tf_op jit(solution)/shard_map/ppermute | solution.py:29
  462.3 27.3 %collective-permute-start.150 = (bf16[256,896]{1,0:T(8,128)(2,1)S(1)}, bf16[256,896]{1,0:T(8,128)(2,1)S(1)}, u32[]{:S(2)}, u32[]{:S(2)}) collective-permute-start(bf16[256,896]{1,0:T(8,128)(2,1)S(1)} %copy-done.6), channel_id=1, source_target_pairs={{0,8},{1,9},{2,10},{3,11},{4,12},{5,13},{6,14},{7,15},{8,0},{9,1},... | collective-permute-start | bytes 1376264 | tf_op jit(solution)/shard_map/ppermute | solution.py:29
  462.6 20.7 %collective-permute-start.149 = (bf16[256,224]{1,0:T(8,128)(2,1)S(1)}, bf16[256,224]{1,0:T(8,128)(2,1)S(1)}, u32[]{:S(2)}, u32[]{:S(2)}) collective-permute-start(bf16[256,224]{1,0:T(8,128)(2,1)S(1)} %add_convert_fusion.3), channel_id=1, source_target_pairs={{32,16},{33,17},{34,18},{35,19},{36,20},{37,21},{38,22},{39,23},{4... | collective-permute-start | bytes 344072 | tf_op jit(solution)/shard_map/ppermute | solution.py:29
  463.8 20.7 %collective-permute-start.148 = (bf16[256,224]{1,0:T(8,128)(2,1)S(1)}, bf16[256,224]{1,0:T(8,128)(2,1)S(1)}, u32[]{:S(2)}, u32[]{:S(2)}) collective-permute-start(bf16[256,224]{1,0:T(8,128)(2,1)S(1)} %add_convert_fusion.3), channel_id=1, source_target_pairs={{32,8},{33,9},{34,10},{35,11},{36,12},{37,13},{38,14},{39,15},{40,... | collective-permute-start | bytes 344072 | tf_op jit(solution)/shard_map/ppermute | solution.py:29
  465.1 20.7 %collective-permute-start.147 = (bf16[256,224]{1,0:T(8,128)(2,1)S(1)}, bf16[256,224]{1,0:T(8,128)(2,1)S(1)}, u32[]{:S(2)}, u32[]{:S(2)}) collective-permute-start(bf16[256,224]{1,0:T(8,128)(2,1)S(1)} %add_convert_fusion.3), channel_id=1, source_target_pairs={{32,4},{33,5},{34,6},{35,7},{36,0},{37,1},{38,2},{39,3},{40,12},{4... | collective-permute-start | bytes 344072 | tf_op jit(solution)/shard_map/ppermute | solution.py:29
  532.1 31.7 %collective-permute-start.173 = (bf16[256,224]{1,0:T(8,128)(2,1)S(1)}, bf16[256,224]{1,0:T(8,128)(2,1)S(1)}, u32[]{:S(2)}, u32[]{:S(2)}) collective-permute-start(bf16[256,224]{1,0:T(8,128)(2,1)S(1)} %add_convert_fusion.1), channel_id=1, source_target_pairs={{32,16},{33,17},{34,18},{35,19},{36,20},{37,21},{38,22},{39,23},{4... | collective-permute-start | bytes 344072 | tf_op jit(solution)/shard_map/ppermute | solution.py:29
  533.4 31.7 %collective-permute-start.172 = (bf16[256,224]{1,0:T(8,128)(2,1)S(1)}, bf16[256,224]{1,0:T(8,128)(2,1)S(1)}, u32[]{:S(2)}, u32[]{:S(2)}) collective-permute-start(bf16[256,224]{1,0:T(8,128)(2,1)S(1)} %add_convert_fusion.1), channel_id=1, source_target_pairs={{32,8},{33,9},{34,10},{35,11},{36,12},{37,13},{38,14},{39,15},{40,... | collective-permute-start | bytes 344072 | tf_op jit(solution)/shard_map/ppermute | solution.py:29
  534.7 35.1 %collective-permute-start.171 = (bf16[256,224]{1,0:T(8,128)(2,1)S(1)}, bf16[256,224]{1,0:T(8,128)(2,1)S(1)}, u32[]{:S(2)}, u32[]{:S(2)}) collective-permute-start(bf16[256,224]{1,0:T(8,128)(2,1)S(1)} %add_convert_fusion.1), channel_id=1, source_target_pairs={{32,4},{33,5},{34,6},{35,7},{36,0},{37,1},{38,2},{39,3},{40,12},{4... | collective-permute-start | bytes 344072 | tf_op jit(solution)/shard_map/ppermute | solution.py:29
  536.0 35.6 %collective-permute-start.170 = (bf16[256,224]{1,0:T(8,128)(2,1)S(1)}, bf16[256,224]{1,0:T(8,128)(2,1)S(1)}, u32[]{:S(2)}, u32[]{:S(2)}) collective-permute-start(bf16[256,224]{1,0:T(8,128)(2,1)S(1)} %add_convert_fusion.1), channel_id=1, source_target_pairs={{32,2},{33,3},{34,0},{35,1},{36,6},{37,7},{38,4},{39,5},{40,10},{4... | collective-permute-start | bytes 344072 | tf_op jit(solution)/shard_map/ppermute | solution.py:29
  537.3 34.3 %collective-permute-start.169 = (bf16[256,224]{1,0:T(8,128)(2,1)S(1)}, bf16[256,224]{1,0:T(8,128)(2,1)S(1)}, u32[]{:S(2)}, u32[]{:S(2)}) collective-permute-start(bf16[256,224]{1,0:T(8,128)(2,1)S(1)} %add_convert_fusion.1), channel_id=1, source_target_pairs={{32,1},{33,0},{34,3},{35,2},{36,5},{37,4},{38,7},{39,6},{40,9},{41... | collective-permute-start | bytes 344072 | tf_op jit(solution)/shard_map/ppermute | solution.py:29
  (178 other events, 1727.0 us)

commit v3 on v2

v3 whole, which is shorter than its diff:
```python
import functools

import jax
import jax.numpy as jnp
from jax import lax
from jax.experimental import pallas as pl
from jax.experimental.pallas import tpu as pltpu
from jax.sharding import PartitionSpec as P

AXES = ("pipe", "tensor")
GELU_C = 0.7978845608028654
GELU_A = 0.044715
VMEM = pl.BlockSpec(memory_space=pltpu.VMEM)
SMEM = pl.BlockSpec(memory_space=pltpu.SMEM)
ANY = pl.BlockSpec(memory_space=pl.ANY)
F32 = jnp.float32
BF16 = jnp.bfloat16


def partner(index, term):
    return index if term == 0 else index ^ (1 << (term - 1))


def send(value, term, routes):
    width = lax.axis_size("tensor")
    pairs = [
        (a * width + i, b * width + partner(i, term)) for a, b in routes for i in range(width)
    ]
    return lax.ppermute(value, AXES, pairs)


def column_chunks(width):
    return [(start, min(256, width - start)) for start in range(0, width, 256)]


def dot_nn(a, b):
    return lax.dot_general(a, b, (((1,), (0,)), ((), ())), preferred_element_type=F32)


def dot_nt(a, b):
    return lax.dot_general(a, b, (((1,), (1,)), ((), ())), preferred_element_type=F32)


def dot_tn(a, b):
    return lax.dot_general(a, b, (((0,), (0,)), ((), ())), preferred_element_type=F32)


def in_order(refs, order):
    by_term = dict(zip(order, refs))
    return [by_term[k] for k in range(len(refs))]


def forward_kernel(n, layer, last, order, rider, tokens, n_state, *refs):
    place, refs = refs[0], refs[1:]
    ins, refs = in_order(refs[:n], order), refs[n:]
    first, refs = refs[0], refs[1:]
    second, refs = refs[:n], refs[n:]
    riding, refs = (refs[0], refs[1:]) if rider is not None else (None, refs)
    refs = refs[n_state:]
    st_ins, st_pre, st_hid = refs[:3]
    outs, refs = (refs[3:3], refs[3:]) if last else (refs[3 : 3 + n], refs[3 + n :])
    preact, hidden, pieces, sems = refs
    rows = pl.ds(0, tokens)
    slab = ins[0].shape[1]

    @pl.when(place[0] == layer)
    def _():
        saves = [
            pltpu.make_async_copy(ins[k].at[rows], st_ins.at[k], sems.at[k]) for k in range(n)
        ]
        for copy in saves:
            copy.start()
        for start, size in column_chunks(preact.shape[1]):
            cols = slice(start, start + size)
            total = dot_nn(ins[0][rows, :], first[0, :, cols])
            for k in range(1, n):
                total = total + dot_nn(ins[k][rows, :], first[k, :, cols])
            preact[:, cols] = total
            inner = GELU_C * (total + GELU_A * (total * total * total))
            hidden[:, cols] = (0.5 * total * (1.0 + jnp.tanh(inner))).astype(BF16)
        save_pre = pltpu.make_async_copy(preact, st_pre, sems.at[n])
        save_pre.start()
        if not last:
            outs[0][...] = ins[0][rows, :].astype(F32) + dot_nt(hidden[...], second[0][...])
            for k in range(1, n):
                outs[k][...] = dot_nt(hidden[...], second[k][...]).astype(BF16)
        for c in range(pieces.shape[0]):
            pieces[c] = hidden[:, c * slab : (c + 1) * slab]
        save_hid = pltpu.make_async_copy(pieces, st_hid, sems.at[n + 1])
        save_hid.start()
        for copy in saves:
            copy.wait()
        save_pre.wait()
        save_hid.wait()

    if rider is not None:

        @pl.when(place[0] == rider)
        def _():
            for k in range(1, n):
                outs[k][...] = riding[...]


def idle_half(me, layer, half):
    return me < half if layer >= half else me >= half


def reduce_kernel(n, order, out_layer, n_state, *refs):
    place, terms, refs = refs[0], refs[1], refs[2:]
    got, refs = dict(zip(order, refs[: n - 1])), refs[n - 1 + n_state :]
    out, refs = refs[0], refs[1:]
    total = terms[...]
    for k in order:
        total = total + got[k][...].astype(F32)
    out[...] = total.astype(BF16)
    if out_layer is not None:
        st_out, sem = refs

        @pl.when(place[0] == out_layer)
        def _():
            copy = pltpu.make_async_copy(out, st_out, sem.at[0])
            copy.start()
            copy.wait()


def backward_kernel(n, layer, half, order, tokens, piece, earlier, n_state, *refs):
    place, refs = refs[0], refs[1:]
    ins, refs = in_order(refs[:n], order), refs[n:]
    first, refs = refs[0], refs[1:]
    second, refs = refs[:n], refs[n:]
    st_pre, st_hid, refs = refs[0], refs[1], refs[2:]
    got, refs = (refs[: n - 1], refs[n - 1 :]) if earlier is not None else (None, refs)
    refs = refs[n_state:]
    st_dpre, st_grad, st_near = refs[:3]
    outs, refs = refs[3 : 3 + n], refs[3 + n :]
    preact, dpre, sems = refs
    rows = pl.ds(0, tokens)

    @pl.when(place[0] == layer)
    def _():
        from_pre = pltpu.make_async_copy(st_pre, preact, sems.at[0])
        from_pre.start()
        save_grad = pltpu.make_async_copy(ins[0].at[rows], st_grad, sems.at[1])
        save_grad.start()
        for start, size in column_chunks(preact.shape[1]):
            cols = slice(start, start + size)
            total = dot_nn(ins[0][rows, :], second[0][:, cols])
            for k in range(1, n):
                total = total + dot_nn(ins[k][rows, :], second[k][:, cols])
            if start == 0:
                from_pre.wait()
            x = preact[:, cols]
            square = x * x
            bent = jnp.tanh(GELU_C * (x + GELU_A * (square * x)))
            slope = 0.5 * (1.0 + bent) + 0.5 * x * (1.0 - bent * bent) * (
                GELU_C * (1.0 + 3.0 * GELU_A * square)
            )
            dpre[:, cols] = (total * slope).astype(BF16)
        save_dpre = pltpu.make_async_copy(dpre, st_dpre, sems.at[2])
        save_dpre.start()
        outs[0][...] = ins[0][rows, :].astype(F32) + dot_nt(dpre[...], first[0])
        for k in range(1, n):
            outs[k][...] = dot_nt(dpre[...], first[k]).astype(BF16)
        save_grad.wait()
        save_dpre.wait()

    @pl.when(idle_half(place[0], layer, half))
    def _():
        copies = [
            pltpu.make_async_copy(st_hid.at[piece], outs[k], sems.at[k]) for k in range(1, n)
        ]
        for copy in copies:
            copy.start()
        for copy in copies:
            copy.wait()

    if earlier is not None:

        @pl.when(idle_half(place[0], layer + 1, half))
        def _():
            copies = [
                pltpu.make_async_copy(got[k], st_near.at[earlier, k], sems.at[n + k])
                for k in range(n - 1)
            ]
            for copy in copies:
                copy.start()
            for copy in copies:
                copy.wait()


def grad_kernel(n, half, *refs):
    place, ins, dpre, own, near, refs = refs[0], refs[1], refs[2], refs[3], refs[4], refs[5:]
    got, grad, refs = refs[: n - 1], refs[n - 1], refs[n:]
    out_first, out_second, v_first, v_second, block, sems = refs
    n_pieces, slab = own.shape[0], own.shape[2]
    copies = []
    for k in range(n):
        v_first[k] = dot_tn(ins[k], dpre[...]).astype(BF16)
        copies.append(pltpu.make_async_copy(v_first.at[k], out_first.at[k], sems.at[k]))
        copies[-1].start()
    for k in range(n):
        for c in range(n_pieces):
            cols = slice(c * slab, (c + 1) * slab)
            if k == 0:
                block[:, cols] = own[c]
            elif c < n_pieces - 1:
                block[:, cols] = near[c, k - 1]
            else:
                block[:, cols] = jnp.where(place[0] >= half, got[k - 1][...], near[c, k - 1])
        v_second[k] = dot_tn(grad[...], block[...]).astype(BF16)
        copies.append(pltpu.make_async_copy(v_second.at[k], out_second.at[k], sems.at[n + k]))
        copies[-1].start()
    for copy in copies:
        copy.wait()


def body(x_in, cotangent, w_in, w_out):
    sections = lax.axis_size("pipe")
    n = lax.axis_size("tensor").bit_length()
    me = lax.axis_index("pipe")
    batches, tok_rows, slab = x_in.shape
    tokens = batches * tok_rows
    first = w_in[0]
    owned = jnp.swapaxes(w_out[0], 1, 2)
    hid = first.shape[2]
    n_pieces = hid // slab
    shape = jax.ShapeDtypeStruct
    cost = pl.CostEstimate(
        flops=4 * tokens * n * slab * hid, bytes_accessed=4 * n * slab * hid, transcendentals=0
    )
    params = pltpu.CompilerParams(vmem_limit_bytes=12 * 1024 * 1024)
    work = [pltpu.VMEM((tokens, hid), F32), pltpu.VMEM((tokens, hid), BF16)]
    term_shapes = [shape((tokens, slab), F32)] + [shape((tokens, slab), BF16)] * (n - 1)

    everyone = [(s, s) for s in range(sections)]
    order = [k for k in (3, 5, 2, 4, 1) if k < n]

    def exchange(values, routes):
        got = {k: send(values[k], k, routes) for k in order}
        return [got[k] for k in range(1, n)]

    def neighbours(layer, step):
        return [
            (s, s + step)
            for s in range(layer % 2, sections, 2)
            if 0 <= s + step < sections
        ]

    def reduced(terms, got, out_layer=None, state=()):
        saves = out_layer is not None
        return pl.pallas_call(
            functools.partial(reduce_kernel, n, order, out_layer, len(state)),
            out_shape=[shape((tokens, slab), BF16)] * (1 + saves),
            in_specs=[SMEM] + [VMEM] * n + [ANY] * len(state),
            out_specs=[VMEM] + [ANY] * saves,
            scratch_shapes=[pltpu.SemaphoreType.DMA((1,))] * saves,
            input_output_aliases={1 + n: 1} if state else {},
            compiler_params=params,
        )(place, terms[0], *[got[k - 1] for k in order], *state)

    half = sections // 2
    place = me.astype(jnp.int32).reshape(1)
    x = x_in.reshape(tokens, slab)
    cot = cotangent.reshape(tokens, slab)
    ins = [x] + exchange([x] * n, everyone)
    second = [owned[0]] + exchange(owned, everyone)
    operands = [k for k in (0, 1, 4, 2, 3, 5) if k < n]

    state = []
    for layer in range(sections):
        last = layer == sections - 1
        rider = sections - 1 if layer == 0 else None
        riding = [cot] if layer == 0 else []
        state_shapes = [
            shape((n, tokens, slab), BF16),
            shape((tokens, hid), F32),
            shape((n_pieces, tokens, slab), BF16),
        ]
        outs = [] if last else term_shapes
        results = pl.pallas_call(
            functools.partial(forward_kernel, n, layer, last, operands, rider, tokens, len(state)),
            out_shape=state_shapes + outs,
            in_specs=[SMEM] + [VMEM] * (2 * n + 1 + len(riding)) + [ANY] * len(state),
            out_specs=[ANY] * 3 + [VMEM] * len(outs),
            scratch_shapes=work
            + [pltpu.VMEM((n_pieces, tokens, slab), BF16), pltpu.SemaphoreType.DMA((n + 2,))],
            input_output_aliases={2 + 2 * n + len(riding) + i: i for i in range(len(state))},
            cost_estimate=cost,
            compiler_params=params,
        )(place, *[ins[k] for k in operands], first, *second, *riding, *state)
        state, terms = list(results[:3]), results[3:]
        if last:
            break
        got = exchange(terms, everyone)
        if layer == 0:
            first_grads = [cot] + got
        (out,) = reduced(terms, got)
        route = neighbours(layer, 1)
        ins = exchange([out] * n, route)
        ins = [send(out, 0, route)] + ins

    st_ins, st_pre, st_hid = state
    state = []
    got = []
    grads_in = first_grads
    st_out = []
    for layer in reversed(range(sections)):
        piece = (sections - 1 - layer) % half
        earlier = (piece - 1) % half if got else None
        results = pl.pallas_call(
            functools.partial(
                backward_kernel,
                n,
                layer,
                half,
                operands,
                tokens,
                piece,
                earlier,
                len(state),
            ),
            out_shape=[
                shape((tokens, hid), BF16),
                shape((tokens, slab), BF16),
                shape((n_pieces, n - 1, tokens, slab), BF16),
            ]
            + term_shapes,
            in_specs=[SMEM]
            + [VMEM] * (2 * n + 1)
            + [ANY] * 2
            + [VMEM] * len(got)
            + [ANY] * len(state),
            out_specs=[ANY] * 3 + [VMEM] * n,
            scratch_shapes=work + [pltpu.SemaphoreType.DMA((2 * n,))],
            input_output_aliases={4 + 2 * n + len(got) + i: i for i in range(len(state))},
            cost_estimate=cost,
            compiler_params=params,
        )(
            place,
            *[grads_in[k] for k in operands],
            first,
            *second,
            st_pre,
            st_hid,
            *got,
            *state,
        )
        state, terms = list(results[:3]), results[3:]
        got = exchange(terms, everyone)
        out, st_out = reduced(terms, got, layer, st_out)
        st_out = [st_out]
        if layer > 0:
            route = neighbours(layer, -1)
            grads_in = exchange([out] * n, route)
            grads_in = [send(out, 0, route)] + grads_in

    st_dpre, st_grad, st_near = state
    grad_first, grad_second = pl.pallas_call(
        functools.partial(grad_kernel, n, half),
        out_shape=[shape((n, slab, hid), BF16)] * 2,
        in_specs=[SMEM] + [VMEM] * (4 + n),
        out_specs=[ANY] * 2,
        scratch_shapes=[pltpu.VMEM((n, slab, hid), BF16)] * 2
        + [pltpu.VMEM((tokens, hid), BF16), pltpu.SemaphoreType.DMA((2 * n,))],
        cost_estimate=cost,
        compiler_params=params,
    )(place, st_ins, st_dpre, st_hid, st_near, *got, st_grad)
    acts = st_out[0].reshape(batches, tok_rows, slab)
    return acts[None], grad_first[None], jnp.swapaxes(grad_second, 1, 2)[None]


def solution(mesh):
    placed = (
        P(None, None, "tensor"),
        P(None, None, "tensor"),
        P("pipe", None, None, "tensor"),
        P("pipe", None, None, "tensor"),
    )
    return jax.shard_map(
        body,
        mesh=mesh,
        in_specs=placed,
        out_specs=(P("pipe", None, None, "tensor"),) * 3,
        check_vma=False,
    )
```

time: 602 us -> 563 us (0.935)
  the two profiles are of different devices: /device:TPU:8 before, /device:TPU:5 now
where the time goes in v3:
time: 563 us; the launch traced here: 553 us
  starting transfers between devices  255 us (45%)
  waiting for transfers between devices  241 us (43%)
  Pallas kernels  44.1 us (8%)
  local copies, waits for them, and re-layouts  10.7 us (2%)
    ppermute x169, starting transfers between devices, send(): return lax.ppermute(value, AXES, pairs)  255 us
    ppermute x169, waiting for transfers between devices, send(): return lax.ppermute(value, AXES, pairs)  241 us
    pallas_call x8, Pallas kernels, body(): pl.pallas_call(functools.partial(backward_kernel, n, layer, half, operand...  23 us
    pallas_call x8, Pallas kernels, body(): pl.pallas_call(functools.partial(forward_kernel, n, layer, last, operands...  15.5 us
  transfers between devices with their start and end apart: 169, of which 75 were waited for; matrix products, arithmetic and copies ran while one was open for 1% of the time, Pallas kernels for 0%

profile of v3, /device:TPU:5, one launch (start us, length us, event | category | flops | bytes accessed | tf_op | source)
XLA Modules:
  0.0 553.1 jit_solution(9879821676446679390)
XLA Ops:
  3.7 6.9 %collective-permute-start.3 = (bf16[256,224]{1,0:T(8,128)(2,1)}, bf16[256,224]{1,0:T(8,128)(2,1)S(1)}, u32[]{:S(2)}, u32[]{:S(2)}) collective-permute-start(bf16[256,224]{1,0:T(8,128)(2,1)} %bitcast.43), channel_id=1, source_target_pairs={{0,4},{1,5},{2,6},{3,7},{4,0},{5,1},{6,2},{7,3},{8,12},{9,13},{10,... | collective-permute-start | bytes 344072 | tf_op jit(solution)/shard_map/ppermute | solution.py:29
  18.7 5.0 collective-permute-done.2.refs_4_
  28.8 5.2 collective-permute-done.8.refs_12_
  34.0 12.1 %collective-permute-done.7.refs_11_ = bf16[224,896]{1,0:T(8,128)(2,1)} collective-permute-done((bf16[224,896]{1,0:T(8,128)(2,1)}, bf16[224,896]{1,0:T(8,128)(2,1)}, u32[]{:S(2)}, u32[]{:S(2)}) %collective-permute-start.7) | collective-permute-done | bytes 401440 | tf_op jit(solution)/shard_map/ppermute | solution.py:29
  46.1 17.0 %collective-permute-done.6.refs_10_ = bf16[224,896]{1,0:T(8,128)(2,1)} collective-permute-done((bf16[224,896]{1,0:T(8,128)(2,1)}, bf16[224,896]{1,0:T(8,128)(2,1)}, u32[]{:S(2)}, u32[]{:S(2)}) %collective-permute-start.6) | collective-permute-done | bytes 401440 | tf_op jit(solution)/shard_map/ppermute | solution.py:29
  75.3 5.4 collective-permute-done.13.refs_2_.refs_5_
  97.6 4.1 collective-permute-start.21
  107.4 8.1 %collective-permute-done.23.refs_4_ = bf16[256,224]{1,0:T(8,128)(2,1)S(1)} collective-permute-done((bf16[256,224]{1,0:T(8,128)(2,1)S(1)}, bf16[256,224]{1,0:T(8,128)(2,1)S(1)}, u32[]{:S(2)}, u32[]{:S(2)}) %collective-permute-start.23) | collective-permute-done | bytes 114720 | tf_op jit(solution)/shard_map/ppermute | solution.py:29
  139.6 5.6 %collective-permute-done.32.refs_2_ = bf16[256,224]{1,0:T(8,128)(2,1)S(1)} collective-permute-done((bf16[256,224]{1,0:T(8,128)(2,1)S(1)}, bf16[256,224]{1,0:T(8,128)(2,1)S(1)}, u32[]{:S(2)}, u32[]{:S(2)}) %collective-permute-start.32) | collective-permute-done | bytes 114720 | tf_op jit(solution)/shard_map/ppermute | solution.py:29
  176.3 5.7 %collective-permute-done.45.refs_4_ = bf16[256,224]{1,0:T(8,128)(2,1)S(1)} collective-permute-done((bf16[256,224]{1,0:T(8,128)(2,1)S(1)}, bf16[256,224]{1,0:T(8,128)(2,1)S(1)}, u32[]{:S(2)}, u32[]{:S(2)}) %collective-permute-start.45) | collective-permute-done | bytes 114720 | tf_op jit(solution)/shard_map/ppermute | solution.py:29
  211.8 12.2 %collective-permute-done.64.refs_6_ = bf16[256,224]{1,0:T(8,128)(2,1)S(1)} collective-permute-done((bf16[256,224]{1,0:T(8,128)(2,1)S(1)}, bf16[256,224]{1,0:T(8,128)(2,1)S(1)}, u32[]{:S(2)}, u32[]{:S(2)}) %collective-permute-start.64) | collective-permute-done | bytes 114720 | tf_op jit(solution)/shard_map/ppermute | solution.py:29
  229.1 5.0 shard_map.77
  279.1 5.5 %collective-permute-done.86.refs_6_ = bf16[256,224]{1,0:T(8,128)(2,1)S(1)} collective-permute-done((bf16[256,224]{1,0:T(8,128)(2,1)S(1)}, bf16[256,224]{1,0:T(8,128)(2,1)S(1)}, u32[]{:S(2)}, u32[]{:S(2)}) %collective-permute-start.86) | collective-permute-done | bytes 114720 | tf_op jit(solution)/shard_map/ppermute | solution.py:29
  302.2 7.0 %collective-permute-done.89.refs_4_.refs_17_ = bf16[256,224]{1,0:T(8,128)(2,1)S(1)} collective-permute-done((bf16[256,224]{1,0:T(8,128)(2,1)S(1)}, bf16[256,224]{1,0:T(8,128)(2,1)S(1)}, u32[]{:S(2)}, u32[]{:S(2)}) %collective-permute-start.89) | collective-permute-done | bytes 114720 | tf_op jit(solution)/shard_map/ppermute | solution.py:29
  309.3 4.2 collective-permute-start.97
  331.7 9.1 %collective-permute-done.100.refs_4_.refs_17_ = bf16[256,224]{1,0:T(8,128)(2,1)S(1)} collective-permute-done((bf16[256,224]{1,0:T(8,128)(2,1)S(1)}, bf16[256,224]{1,0:T(8,128)(2,1)S(1)}, u32[]{:S(2)}, u32[]{:S(2)}) %collective-permute-start.100) | collective-permute-done | bytes 114720 | tf_op jit(solution)/shard_map/ppermute | solution.py:29
  350.8 6.7 %collective-permute-done.107.refs_5_ = bf16[256,224]{1,0:T(8,128)(2,1)S(1)} collective-permute-done((bf16[256,224]{1,0:T(8,128)(2,1)S(1)}, bf16[256,224]{1,0:T(8,128)(2,1)S(1)}, u32[]{:S(2)}, u32[]{:S(2)}) %collective-permute-start.107) | collective-permute-done | bytes 114720 | tf_op jit(solution)/shard_map/ppermute | solution.py:29
  359.1 4.9 shard_map.86
  373.9 7.0 %collective-permute-done.111.refs_4_.refs_17_ = bf16[256,224]{1,0:T(8,128)(2,1)S(1)} collective-permute-done((bf16[256,224]{1,0:T(8,128)(2,1)S(1)}, bf16[256,224]{1,0:T(8,128)(2,1)S(1)}, u32[]{:S(2)}, u32[]{:S(2)}) %collective-permute-start.111) | collective-permute-done | bytes 114720 | tf_op jit(solution)/shard_map/ppermute | solution.py:29
  416.6 7.0 %collective-permute-done.129.refs_5_ = bf16[256,224]{1,0:T(8,128)(2,1)S(1)} collective-permute-done((bf16[256,224]{1,0:T(8,128)(2,1)S(1)}, bf16[256,224]{1,0:T(8,128)(2,1)S(1)}, u32[]{:S(2)}, u32[]{:S(2)}) %collective-permute-start.129) | collective-permute-done | bytes 114720 | tf_op jit(solution)/shard_map/ppermute | solution.py:29
  440.4 11.4 %collective-permute-start.141 = (bf16[256,224]{1,0:T(8,128)(2,1)S(1)}, bf16[256,224]{1,0:T(8,128)(2,1)S(1)}, u32[]{:S(2)}, u32[]{:S(2)}) collective-permute-start(bf16[256,224]{1,0:T(8,128)(2,1)S(1)} %get-tuple-element.273), channel_id=1, source_target_pairs={{32,16},{33,17},{34,18},{35,19},{36,20},{37,21},{38,22},{39,23},{4... | collective-permute-start | bytes 344072 | tf_op jit(solution)/shard_map/ppermute | solution.py:29
  472.5 8.1 %collective-permute-done.144.refs_4_.refs_17_ = bf16[256,224]{1,0:T(8,128)(2,1)S(1)} collective-permute-done((bf16[256,224]{1,0:T(8,128)(2,1)S(1)}, bf16[256,224]{1,0:T(8,128)(2,1)S(1)}, u32[]{:S(2)}, u32[]{:S(2)}) %collective-permute-start.144) | collective-permute-done | bytes 114720 | tf_op jit(solution)/shard_map/ppermute | solution.py:29
  490.7 4.9 collective-permute-done.151.refs_5_
  541.0 8.1 %collective-permute-done.166.refs_4_.refs_6_ = bf16[256,224]{1,0:T(8,128)(2,1)S(1)} collective-permute-done((bf16[256,224]{1,0:T(8,128)(2,1)S(1)}, bf16[256,224]{1,0:T(8,128)(2,1)S(1)}, u32[]{:S(2)}, u32[]{:S(2)}) %collective-permute-start.166) | collective-permute-done | bytes 114720 | tf_op jit(solution)/shard_map/ppermute | solution.py:29
  (373 shorter events, 374.6 us)
Async XLA Ops:
  0.7 15.2 %collective-permute-start.4 = (bf16[256,224]{1,0:T(8,128)(2,1)}, bf16[256,224]{1,0:T(8,128)(2,1)S(1)}, u32[]{:S(2)}, u32[]{:S(2)}) collective-permute-start(bf16[256,224]{1,0:T(8,128)(2,1)} %bitcast.42), channel_id=1, source_target_pairs={{0,16},{1,17},{2,18},{3,19},{4,20},{5,21},{6,22},{7,23},{8,24},{9,... | collective-permute-start | bytes 344072 | tf_op jit(solution)/shard_map/ppermute | solution.py:29
  3.7 14.4 %collective-permute-start.3 = (bf16[256,224]{1,0:T(8,128)(2,1)}, bf16[256,224]{1,0:T(8,128)(2,1)S(1)}, u32[]{:S(2)}, u32[]{:S(2)}) collective-permute-start(bf16[256,224]{1,0:T(8,128)(2,1)} %bitcast.43), channel_id=1, source_target_pairs={{0,4},{1,5},{2,6},{3,7},{4,0},{5,1},{6,2},{7,3},{8,12},{9,13},{10,... | collective-permute-start | bytes 344072 | tf_op jit(solution)/shard_map/ppermute | solution.py:29
  12.2 14.2 %collective-permute-start = (bf16[256,224]{1,0:T(8,128)(2,1)}, bf16[256,224]{1,0:T(8,128)(2,1)S(1)}, u32[]{:S(2)}, u32[]{:S(2)}) collective-permute-start(bf16[256,224]{1,0:T(8,128)(2,1)} %bitcast.46), channel_id=1, source_target_pairs={{0,1},{1,0},{2,3},{3,2},{4,5},{5,4},{6,7},{7,6},{8,9},{9,8},{10,11... | collective-permute-start | bytes 344072 | tf_op jit(solution)/shard_map/ppermute | solution.py:29
  18.7 15.3 %collective-permute-start.8 = (bf16[224,896]{1,0:T(8,128)(2,1)}, bf16[224,896]{1,0:T(8,128)(2,1)}, u32[]{:S(2)}, u32[]{:S(2)}) collective-permute-start(bf16[224,896]{1,0:T(8,128)(2,1)} %get-tuple-element.314), channel_id=1, source_target_pairs={{0,8},{1,9},{2,10},{3,11},{4,12},{5,13},{6,14},{7,15},{8,0},{9,1},... | collective-permute-start | bytes 1204232 | tf_op jit(solution)/shard_map/ppermute | solution.py:29
  24.4 21.7 %collective-permute-start.7 = (bf16[224,896]{1,0:T(8,128)(2,1)}, bf16[224,896]{1,0:T(8,128)(2,1)}, u32[]{:S(2)}, u32[]{:S(2)}) collective-permute-start(bf16[224,896]{1,0:T(8,128)(2,1)} %get-tuple-element.315), channel_id=1, source_target_pairs={{0,4},{1,5},{2,6},{3,7},{4,0},{5,1},{6,2},{7,3},{8,12},{9,13},{10,... | collective-permute-start | bytes 1204232 | tf_op jit(solution)/shard_map/ppermute | solution.py:29
  26.4 36.7 %collective-permute-start.6 = (bf16[224,896]{1,0:T(8,128)(2,1)}, bf16[224,896]{1,0:T(8,128)(2,1)}, u32[]{:S(2)}, u32[]{:S(2)}) collective-permute-start(bf16[224,896]{1,0:T(8,128)(2,1)} %get-tuple-element.316), channel_id=1, source_target_pairs={{0,2},{1,3},{2,0},{3,1},{4,6},{5,7},{6,4},{7,5},{8,10},{9,11},{10,... | collective-permute-start | bytes 1204232 | tf_op jit(solution)/shard_map/ppermute | solution.py:29
  27.0 36.0 %collective-permute-start.5 = (bf16[224,896]{1,0:T(8,128)(2,1)}, bf16[224,896]{1,0:T(8,128)(2,1)}, u32[]{:S(2)}, u32[]{:S(2)}) collective-permute-start(bf16[224,896]{1,0:T(8,128)(2,1)} %get-tuple-element.317), channel_id=1, source_target_pairs={{0,1},{1,0},{2,3},{3,2},{4,5},{5,4},{6,7},{7,6},{8,9},{9,8},{10,11... | collective-permute-start | bytes 1204232 | tf_op jit(solution)/shard_map/ppermute | solution.py:29
  205.3 18.7 %collective-permute-start.64 = (bf16[256,224]{1,0:T(8,128)(2,1)S(1)}, bf16[256,224]{1,0:T(8,128)(2,1)S(1)}, u32[]{:S(2)}, u32[]{:S(2)}) collective-permute-start(bf16[256,224]{1,0:T(8,128)(2,1)S(1)} %shard_map.76), channel_id=1, source_target_pairs={{0,48},{1,49},{2,50},{3,51},{4,52},{5,53},{6,54},{7,55},{8,56},{9,... | collective-permute-start | bytes 344072 | tf_op jit(solution)/shard_map/ppermute | solution.py:29
  206.6 20.2 %collective-permute-start.63 = (bf16[256,224]{1,0:T(8,128)(2,1)S(1)}, bf16[256,224]{1,0:T(8,128)(2,1)S(1)}, u32[]{:S(2)}, u32[]{:S(2)}) collective-permute-start(bf16[256,224]{1,0:T(8,128)(2,1)S(1)} %shard_map.76), channel_id=1, source_target_pairs={{0,36},{1,37},{2,38},{3,39},{4,32},{5,33},{6,34},{7,35},{8,44},{9,... | collective-permute-start | bytes 344072 | tf_op jit(solution)/shard_map/ppermute | solution.py:29
  207.9 21.2 %collective-permute-start.62 = (bf16[256,224]{1,0:T(8,128)(2,1)S(1)}, bf16[256,224]{1,0:T(8,128)(2,1)S(1)}, u32[]{:S(2)}, u32[]{:S(2)}) collective-permute-start(bf16[256,224]{1,0:T(8,128)(2,1)S(1)} %shard_map.76), channel_id=1, source_target_pairs={{0,34},{1,35},{2,32},{3,33},{4,38},{5,39},{6,36},{7,37},{8,42},{9,... | collective-permute-start | bytes 344072 | tf_op jit(solution)/shard_map/ppermute | solution.py:29
  209.2 19.9 %collective-permute-start.61 = (bf16[256,224]{1,0:T(8,128)(2,1)S(1)}, bf16[256,224]{1,0:T(8,128)(2,1)S(1)}, u32[]{:S(2)}, u32[]{:S(2)}) collective-permute-start(bf16[256,224]{1,0:T(8,128)(2,1)S(1)} %shard_map.76), channel_id=1, source_target_pairs={{0,40},{1,41},{2,42},{3,43},{4,44},{5,45},{6,46},{7,47},{8,32},{9,... | collective-permute-start | bytes 344072 | tf_op jit(solution)/shard_map/ppermute | solution.py:29
  210.5 18.6 %collective-permute-start.60 = (bf16[256,224]{1,0:T(8,128)(2,1)S(1)}, bf16[256,224]{1,0:T(8,128)(2,1)S(1)}, u32[]{:S(2)}, u32[]{:S(2)}) collective-permute-start(bf16[256,224]{1,0:T(8,128)(2,1)S(1)} %shard_map.76), channel_id=1, source_target_pairs={{0,33},{1,32},{2,35},{3,34},{4,37},{5,36},{6,39},{7,38},{8,41},{9,... | collective-permute-start | bytes 344072 | tf_op jit(solution)/shard_map/ppermute | solution.py:29
  273.9 15.0 %collective-permute-start.85 = (bf16[256,224]{1,0:T(8,128)(2,1)S(1)}, bf16[256,224]{1,0:T(8,128)(2,1)S(1)}, u32[]{:S(2)}, u32[]{:S(2)}) collective-permute-start(bf16[256,224]{1,0:T(8,128)(2,1)S(1)} %shard_map.80), channel_id=1, source_target_pairs={{0,36},{1,37},{2,38},{3,39},{4,32},{5,33},{6,34},{7,35},{8,44},{9,... | collective-permute-start | bytes 344072 | tf_op jit(solution)/shard_map/ppermute | solution.py:29
  275.2 15.4 %collective-permute-start.84 = (bf16[256,224]{1,0:T(8,128)(2,1)S(1)}, bf16[256,224]{1,0:T(8,128)(2,1)S(1)}, u32[]{:S(2)}, u32[]{:S(2)}) collective-permute-start(bf16[256,224]{1,0:T(8,128)(2,1)S(1)} %shard_map.80), channel_id=1, source_target_pairs={{0,34},{1,35},{2,32},{3,33},{4,38},{5,39},{6,36},{7,37},{8,42},{9,... | collective-permute-start | bytes 344072 | tf_op jit(solution)/shard_map/ppermute | solution.py:29
  276.5 14.1 %collective-permute-start.83 = (bf16[256,224]{1,0:T(8,128)(2,1)S(1)}, bf16[256,224]{1,0:T(8,128)(2,1)S(1)}, u32[]{:S(2)}, u32[]{:S(2)}) collective-permute-start(bf16[256,224]{1,0:T(8,128)(2,1)S(1)} %shard_map.80), channel_id=1, source_target_pairs={{0,40},{1,41},{2,42},{3,43},{4,44},{5,45},{6,46},{7,47},{8,32},{9,... | collective-permute-start | bytes 344072 | tf_op jit(solution)/shard_map/ppermute | solution.py:29
  342.1 15.3 %collective-permute-start.107 = (bf16[256,224]{1,0:T(8,128)(2,1)S(1)}, bf16[256,224]{1,0:T(8,128)(2,1)S(1)}, u32[]{:S(2)}, u32[]{:S(2)}) collective-permute-start(bf16[256,224]{1,0:T(8,128)(2,1)S(1)} %get-tuple-element.240), channel_id=1, source_target_pairs={{64,36},{65,37},{66,38},{67,39},{68,32},{69,33},{70,34},{71,35},{7... | collective-permute-start | bytes 344072 | tf_op jit(solution)/shard_map/ppermute | solution.py:29
  343.4 14.4 %collective-permute-start.106 = (bf16[256,224]{1,0:T(8,128)(2,1)S(1)}, bf16[256,224]{1,0:T(8,128)(2,1)S(1)}, u32[]{:S(2)}, u32[]{:S(2)}) collective-permute-start(bf16[256,224]{1,0:T(8,128)(2,1)S(1)} %get-tuple-element.240), channel_id=1, source_target_pairs={{64,34},{65,35},{66,32},{67,33},{68,38},{69,39},{70,36},{71,37},{7... | collective-permute-start | bytes 344072 | tf_op jit(solution)/shard_map/ppermute | solution.py:29
  407.9 15.7 %collective-permute-start.129 = (bf16[256,224]{1,0:T(8,128)(2,1)S(1)}, bf16[256,224]{1,0:T(8,128)(2,1)S(1)}, u32[]{:S(2)}, u32[]{:S(2)}) collective-permute-start(bf16[256,224]{1,0:T(8,128)(2,1)S(1)} %get-tuple-element.262), channel_id=1, source_target_pairs={{64,36},{65,37},{66,38},{67,39},{68,32},{69,33},{70,34},{71,35},{7... | collective-permute-start | bytes 344072 | tf_op jit(solution)/shard_map/ppermute | solution.py:29
  409.2 17.7 %collective-permute-start.128 = (bf16[256,224]{1,0:T(8,128)(2,1)S(1)}, bf16[256,224]{1,0:T(8,128)(2,1)S(1)}, u32[]{:S(2)}, u32[]{:S(2)}) collective-permute-start(bf16[256,224]{1,0:T(8,128)(2,1)S(1)} %get-tuple-element.262), channel_id=1, source_target_pairs={{64,34},{65,35},{66,32},{67,33},{68,38},{69,39},{70,36},{71,37},{7... | collective-permute-start | bytes 344072 | tf_op jit(solution)/shard_map/ppermute | solution.py:29
  410.5 16.4 %collective-permute-start.127 = (bf16[256,224]{1,0:T(8,128)(2,1)S(1)}, bf16[256,224]{1,0:T(8,128)(2,1)S(1)}, u32[]{:S(2)}, u32[]{:S(2)}) collective-permute-start(bf16[256,224]{1,0:T(8,128)(2,1)S(1)} %get-tuple-element.262), channel_id=1, source_target_pairs={{64,40},{65,41},{66,42},{67,43},{68,44},{69,45},{70,46},{71,47},{7... | collective-permute-start | bytes 344072 | tf_op jit(solution)/shard_map/ppermute | solution.py:29
  411.8 15.1 %collective-permute-start.126 = (bf16[256,224]{1,0:T(8,128)(2,1)S(1)}, bf16[256,224]{1,0:T(8,128)(2,1)S(1)}, u32[]{:S(2)}, u32[]{:S(2)}) collective-permute-start(bf16[256,224]{1,0:T(8,128)(2,1)S(1)} %get-tuple-element.262), channel_id=1, source_target_pairs={{64,33},{65,32},{66,35},{67,34},{68,37},{69,36},{70,39},{71,38},{7... | collective-permute-start | bytes 344072 | tf_op jit(solution)/shard_map/ppermute | solution.py:29
  440.4 18.0 %collective-permute-start.141 = (bf16[256,224]{1,0:T(8,128)(2,1)S(1)}, bf16[256,224]{1,0:T(8,128)(2,1)S(1)}, u32[]{:S(2)}, u32[]{:S(2)}) collective-permute-start(bf16[256,224]{1,0:T(8,128)(2,1)S(1)} %get-tuple-element.273), channel_id=1, source_target_pairs={{32,16},{33,17},{34,18},{35,19},{36,20},{37,21},{38,22},{39,23},{4... | collective-permute-start | bytes 344072 | tf_op jit(solution)/shard_map/ppermute | solution.py:29
  483.3 15.4 %collective-permute-start.150 = (bf16[256,224]{1,0:T(8,128)(2,1)S(1)}, bf16[256,224]{1,0:T(8,128)(2,1)S(1)}, u32[]{:S(2)}, u32[]{:S(2)}) collective-permute-start(bf16[256,224]{1,0:T(8,128)(2,1)S(1)} %get-tuple-element.284), channel_id=1, source_target_pairs={{64,34},{65,35},{66,32},{67,33},{68,38},{69,39},{70,36},{71,37},{7... | collective-permute-start | bytes 344072 | tf_op jit(solution)/shard_map/ppermute | solution.py:29
  484.6 14.4 %collective-permute-start.149 = (bf16[256,224]{1,0:T(8,128)(2,1)S(1)}, bf16[256,224]{1,0:T(8,128)(2,1)S(1)}, u32[]{:S(2)}, u32[]{:S(2)}) collective-permute-start(bf16[256,224]{1,0:T(8,128)(2,1)S(1)} %get-tuple-element.284), channel_id=1, source_target_pairs={{64,40},{65,41},{66,42},{67,43},{68,44},{69,45},{70,46},{71,47},{7... | collective-permute-start | bytes 344072 | tf_op jit(solution)/shard_map/ppermute | solution.py:29
  (158 other events, 1388.2 us)

commit v4 on v3

--- a/solution.py
+++ b/solution.py
@@ -29,6 +29,16 @@
     return lax.ppermute(value, AXES, pairs)
 
 
+def turn_back(value, ring, distance):
+    width = lax.axis_size("tensor")
+    pairs = [
+        (s * width + i, s * width + i // ring * ring + (i - distance) % ring)
+        for s in range(lax.axis_size("pipe"))
+        for i in range(width)
+    ]
+    return lax.ppermute(value, AXES, pairs)
+
+
 def column_chunks(width):
     return [(start, min(256, width - start)) for start in range(0, width, 256)]
 
@@ -43,6 +53,36 @@
 
 def dot_tn(a, b):
     return lax.dot_general(a, b, (((0,), (0,)), ((), ())), preferred_element_type=F32)
+
+
+def split_kernel(far, *refs):
+    owned, outs, sems = refs[0], refs[1:-1], refs[-1]
+    half = owned.shape[1] // 2
+    sources = [owned.at[far, pl.ds(0, half)], owned.at[far, pl.ds(half, half)]]
+    sources += [owned.at[k] for k in range(owned.shape[0]) if k != far]
+    copies = [
+        pltpu.make_async_copy(source, out, sems.at[i])
+        for i, (source, out) in enumerate(zip(sources, outs))
+    ]
+    for copy in copies:
+        copy.start()
+    for copy in copies:
+        copy.wait()
+
+
+def join_kernel(far, *refs):
+    ins, out, sems = refs[:-2], refs[-2], refs[-1]
+    half = ins[0].shape[0]
+    places = [out.at[far, pl.ds(0, half)], out.at[far, pl.ds(half, half)]]
+    places += [out.at[k] for k in range(out.shape[0]) if k != far]
+    copies = [
+        pltpu.make_async_copy(source, place, sems.at[i])
+        for i, (source, place) in enumerate(zip(ins, places))
+    ]
+    for copy in copies:
+        copy.start()
+    for copy in copies:
+        copy.wait()
 
 
 def in_order(refs, order):
@@ -53,8 +93,7 @@
 def forward_kernel(n, layer, last, order, rider, tokens, n_state, *refs):
     place, refs = refs[0], refs[1:]
     ins, refs = in_order(refs[:n], order), refs[n:]
-    first, refs = refs[0], refs[1:]
-    second, refs = refs[:n], refs[n:]
+    first, second, refs = refs[0], refs[1], refs[2:]
     riding, refs = (refs[0], refs[1:]) if rider is not None else (None, refs)
     refs = refs[n_state:]
     st_ins, st_pre, st_hid = refs[:3]
@@ -81,9 +120,9 @@
         save_pre = pltpu.make_async_copy(preact, st_pre, sems.at[n])
         save_pre.start()
         if not last:
-            outs[0][...] = ins[0][rows, :].astype(F32) + dot_nt(hidden[...], second[0][...])
+            outs[0][...] = ins[0][rows, :].astype(F32) + dot_nt(hidden[...], second[0])
             for k in range(1, n):
-                outs[k][...] = dot_nt(hidden[...], second[k][...]).astype(BF16)
+                outs[k][...] = dot_nt(hidden[...], second[k]).astype(BF16)
         for c in range(pieces.shape[0]):
             pieces[c] = hidden[:, c * slab : (c + 1) * slab]
         save_hid = pltpu.make_async_copy(pieces, st_hid, sems.at[n + 1])
@@ -126,8 +165,7 @@
 def backward_kernel(n, layer, half, order, tokens, piece, earlier, n_state, *refs):
     place, refs = refs[0], refs[1:]
     ins, refs = in_order(refs[:n], order), refs[n:]
-    first, refs = refs[0], refs[1:]
-    second, refs = refs[:n], refs[n:]
+    first, second, refs = refs[0], refs[1], refs[2:]
     st_pre, st_hid, refs = refs[0], refs[1], refs[2:]
     got, refs = (refs[: n - 1], refs[n - 1 :]) if earlier is not None else (None, refs)
     refs = refs[n_state:]
@@ -144,9 +182,9 @@
         save_grad.start()
         for start, size in column_chunks(preact.shape[1]):
             cols = slice(start, start + size)
-            total = dot_nn(ins[0][rows, :], second[0][:, cols])
+            total = dot_nn(ins[0][rows, :], second[0, :, cols])
             for k in range(1, n):
-                total = total + dot_nn(ins[k][rows, :], second[k][:, cols])
+                total = total + dot_nn(ins[k][rows, :], second[k, :, cols])
             if start == 0:
                 from_pre.wait()
             x = preact[:, cols]
@@ -263,7 +301,29 @@
     x = x_in.reshape(tokens, slab)
     cot = cotangent.reshape(tokens, slab)
     ins = [x] + exchange([x] * n, everyone)
-    second = [owned[0]] + exchange(owned, everyone)
+    far = 3
+    low, high, *rest = pl.pallas_call(
+        functools.partial(split_kernel, far),
+        out_shape=[shape((slab // 2, hid), BF16)] * 2 + [shape((slab, hid), BF16)] * (n - 1),
+        in_specs=[ANY],
+        out_specs=[ANY] * (n + 1),
+        scratch_shapes=[pltpu.SemaphoreType.DMA((n + 1,))],
+        compiler_params=params,
+    )(owned)
+    blocks = dict(zip([k for k in range(n) if k != far], rest))
+    high = turn_back(high, 8, 2)
+    low = send(low, far, everyone)
+    swapped = {k: send(blocks[k], k, everyone) for k in order if k != far}
+    high = turn_back(high, 8, 2)
+    pieces = [low, high, blocks[0]] + [swapped[k] for k in range(1, n) if k != far]
+    (second,) = pl.pallas_call(
+        functools.partial(join_kernel, far),
+        out_shape=[shape((n, slab, hid), BF16)],
+        in_specs=[ANY] * len(pieces),
+        out_specs=[VMEM],
+        scratch_shapes=[pltpu.SemaphoreType.DMA((n + 1,))],
+        compiler_params=params,
+    )(*pieces)
     operands = [k for k in (0, 1, 4, 2, 3, 5) if k < n]
 
     state = []
@@ -280,14 +340,14 @@
         results = pl.pallas_call(
             functools.partial(forward_kernel, n, layer, last, operands, rider, tokens, len(state)),
             out_shape=state_shapes + outs,
-            in_specs=[SMEM] + [VMEM] * (2 * n + 1 + len(riding)) + [ANY] * len(state),
+            in_specs=[SMEM] + [VMEM] * (n + 2 + len(riding)) + [ANY] * len(state),
             out_specs=[ANY] * 3 + [VMEM] * len(outs),
             scratch_shapes=work
             + [pltpu.VMEM((n_pieces, tokens, slab), BF16), pltpu.SemaphoreType.DMA((n + 2,))],
-            input_output_aliases={2 + 2 * n + len(riding) + i: i for i in range(len(state))},
+            input_output_aliases={3 + n + len(riding) + i: i for i in range(len(state))},
             cost_estimate=cost,
             compiler_params=params,
-        )(place, *[ins[k] for k in operands], first, *second, *riding, *state)
+        )(place, *[ins[k] for k in operands], first, second, *riding, *state)
         state, terms = list(results[:3]), results[3:]
         if last:
             break
@@ -326,20 +386,20 @@
             ]
             + term_shapes,
             in_specs=[SMEM]
-            + [VMEM] * (2 * n + 1)
+            + [VMEM] * (n + 2)
             + [ANY] * 2
             + [VMEM] * len(got)
             + [ANY] * len(state),
             out_specs=[ANY] * 3 + [VMEM] * n,
             scratch_shapes=work + [pltpu.SemaphoreType.DMA((2 * n,))],
-            input_output_aliases={4 + 2 * n + len(got) + i: i for i in range(len(state))},
+            input_output_aliases={5 + n + len(got) + i: i for i in range(len(state))},
             cost_estimate=cost,
             compiler_params=params,
         )(
             place,
             *[grads_in[k] for k in operands],
             first,
-            *second,
+            second,
             st_pre,
             st_hid,
             *got,

time: 563 us -> 552 us (0.980)
  starting transfers between devices: 255 us -> 281 us
  Pallas kernels: 44.1 us -> 26 us
  waiting for transfers between devices: 241 us -> 224 us
    ppermute x169, waiting for transfers between devices: 241 us -> 204 us  [send(): return lax.ppermute(value, AXES, pairs)]
    ppermute x169, starting transfers between devices: 255 us -> 276 us  [send(): return lax.ppermute(value, AXES, pairs)]
    ppermute x0 -> x2, waiting for transfers between devices: none -> 20.1 us  [turn_back(): return lax.ppermute(value, AXES, pairs)]
    pallas_call x8, Pallas kernels: 23 us -> 12 us  [body(): pl.pallas_call(functools.partial(backward_kernel, n, layer, half, operand...]
    pallas_call x8, Pallas kernels: 15.5 us -> 5.32 us  [body(): pl.pallas_call(functools.partial(forward_kernel, n, layer, last, operands...]
  transfers between devices with their start and end apart: 169 -> 171, of which waited for: 75 -> 72; matrix products, arithmetic and copies ran while one was open for 1% -> 0% of each run, Pallas kernels for 0% -> 0%
where the time goes in v4:
time: 552 us; the launch traced here: 542 us
  starting transfers between devices  281 us (51%)
  waiting for transfers between devices  224 us (41%)
  Pallas kernels  26 us (5%)
  local copies, waits for them, and re-layouts  8.54 us (2%)
    ppermute x169, starting transfers between devices, send(): return lax.ppermute(value, AXES, pairs)  276 us
    ppermute x169, waiting for transfers between devices, send(): return lax.ppermute(value, AXES, pairs)  204 us
    ppermute x2, waiting for transfers between devices, turn_back(): return lax.ppermute(value, AXES, pairs)  20.1 us
    pallas_call x8, Pallas kernels, body(): pl.pallas_call(functools.partial(backward_kernel, n, layer, half, operand...  12 us
  transfers between devices with their start and end apart: 171, of which 72 were waited for; matrix products, arithmetic and copies ran while one was open for 0% of the time, Pallas kernels for 0%

profile of v4, /device:TPU:5, one launch (start us, length us, event | category | flops | bytes accessed | tf_op | source)
XLA Modules:
  0.0 541.8 jit_solution(943252579269146816)
XLA Ops:
  3.9 7.0 %collective-permute-start.5 = (bf16[112,896]{1,0:T(8,128)(2,1)S(1)}, bf16[112,896]{1,0:T(8,128)(2,1)S(1)}, u32[]{:S(2)}, u32[]{:S(2)}) collective-permute-start(bf16[112,896]{1,0:T(8,128)(2,1)S(1)} %get-tuple-element.165), channel_id=1, source_target_pairs={{0,4},{1,5},{2,6},{3,7},{4,0},{5,1},{6,2},{7,3},{8,12},{9,13},{10,... | collective-permute-start | bytes 602120 | tf_op jit(solution)/shard_map/ppermute | solution.py:29
  18.5 11.1 %collective-permute-done.6 = bf16[112,896]{1,0:T(8,128)(2,1)S(1)} collective-permute-done((bf16[112,896]{1,0:T(8,128)(2,1)S(1)}, bf16[112,896]{1,0:T(8,128)(2,1)S(1)}, u32[]{:S(2)}, u32[]{:S(2)}) %collective-permute-start.6) | collective-permute-done | bytes 200736 | tf_op jit(solution)/shard_map/ppermute | solution.py:39
  29.6 4.3 collective-permute-start.7
  34.0 9.0 %collective-permute-done.7.refs_1_ = bf16[112,896]{1,0:T(8,128)(2,1)S(1)} collective-permute-done((bf16[112,896]{1,0:T(8,128)(2,1)S(1)}, bf16[112,896]{1,0:T(8,128)(2,1)S(1)}, u32[]{:S(2)}, u32[]{:S(2)}) %collective-permute-start.7) | collective-permute-done | bytes 200736 | tf_op jit(solution)/shard_map/ppermute | solution.py:39
  54.3 12.4 %collective-permute-start = (bf16[256,224]{1,0:T(8,128)(2,1)}, bf16[256,224]{1,0:T(8,128)(2,1)}, u32[]{:S(2)}, u32[]{:S(2)}) collective-permute-start(bf16[256,224]{1,0:T(8,128)(2,1)} %bitcast.35), channel_id=1, source_target_pairs={{0,1},{1,0},{2,3},{3,2},{4,5},{5,4},{6,7},{7,6},{8,9},{9,8},{10,11... | collective-permute-start | bytes 344072 | tf_op jit(solution)/shard_map/ppermute | solution.py:29
  79.5 6.4 %collective-permute-done.15.refs_2_.refs_5_ = bf16[256,224]{1,0:T(8,128)(2,1)S(1)} collective-permute-done((bf16[256,224]{1,0:T(8,128)(2,1)S(1)}, bf16[256,224]{1,0:T(8,128)(2,1)S(1)}, u32[]{:S(2)}, u32[]{:S(2)}) %collective-permute-start.15) | collective-permute-done | bytes 114720 | tf_op jit(solution)/shard_map/ppermute | solution.py:29
  97.6 5.0 collective-permute-done.20.refs_4_
  112.3 6.1 %collective-permute-done.25.refs_4_ = bf16[256,224]{1,0:T(8,128)(2,1)S(1)} collective-permute-done((bf16[256,224]{1,0:T(8,128)(2,1)S(1)}, bf16[256,224]{1,0:T(8,128)(2,1)S(1)}, u32[]{:S(2)}, u32[]{:S(2)}) %collective-permute-start.25) | collective-permute-done | bytes 114720 | tf_op jit(solution)/shard_map/ppermute | solution.py:29
  118.5 5.3 collective-permute-start.33
  140.4 5.0 collective-permute-done.34.refs_2_
  145.5 5.4 %collective-permute-done.36.refs_4_ = bf16[256,224]{1,0:T(8,128)(2,1)S(1)} collective-permute-done((bf16[256,224]{1,0:T(8,128)(2,1)S(1)}, bf16[256,224]{1,0:T(8,128)(2,1)S(1)}, u32[]{:S(2)}, u32[]{:S(2)}) %collective-permute-start.36) | collective-permute-done | bytes 114720 | tf_op jit(solution)/shard_map/ppermute | solution.py:29
  167.6 10.0 %collective-permute-start.46 = (bf16[256,224]{1,0:T(8,128)(2,1)S(1)}, bf16[256,224]{1,0:T(8,128)(2,1)S(1)}, u32[]{:S(2)}, u32[]{:S(2)}) collective-permute-start(bf16[256,224]{1,0:T(8,128)(2,1)S(1)} %get-tuple-element.201), channel_id=1, source_target_pairs={{0,16},{1,17},{2,18},{3,19},{4,20},{5,21},{6,22},{7,23},{8,24},{9,... | collective-permute-start | bytes 344072 | tf_op jit(solution)/shard_map/ppermute | solution.py:29
  217.5 10.9 %collective-permute-done.66.refs_6_ = bf16[256,224]{1,0:T(8,128)(2,1)S(1)} collective-permute-done((bf16[256,224]{1,0:T(8,128)(2,1)S(1)}, bf16[256,224]{1,0:T(8,128)(2,1)S(1)}, u32[]{:S(2)}, u32[]{:S(2)}) %collective-permute-start.66) | collective-permute-done | bytes 114720 | tf_op jit(solution)/shard_map/ppermute | solution.py:29
  280.6 6.7 %collective-permute-done.88.refs_6_ = bf16[256,224]{1,0:T(8,128)(2,1)S(1)} collective-permute-done((bf16[256,224]{1,0:T(8,128)(2,1)S(1)}, bf16[256,224]{1,0:T(8,128)(2,1)S(1)}, u32[]{:S(2)}, u32[]{:S(2)}) %collective-permute-start.88) | collective-permute-done | bytes 114720 | tf_op jit(solution)/shard_map/ppermute | solution.py:29
  301.9 5.8 %collective-permute-done.91.refs_4_.refs_12_ = bf16[256,224]{1,0:T(8,128)(2,1)S(1)} collective-permute-done((bf16[256,224]{1,0:T(8,128)(2,1)S(1)}, bf16[256,224]{1,0:T(8,128)(2,1)S(1)}, u32[]{:S(2)}, u32[]{:S(2)}) %collective-permute-start.91) | collective-permute-done | bytes 114720 | tf_op jit(solution)/shard_map/ppermute | solution.py:29
  307.8 4.7 collective-permute-start.99
  329.0 9.4 %collective-permute-done.102.refs_4_.refs_12_ = bf16[256,224]{1,0:T(8,128)(2,1)S(1)} collective-permute-done((bf16[256,224]{1,0:T(8,128)(2,1)S(1)}, bf16[256,224]{1,0:T(8,128)(2,1)S(1)}, u32[]{:S(2)}, u32[]{:S(2)}) %collective-permute-start.102) | collective-permute-done | bytes 114720 | tf_op jit(solution)/shard_map/ppermute | solution.py:29
  348.6 4.3 collective-permute-done.109.refs_5_
  369.0 7.9 %collective-permute-done.113.refs_4_.refs_12_ = bf16[256,224]{1,0:T(8,128)(2,1)S(1)} collective-permute-done((bf16[256,224]{1,0:T(8,128)(2,1)S(1)}, bf16[256,224]{1,0:T(8,128)(2,1)S(1)}, u32[]{:S(2)}, u32[]{:S(2)}) %collective-permute-start.113) | collective-permute-done | bytes 114720 | tf_op jit(solution)/shard_map/ppermute | solution.py:29
  411.1 6.5 %collective-permute-done.131.refs_5_ = bf16[256,224]{1,0:T(8,128)(2,1)S(1)} collective-permute-done((bf16[256,224]{1,0:T(8,128)(2,1)S(1)}, bf16[256,224]{1,0:T(8,128)(2,1)S(1)}, u32[]{:S(2)}, u32[]{:S(2)}) %collective-permute-start.131) | collective-permute-done | bytes 114720 | tf_op jit(solution)/shard_map/ppermute | solution.py:29
  433.3 12.4 %collective-permute-start.143 = (bf16[256,224]{1,0:T(8,128)(2,1)S(1)}, bf16[256,224]{1,0:T(8,128)(2,1)S(1)}, u32[]{:S(2)}, u32[]{:S(2)}) collective-permute-start(bf16[256,224]{1,0:T(8,128)(2,1)S(1)} %get-tuple-element.287), channel_id=1, source_target_pairs={{32,16},{33,17},{34,18},{35,19},{36,20},{37,21},{38,22},{39,23},{4... | collective-permute-start | bytes 344072 | tf_op jit(solution)/shard_map/ppermute | solution.py:29
  463.8 10.0 %collective-permute-done.146.refs_4_.refs_12_ = bf16[256,224]{1,0:T(8,128)(2,1)S(1)} collective-permute-done((bf16[256,224]{1,0:T(8,128)(2,1)S(1)}, bf16[256,224]{1,0:T(8,128)(2,1)S(1)}, u32[]{:S(2)}, u32[]{:S(2)}) %collective-permute-start.146) | collective-permute-done | bytes 114720 | tf_op jit(solution)/shard_map/ppermute | solution.py:29
  499.7 4.5 collective-permute-done.155.refs_2_.refs_13_
  530.3 7.5 %collective-permute-done.168.refs_4_.refs_6_ = bf16[256,224]{1,0:T(8,128)(2,1)S(1)} collective-permute-done((bf16[256,224]{1,0:T(8,128)(2,1)S(1)}, bf16[256,224]{1,0:T(8,128)(2,1)S(1)}, u32[]{:S(2)}, u32[]{:S(2)}) %collective-permute-start.168) | collective-permute-done | bytes 114720 | tf_op jit(solution)/shard_map/ppermute | solution.py:29
  (376 shorter events, 361.5 us)
Async XLA Ops:
  10.9 18.8 %collective-permute-start.6 = (bf16[112,896]{1,0:T(8,128)(2,1)S(1)}, bf16[112,896]{1,0:T(8,128)(2,1)S(1)}, u32[]{:S(2)}, u32[]{:S(2)}) collective-permute-start(bf16[112,896]{1,0:T(8,128)(2,1)S(1)} %get-tuple-element.166), channel_id=1, source_target_pairs={{0,6},{1,7},{2,0},{3,1},{4,2},{5,3},{6,4},{7,5},{8,14},{9,15},{10,... | collective-permute-start | bytes 602120 | tf_op jit(solution)/shard_map/ppermute | solution.py:39
  10.9 39.8 %collective-permute-start.8 = (bf16[224,896]{1,0:T(8,128)(2,1)S(1)}, bf16[224,896]{1,0:T(8,128)(2,1)S(1)}, u32[]{:S(2)}, u32[]{:S(2)}) collective-permute-start(bf16[224,896]{1,0:T(8,128)(2,1)S(1)} %get-tuple-element.168), channel_id=1, source_target_pairs={{0,1},{1,0},{2,3},{3,2},{4,5},{5,4},{6,7},{7,6},{8,9},{9,8},{10,11... | collective-permute-start | bytes 1204232 | tf_op jit(solution)/shard_map/ppermute | solution.py:29
  11.9 38.9 %collective-permute-start.9 = (bf16[224,896]{1,0:T(8,128)(2,1)S(1)}, bf16[224,896]{1,0:T(8,128)(2,1)S(1)}, u32[]{:S(2)}, u32[]{:S(2)}) collective-permute-start(bf16[224,896]{1,0:T(8,128)(2,1)S(1)} %get-tuple-element.169), channel_id=1, source_target_pairs={{0,2},{1,3},{2,0},{3,1},{4,6},{5,7},{6,4},{7,5},{8,10},{9,11},{10,... | collective-permute-start | bytes 1204232 | tf_op jit(solution)/shard_map/ppermute | solution.py:29
  14.0 37.5 %collective-permute-start.10 = (bf16[224,896]{1,0:T(8,128)(2,1)S(1)}, bf16[224,896]{1,0:T(8,128)(2,1)S(1)}, u32[]{:S(2)}, u32[]{:S(2)}) collective-permute-start(bf16[224,896]{1,0:T(8,128)(2,1)S(1)} %get-tuple-element.170), channel_id=1, source_target_pairs={{0,8},{1,9},{2,10},{3,11},{4,12},{5,13},{6,14},{7,15},{8,0},{9,1},... | collective-permute-start | bytes 1204232 | tf_op jit(solution)/shard_map/ppermute | solution.py:29
  15.6 38.0 %collective-permute-start.11 = (bf16[224,896]{1,0:T(8,128)(2,1)S(1)}, bf16[224,896]{1,0:T(8,128)(2,1)S(1)}, u32[]{:S(2)}, u32[]{:S(2)}) collective-permute-start(bf16[224,896]{1,0:T(8,128)(2,1)S(1)} %get-tuple-element.171), channel_id=1, source_target_pairs={{0,16},{1,17},{2,18},{3,19},{4,20},{5,21},{6,22},{7,23},{8,24},{9,... | collective-permute-start | bytes 1204232 | tf_op jit(solution)/shard_map/ppermute | solution.py:29
  43.6 28.6 %collective-permute-start.4 = (bf16[256,224]{1,0:T(8,128)(2,1)}, bf16[256,224]{1,0:T(8,128)(2,1)}, u32[]{:S(2)}, u32[]{:S(2)}) collective-permute-start(bf16[256,224]{1,0:T(8,128)(2,1)} %bitcast.31), channel_id=1, source_target_pairs={{0,16},{1,17},{2,18},{3,19},{4,20},{5,21},{6,22},{7,23},{8,24},{9,... | collective-permute-start | bytes 344072 | tf_op jit(solution)/shard_map/ppermute | solution.py:29
  50.6 21.6 %collective-permute-start.3 = (bf16[256,224]{1,0:T(8,128)(2,1)}, bf16[256,224]{1,0:T(8,128)(2,1)}, u32[]{:S(2)}, u32[]{:S(2)}) collective-permute-start(bf16[256,224]{1,0:T(8,128)(2,1)} %bitcast.32), channel_id=1, source_target_pairs={{0,4},{1,5},{2,6},{3,7},{4,0},{5,1},{6,2},{7,3},{8,12},{9,13},{10,... | collective-permute-start | bytes 344072 | tf_op jit(solution)/shard_map/ppermute | solution.py:29
  51.5 20.8 %collective-permute-start.2 = (bf16[256,224]{1,0:T(8,128)(2,1)}, bf16[256,224]{1,0:T(8,128)(2,1)}, u32[]{:S(2)}, u32[]{:S(2)}) collective-permute-start(bf16[256,224]{1,0:T(8,128)(2,1)} %bitcast.33), channel_id=1, source_target_pairs={{0,2},{1,3},{2,0},{3,1},{4,6},{5,7},{6,4},{7,5},{8,10},{9,11},{10,... | collective-permute-start | bytes 344072 | tf_op jit(solution)/shard_map/ppermute | solution.py:29
  52.3 20.0 %collective-permute-start.1 = (bf16[256,224]{1,0:T(8,128)(2,1)}, bf16[256,224]{1,0:T(8,128)(2,1)}, u32[]{:S(2)}, u32[]{:S(2)}) collective-permute-start(bf16[256,224]{1,0:T(8,128)(2,1)} %bitcast.34), channel_id=1, source_target_pairs={{0,8},{1,9},{2,10},{3,11},{4,12},{5,13},{6,14},{7,15},{8,0},{9,1},... | collective-permute-start | bytes 344072 | tf_op jit(solution)/shard_map/ppermute | solution.py:29
  54.3 18.0 %collective-permute-start = (bf16[256,224]{1,0:T(8,128)(2,1)}, bf16[256,224]{1,0:T(8,128)(2,1)}, u32[]{:S(2)}, u32[]{:S(2)}) collective-permute-start(bf16[256,224]{1,0:T(8,128)(2,1)} %bitcast.35), channel_id=1, source_target_pairs={{0,1},{1,0},{2,3},{3,2},{4,5},{5,4},{6,7},{7,6},{8,9},{9,8},{10,11... | collective-permute-start | bytes 344072 | tf_op jit(solution)/shard_map/ppermute | solution.py:29
  164.9 15.5 %collective-permute-start.45 = (bf16[256,224]{1,0:T(8,128)(2,1)S(1)}, bf16[256,224]{1,0:T(8,128)(2,1)S(1)}, u32[]{:S(2)}, u32[]{:S(2)}) collective-permute-start(bf16[256,224]{1,0:T(8,128)(2,1)S(1)} %get-tuple-element.200), channel_id=1, source_target_pairs={{0,4},{1,5},{2,6},{3,7},{4,0},{5,1},{6,2},{7,3},{8,12},{9,13},{10,... | collective-permute-start | bytes 344072 | tf_op jit(solution)/shard_map/ppermute | solution.py:29
  167.6 15.0 %collective-permute-start.46 = (bf16[256,224]{1,0:T(8,128)(2,1)S(1)}, bf16[256,224]{1,0:T(8,128)(2,1)S(1)}, u32[]{:S(2)}, u32[]{:S(2)}) collective-permute-start(bf16[256,224]{1,0:T(8,128)(2,1)S(1)} %get-tuple-element.201), channel_id=1, source_target_pairs={{0,16},{1,17},{2,18},{3,19},{4,20},{5,21},{6,22},{7,23},{8,24},{9,... | collective-permute-start | bytes 344072 | tf_op jit(solution)/shard_map/ppermute | solution.py:29
  211.0 17.4 %collective-permute-start.66 = (bf16[256,224]{1,0:T(8,128)(2,1)S(1)}, bf16[256,224]{1,0:T(8,128)(2,1)S(1)}, u32[]{:S(2)}, u32[]{:S(2)}) collective-permute-start(bf16[256,224]{1,0:T(8,128)(2,1)S(1)} %shard_map.78), channel_id=1, source_target_pairs={{0,48},{1,49},{2,50},{3,51},{4,52},{5,53},{6,54},{7,55},{8,56},{9,... | collective-permute-start | bytes 344072 | tf_op jit(solution)/shard_map/ppermute | solution.py:29
  212.3 19.3 %collective-permute-start.65 = (bf16[256,224]{1,0:T(8,128)(2,1)S(1)}, bf16[256,224]{1,0:T(8,128)(2,1)S(1)}, u32[]{:S(2)}, u32[]{:S(2)}) collective-permute-start(bf16[256,224]{1,0:T(8,128)(2,1)S(1)} %shard_map.78), channel_id=1, source_target_pairs={{0,36},{1,37},{2,38},{3,39},{4,32},{5,33},{6,34},{7,35},{8,44},{9,... | collective-permute-start | bytes 344072 | tf_op jit(solution)/shard_map/ppermute | solution.py:29
  213.6 19.5 %collective-permute-start.64 = (bf16[256,224]{1,0:T(8,128)(2,1)S(1)}, bf16[256,224]{1,0:T(8,128)(2,1)S(1)}, u32[]{:S(2)}, u32[]{:S(2)}) collective-permute-start(bf16[256,224]{1,0:T(8,128)(2,1)S(1)} %shard_map.78), channel_id=1, source_target_pairs={{0,34},{1,35},{2,32},{3,33},{4,38},{5,39},{6,36},{7,37},{8,42},{9,... | collective-permute-start | bytes 344072 | tf_op jit(solution)/shard_map/ppermute | solution.py:29
  214.9 18.2 %collective-permute-start.63 = (bf16[256,224]{1,0:T(8,128)(2,1)S(1)}, bf16[256,224]{1,0:T(8,128)(2,1)S(1)}, u32[]{:S(2)}, u32[]{:S(2)}) collective-permute-start(bf16[256,224]{1,0:T(8,128)(2,1)S(1)} %shard_map.78), channel_id=1, source_target_pairs={{0,40},{1,41},{2,42},{3,43},{4,44},{5,45},{6,46},{7,47},{8,32},{9,... | collective-permute-start | bytes 344072 | tf_op jit(solution)/shard_map/ppermute | solution.py:29
  216.2 16.9 %collective-permute-start.62 = (bf16[256,224]{1,0:T(8,128)(2,1)S(1)}, bf16[256,224]{1,0:T(8,128)(2,1)S(1)}, u32[]{:S(2)}, u32[]{:S(2)}) collective-permute-start(bf16[256,224]{1,0:T(8,128)(2,1)S(1)} %shard_map.78), channel_id=1, source_target_pairs={{0,33},{1,32},{2,35},{3,34},{4,37},{5,36},{6,39},{7,38},{8,41},{9,... | collective-permute-start | bytes 344072 | tf_op jit(solution)/shard_map/ppermute | solution.py:29
  275.4 15.0 %collective-permute-start.87 = (bf16[256,224]{1,0:T(8,128)(2,1)S(1)}, bf16[256,224]{1,0:T(8,128)(2,1)S(1)}, u32[]{:S(2)}, u32[]{:S(2)}) collective-permute-start(bf16[256,224]{1,0:T(8,128)(2,1)S(1)} %shard_map.82), channel_id=1, source_target_pairs={{0,36},{1,37},{2,38},{3,39},{4,32},{5,33},{6,34},{7,35},{8,44},{9,... | collective-permute-start | bytes 344072 | tf_op jit(solution)/shard_map/ppermute | solution.py:29
  276.7 15.2 %collective-permute-start.86 = (bf16[256,224]{1,0:T(8,128)(2,1)S(1)}, bf16[256,224]{1,0:T(8,128)(2,1)S(1)}, u32[]{:S(2)}, u32[]{:S(2)}) collective-permute-start(bf16[256,224]{1,0:T(8,128)(2,1)S(1)} %shard_map.82), channel_id=1, source_target_pairs={{0,34},{1,35},{2,32},{3,33},{4,38},{5,39},{6,36},{7,37},{8,42},{9,... | collective-permute-start | bytes 344072 | tf_op jit(solution)/shard_map/ppermute | solution.py:29
  341.2 14.1 %collective-permute-start.108 = (bf16[256,224]{1,0:T(8,128)(2,1)S(1)}, bf16[256,224]{1,0:T(8,128)(2,1)S(1)}, u32[]{:S(2)}, u32[]{:S(2)}) collective-permute-start(bf16[256,224]{1,0:T(8,128)(2,1)S(1)} %get-tuple-element.254), channel_id=1, source_target_pairs={{64,34},{65,35},{66,32},{67,33},{68,38},{69,39},{70,36},{71,37},{7... | collective-permute-start | bytes 344072 | tf_op jit(solution)/shard_map/ppermute | solution.py:29
  402.4 15.2 %collective-permute-start.131 = (bf16[256,224]{1,0:T(8,128)(2,1)S(1)}, bf16[256,224]{1,0:T(8,128)(2,1)S(1)}, u32[]{:S(2)}, u32[]{:S(2)}) collective-permute-start(bf16[256,224]{1,0:T(8,128)(2,1)S(1)} %get-tuple-element.276), channel_id=1, source_target_pairs={{64,36},{65,37},{66,38},{67,39},{68,32},{69,33},{70,34},{71,35},{7... | collective-permute-start | bytes 344072 | tf_op jit(solution)/shard_map/ppermute | solution.py:29
  403.7 15.9 %collective-permute-start.130 = (bf16[256,224]{1,0:T(8,128)(2,1)S(1)}, bf16[256,224]{1,0:T(8,128)(2,1)S(1)}, u32[]{:S(2)}, u32[]{:S(2)}) collective-permute-start(bf16[256,224]{1,0:T(8,128)(2,1)S(1)} %get-tuple-element.276), channel_id=1, source_target_pairs={{64,34},{65,35},{66,32},{67,33},{68,38},{69,39},{70,36},{71,37},{7... | collective-permute-start | bytes 344072 | tf_op jit(solution)/shard_map/ppermute | solution.py:29
  405.0 14.6 %collective-permute-start.129 = (bf16[256,224]{1,0:T(8,128)(2,1)S(1)}, bf16[256,224]{1,0:T(8,128)(2,1)S(1)}, u32[]{:S(2)}, u32[]{:S(2)}) collective-permute-start(bf16[256,224]{1,0:T(8,128)(2,1)S(1)} %get-tuple-element.276), channel_id=1, source_target_pairs={{64,40},{65,41},{66,42},{67,43},{68,44},{69,45},{70,46},{71,47},{7... | collective-permute-start | bytes 344072 | tf_op jit(solution)/shard_map/ppermute | solution.py:29
  433.3 17.7 %collective-permute-start.143 = (bf16[256,224]{1,0:T(8,128)(2,1)S(1)}, bf16[256,224]{1,0:T(8,128)(2,1)S(1)}, u32[]{:S(2)}, u32[]{:S(2)}) collective-permute-start(bf16[256,224]{1,0:T(8,128)(2,1)S(1)} %get-tuple-element.287), channel_id=1, source_target_pairs={{32,16},{33,17},{34,18},{35,19},{36,20},{37,21},{38,22},{39,23},{4... | collective-permute-start | bytes 344072 | tf_op jit(solution)/shard_map/ppermute | solution.py:29
  (159 other events, 1362.5 us)

commit v5 on v4

--- a/solution.py
+++ b/solution.py
@@ -271,7 +271,7 @@
     term_shapes = [shape((tokens, slab), F32)] + [shape((tokens, slab), BF16)] * (n - 1)
 
     everyone = [(s, s) for s in range(sections)]
-    order = [k for k in (3, 5, 2, 4, 1) if k < n]
+    order = [k for k in (2, 3, 5, 4, 1) if k < n]
 
     def exchange(values, routes):
         got = {k: send(values[k], k, routes) for k in order}
@@ -301,6 +301,7 @@
     x = x_in.reshape(tokens, slab)
     cot = cotangent.reshape(tokens, slab)
     ins = [x] + exchange([x] * n, everyone)
+    owned, *ins = lax.optimization_barrier((owned, *ins))
     far = 3
     low, high, *rest = pl.pallas_call(
         functools.partial(split_kernel, far),
@@ -324,7 +325,7 @@
         scratch_shapes=[pltpu.SemaphoreType.DMA((n + 1,))],
         compiler_params=params,
     )(*pieces)
-    operands = [k for k in (0, 1, 4, 2, 3, 5) if k < n]
+    operands = [k for k in (0, 1, 4, 5, 3, 2) if k < n]
 
     state = []
     for layer in range(sections):

time: 552 us -> 558 us (1.011)
  waiting for transfers between devices: 224 us -> 241 us
  starting transfers between devices: 281 us -> 274 us
    ppermute x169, waiting for transfers between devices: 204 us -> 221 us  [send(): return lax.ppermute(value, AXES, pairs)]
  transfers between devices with their start and end apart: 171 -> 171, of which waited for: 72 -> 83; matrix products, arithmetic and copies ran while one was open for 0% -> 0% of each run, Pallas kernels for 0% -> 0%
where the time goes in v5:
time: 558 us; the launch traced here: 547 us
  starting transfers between devices  274 us (49%)
  waiting for transfers between devices  241 us (43%)
  Pallas kernels  25.5 us (5%)
    ppermute x169, starting transfers between devices, send(): return lax.ppermute(value, AXES, pairs)  271 us
    ppermute x169, waiting for transfers between devices, send(): return lax.ppermute(value, AXES, pairs)  221 us
    ppermute x2, waiting for transfers between devices, turn_back(): return lax.ppermute(value, AXES, pairs)  20.2 us
    pallas_call x8, Pallas kernels, body(): pl.pallas_call(functools.partial(backward_kernel, n, layer, half, operand...  12 us
  transfers between devices with their start and end apart: 171, of which 83 were waited for; matrix products, arithmetic and copies ran while one was open for 0% of the time, Pallas kernels for 0%

profile of v5, /device:TPU:5, one launch (start us, length us, event | category | flops | bytes accessed | tf_op | source)
XLA Modules:
  0.0 547.3 jit_solution(5253019032317719068)
XLA Ops:
  4.0 6.9 %collective-permute-start.2 = (bf16[256,224]{1,0:T(8,128)(2,1)}, bf16[256,224]{1,0:T(8,128)(2,1)S(1)}, u32[]{:S(2)}, u32[]{:S(2)}) collective-permute-start(bf16[256,224]{1,0:T(8,128)(2,1)} %bitcast.33), channel_id=1, source_target_pairs={{0,4},{1,5},{2,6},{3,7},{4,0},{5,1},{6,2},{7,3},{8,12},{9,13},{10,... | collective-permute-start | bytes 344072 | tf_op jit(solution)/shard_map/ppermute | solution.py:29
  14.8 9.2 %collective-permute-done.1.refs_6_ = bf16[256,224]{1,0:T(8,128)(2,1)S(1)} collective-permute-done((bf16[256,224]{1,0:T(8,128)(2,1)}, bf16[256,224]{1,0:T(8,128)(2,1)S(1)}, u32[]{:S(2)}, u32[]{:S(2)}) %collective-permute-start.1) | collective-permute-done | bytes 114720 | tf_op jit(solution)/shard_map/ppermute | solution.py:29
  35.7 5.5 %collective-permute-done.5.refs_0_ = bf16[112,896]{1,0:T(8,128)(2,1)S(1)} collective-permute-done((bf16[112,896]{1,0:T(8,128)(2,1)S(1)}, bf16[112,896]{1,0:T(8,128)(2,1)S(1)}, u32[]{:S(2)}, u32[]{:S(2)}) %collective-permute-start.5) | collective-permute-done | bytes 200736 | tf_op jit(solution)/shard_map/ppermute | solution.py:29
  42.8 7.6 %collective-permute-done.6 = bf16[112,896]{1,0:T(8,128)(2,1)} collective-permute-done((bf16[112,896]{1,0:T(8,128)(2,1)S(1)}, bf16[112,896]{1,0:T(8,128)(2,1)}, u32[]{:S(2)}, u32[]{:S(2)}) %collective-permute-start.6) | collective-permute-done | bytes 200736 | tf_op jit(solution)/shard_map/ppermute | solution.py:39
  51.5 12.6 %collective-permute-done.7.refs_1_ = bf16[112,896]{1,0:T(8,128)(2,1)} collective-permute-done((bf16[112,896]{1,0:T(8,128)(2,1)}, bf16[112,896]{1,0:T(8,128)(2,1)}, u32[]{:S(2)}, u32[]{:S(2)}) %collective-permute-start.7) | collective-permute-done | bytes 200736 | tf_op jit(solution)/shard_map/ppermute | solution.py:39
  70.8 7.1 %collective-permute-start.12 = (bf16[256,224]{1,0:T(8,128)(2,1)S(1)}, bf16[256,224]{1,0:T(8,128)(2,1)S(1)}, u32[]{:S(2)}, u32[]{:S(2)}) collective-permute-start(bf16[256,224]{1,0:T(8,128)(2,1)S(1)} %get-tuple-element.186), channel_id=1, source_target_pairs={{0,1},{1,0},{2,3},{3,2},{4,5},{5,4},{6,7},{7,6},{8,9},{9,8},{10,11... | collective-permute-start | bytes 344072 | tf_op jit(solution)/shard_map/ppermute | solution.py:29
  88.0 7.1 %collective-permute-done.16.refs_2_.refs_6_ = bf16[256,224]{1,0:T(8,128)(2,1)S(1)} collective-permute-done((bf16[256,224]{1,0:T(8,128)(2,1)S(1)}, bf16[256,224]{1,0:T(8,128)(2,1)S(1)}, u32[]{:S(2)}, u32[]{:S(2)}) %collective-permute-start.16) | collective-permute-done | bytes 114720 | tf_op jit(solution)/shard_map/ppermute | solution.py:29
  116.0 7.3 %collective-permute-done.23.refs_2_ = bf16[256,224]{1,0:T(8,128)(2,1)S(1)} collective-permute-done((bf16[256,224]{1,0:T(8,128)(2,1)S(1)}, bf16[256,224]{1,0:T(8,128)(2,1)S(1)}, u32[]{:S(2)}, u32[]{:S(2)}) %collective-permute-start.23) | collective-permute-done | bytes 114720 | tf_op jit(solution)/shard_map/ppermute | solution.py:29
  148.6 6.0 %collective-permute-done.34.refs_2_ = bf16[256,224]{1,0:T(8,128)(2,1)S(1)} collective-permute-done((bf16[256,224]{1,0:T(8,128)(2,1)S(1)}, bf16[256,224]{1,0:T(8,128)(2,1)S(1)}, u32[]{:S(2)}, u32[]{:S(2)}) %collective-permute-start.34) | collective-permute-done | bytes 114720 | tf_op jit(solution)/shard_map/ppermute | solution.py:29
  177.8 5.0 collective-permute-done.45.refs_2_
  217.4 14.3 %collective-permute-done.66.refs_6_ = bf16[256,224]{1,0:T(8,128)(2,1)S(1)} collective-permute-done((bf16[256,224]{1,0:T(8,128)(2,1)S(1)}, bf16[256,224]{1,0:T(8,128)(2,1)S(1)}, u32[]{:S(2)}, u32[]{:S(2)}) %collective-permute-start.66) | collective-permute-done | bytes 114720 | tf_op jit(solution)/shard_map/ppermute | solution.py:29
  258.0 6.9 %collective-permute-start.72 = (bf16[256,224]{1,0:T(8,128)(2,1)S(1)}, bf16[256,224]{1,0:T(8,128)(2,1)S(1)}, u32[]{:S(2)}, u32[]{:S(2)}) collective-permute-start(bf16[256,224]{1,0:T(8,128)(2,1)S(1)} %shard_map.80), channel_id=1, source_target_pairs={{32,64},{33,65},{34,66},{35,67},{36,68},{37,69},{38,70},{39,71},{4... | collective-permute-start | bytes 344072 | tf_op jit(solution)/shard_map/ppermute | solution.py:29
  285.1 6.2 %collective-permute-done.88.refs_6_ = bf16[256,224]{1,0:T(8,128)(2,1)S(1)} collective-permute-done((bf16[256,224]{1,0:T(8,128)(2,1)S(1)}, bf16[256,224]{1,0:T(8,128)(2,1)S(1)}, u32[]{:S(2)}, u32[]{:S(2)}) %collective-permute-start.88) | collective-permute-done | bytes 114720 | tf_op jit(solution)/shard_map/ppermute | solution.py:29
  332.8 6.2 %collective-permute-done.100.refs_2_.refs_12_ = bf16[256,224]{1,0:T(8,128)(2,1)S(1)} collective-permute-done((bf16[256,224]{1,0:T(8,128)(2,1)S(1)}, bf16[256,224]{1,0:T(8,128)(2,1)S(1)}, u32[]{:S(2)}, u32[]{:S(2)}) %collective-permute-start.100) | collective-permute-done | bytes 114720 | tf_op jit(solution)/shard_map/ppermute | solution.py:29
  346.9 12.3 %collective-permute-done.110.refs_6_ = bf16[256,224]{1,0:T(8,128)(2,1)S(1)} collective-permute-done((bf16[256,224]{1,0:T(8,128)(2,1)S(1)}, bf16[256,224]{1,0:T(8,128)(2,1)S(1)}, u32[]{:S(2)}, u32[]{:S(2)}) %collective-permute-start.110) | collective-permute-done | bytes 114720 | tf_op jit(solution)/shard_map/ppermute | solution.py:29
  360.6 4.9 collective-permute-done.105.refs_1_
  379.8 5.1 collective-permute-done.115.refs_6_.refs_11_
  416.7 7.4 %collective-permute-done.132.refs_6_ = bf16[256,224]{1,0:T(8,128)(2,1)S(1)} collective-permute-done((bf16[256,224]{1,0:T(8,128)(2,1)S(1)}, bf16[256,224]{1,0:T(8,128)(2,1)S(1)}, u32[]{:S(2)}, u32[]{:S(2)}) %collective-permute-start.132) | collective-permute-done | bytes 114720 | tf_op jit(solution)/shard_map/ppermute | solution.py:29
  438.5 5.5 %collective-permute-done.133.refs_2_.refs_12_ = bf16[256,224]{1,0:T(8,128)(2,1)S(1)} collective-permute-done((bf16[256,224]{1,0:T(8,128)(2,1)S(1)}, bf16[256,224]{1,0:T(8,128)(2,1)S(1)}, u32[]{:S(2)}, u32[]{:S(2)}) %collective-permute-start.133) | collective-permute-done | bytes 114720 | tf_op jit(solution)/shard_map/ppermute | solution.py:29
  445.5 5.1 collective-permute-start.143
  470.4 6.2 %collective-permute-done.144.refs_2_.refs_12_ = bf16[256,224]{1,0:T(8,128)(2,1)S(1)} collective-permute-done((bf16[256,224]{1,0:T(8,128)(2,1)S(1)}, bf16[256,224]{1,0:T(8,128)(2,1)S(1)}, u32[]{:S(2)}, u32[]{:S(2)}) %collective-permute-start.144) | collective-permute-done | bytes 114720 | tf_op jit(solution)/shard_map/ppermute | solution.py:29
  484.6 7.6 %collective-permute-done.154.refs_6_ = bf16[256,224]{1,0:T(8,128)(2,1)S(1)} collective-permute-done((bf16[256,224]{1,0:T(8,128)(2,1)S(1)}, bf16[256,224]{1,0:T(8,128)(2,1)S(1)}, u32[]{:S(2)}, u32[]{:S(2)}) %collective-permute-start.154) | collective-permute-done | bytes 114720 | tf_op jit(solution)/shard_map/ppermute | solution.py:29
  519.1 5.6 %collective-permute-start.160 = (bf16[256,224]{1,0:T(8,128)(2,1)S(1)}, bf16[256,224]{1,0:T(8,128)(2,1)S(1)}, u32[]{:S(2)}, u32[]{:S(2)}) collective-permute-start(bf16[256,224]{1,0:T(8,128)(2,1)S(1)} %get-tuple-element.323), channel_id=1, source_target_pairs={{32,0},{33,1},{34,2},{35,3},{36,4},{37,5},{38,6},{39,7},{40,8},{41... | collective-permute-start | bytes 344072 | tf_op jit(solution)/shard_map/ppermute | solution.py:29
  533.0 6.3 %collective-permute-done.166.refs_2_.refs_6_ = bf16[256,224]{1,0:T(8,128)(2,1)S(1)} collective-permute-done((bf16[256,224]{1,0:T(8,128)(2,1)S(1)}, bf16[256,224]{1,0:T(8,128)(2,1)S(1)}, u32[]{:S(2)}, u32[]{:S(2)}) %collective-permute-start.166) | collective-permute-done | bytes 114720 | tf_op jit(solution)/shard_map/ppermute | solution.py:29
  (380 shorter events, 370.8 us)
Async XLA Ops:
  30.4 19.9 %collective-permute-start.6 = (bf16[112,896]{1,0:T(8,128)(2,1)S(1)}, bf16[112,896]{1,0:T(8,128)(2,1)}, u32[]{:S(2)}, u32[]{:S(2)}) collective-permute-start(bf16[112,896]{1,0:T(8,128)(2,1)S(1)} %get-tuple-element.180), channel_id=1, source_target_pairs={{0,6},{1,7},{2,0},{3,1},{4,2},{5,3},{6,4},{7,5},{8,14},{9,15},{10,... | collective-permute-start | bytes 602120 | tf_op jit(solution)/shard_map/ppermute | solution.py:39
  31.7 36.9 %collective-permute-start.8 = (bf16[224,896]{1,0:T(8,128)(2,1)}, bf16[224,896]{1,0:T(8,128)(2,1)S(1)}, u32[]{:S(2)}, u32[]{:S(2)}) collective-permute-start(bf16[224,896]{1,0:T(8,128)(2,1)} %get-tuple-element.182), channel_id=1, source_target_pairs={{0,1},{1,0},{2,3},{3,2},{4,5},{5,4},{6,7},{7,6},{8,9},{9,8},{10,11... | collective-permute-start | bytes 1204232 | tf_op jit(solution)/shard_map/ppermute | solution.py:29
  34.6 33.9 %collective-permute-start.9 = (bf16[224,896]{1,0:T(8,128)(2,1)}, bf16[224,896]{1,0:T(8,128)(2,1)}, u32[]{:S(2)}, u32[]{:S(2)}) collective-permute-start(bf16[224,896]{1,0:T(8,128)(2,1)} %get-tuple-element.183), channel_id=1, source_target_pairs={{0,2},{1,3},{2,0},{3,1},{4,6},{5,7},{6,4},{7,5},{8,10},{9,11},{10,... | collective-permute-start | bytes 1204232 | tf_op jit(solution)/shard_map/ppermute | solution.py:29
  34.6 33.9 %collective-permute-start.10 = (bf16[224,896]{1,0:T(8,128)(2,1)}, bf16[224,896]{1,0:T(8,128)(2,1)}, u32[]{:S(2)}, u32[]{:S(2)}) collective-permute-start(bf16[224,896]{1,0:T(8,128)(2,1)} %get-tuple-element.184), channel_id=1, source_target_pairs={{0,8},{1,9},{2,10},{3,11},{4,12},{5,13},{6,14},{7,15},{8,0},{9,1},... | collective-permute-start | bytes 1204232 | tf_op jit(solution)/shard_map/ppermute | solution.py:29
  41.2 27.4 %collective-permute-start.11 = (bf16[224,896]{1,0:T(8,128)(2,1)}, bf16[224,896]{1,0:T(8,128)(2,1)}, u32[]{:S(2)}, u32[]{:S(2)}) collective-permute-start(bf16[224,896]{1,0:T(8,128)(2,1)} %get-tuple-element.185), channel_id=1, source_target_pairs={{0,16},{1,17},{2,18},{3,19},{4,20},{5,21},{6,22},{7,23},{8,24},{9,... | collective-permute-start | bytes 1204232 | tf_op jit(solution)/shard_map/ppermute | solution.py:29
  50.4 13.8 %collective-permute-start.7 = (bf16[112,896]{1,0:T(8,128)(2,1)}, bf16[112,896]{1,0:T(8,128)(2,1)}, u32[]{:S(2)}, u32[]{:S(2)}) collective-permute-start(bf16[112,896]{1,0:T(8,128)(2,1)} %collective-permute-done.6), channel_id=1, source_target_pairs={{0,6},{1,7},{2,0},{3,1},{4,2},{5,3},{6,4},{7,5},{8,14},{9,15},{10,... | collective-permute-start | bytes 602120 | tf_op jit(solution)/shard_map/ppermute | solution.py:39
  108.8 14.5 %collective-permute-start.23 = (bf16[256,224]{1,0:T(8,128)(2,1)S(1)}, bf16[256,224]{1,0:T(8,128)(2,1)S(1)}, u32[]{:S(2)}, u32[]{:S(2)}) collective-permute-start(bf16[256,224]{1,0:T(8,128)(2,1)S(1)} %get-tuple-element.196), channel_id=1, source_target_pairs={{0,2},{1,3},{2,0},{3,1},{4,6},{5,7},{6,4},{7,5},{8,10},{9,11},{10,... | collective-permute-start | bytes 344072 | tf_op jit(solution)/shard_map/ppermute | solution.py:29
  210.9 20.8 %collective-permute-start.66 = (bf16[256,224]{1,0:T(8,128)(2,1)S(1)}, bf16[256,224]{1,0:T(8,128)(2,1)S(1)}, u32[]{:S(2)}, u32[]{:S(2)}) collective-permute-start(bf16[256,224]{1,0:T(8,128)(2,1)S(1)} %shard_map.78), channel_id=1, source_target_pairs={{0,34},{1,35},{2,32},{3,33},{4,38},{5,39},{6,36},{7,37},{8,42},{9,... | collective-permute-start | bytes 344072 | tf_op jit(solution)/shard_map/ppermute | solution.py:29
  212.2 20.8 %collective-permute-start.65 = (bf16[256,224]{1,0:T(8,128)(2,1)S(1)}, bf16[256,224]{1,0:T(8,128)(2,1)S(1)}, u32[]{:S(2)}, u32[]{:S(2)}) collective-permute-start(bf16[256,224]{1,0:T(8,128)(2,1)S(1)} %shard_map.78), channel_id=1, source_target_pairs={{0,36},{1,37},{2,38},{3,39},{4,32},{5,33},{6,34},{7,35},{8,44},{9,... | collective-permute-start | bytes 344072 | tf_op jit(solution)/shard_map/ppermute | solution.py:29
  213.6 19.7 %collective-permute-start.64 = (bf16[256,224]{1,0:T(8,128)(2,1)S(1)}, bf16[256,224]{1,0:T(8,128)(2,1)S(1)}, u32[]{:S(2)}, u32[]{:S(2)}) collective-permute-start(bf16[256,224]{1,0:T(8,128)(2,1)S(1)} %shard_map.78), channel_id=1, source_target_pairs={{0,48},{1,49},{2,50},{3,51},{4,52},{5,53},{6,54},{7,55},{8,56},{9,... | collective-permute-start | bytes 344072 | tf_op jit(solution)/shard_map/ppermute | solution.py:29
  214.8 18.4 %collective-permute-start.63 = (bf16[256,224]{1,0:T(8,128)(2,1)S(1)}, bf16[256,224]{1,0:T(8,128)(2,1)S(1)}, u32[]{:S(2)}, u32[]{:S(2)}) collective-permute-start(bf16[256,224]{1,0:T(8,128)(2,1)S(1)} %shard_map.78), channel_id=1, source_target_pairs={{0,40},{1,41},{2,42},{3,43},{4,44},{5,45},{6,46},{7,47},{8,32},{9,... | collective-permute-start | bytes 344072 | tf_op jit(solution)/shard_map/ppermute | solution.py:29
  216.2 18.3 %collective-permute-start.62 = (bf16[256,224]{1,0:T(8,128)(2,1)S(1)}, bf16[256,224]{1,0:T(8,128)(2,1)S(1)}, u32[]{:S(2)}, u32[]{:S(2)}) collective-permute-start(bf16[256,224]{1,0:T(8,128)(2,1)S(1)} %shard_map.78), channel_id=1, source_target_pairs={{0,33},{1,32},{2,35},{3,34},{4,37},{5,36},{6,39},{7,38},{8,41},{9,... | collective-permute-start | bytes 344072 | tf_op jit(solution)/shard_map/ppermute | solution.py:29
  324.9 14.1 %collective-permute-start.100 = (bf16[256,224]{1,0:T(8,128)(2,1)S(1)}, bf16[256,224]{1,0:T(8,128)(2,1)S(1)}, u32[]{:S(2)}, u32[]{:S(2)}) collective-permute-start(bf16[256,224]{1,0:T(8,128)(2,1)S(1)} %get-tuple-element.262), channel_id=1, source_target_pairs={{0,2},{1,3},{2,0},{3,1},{4,6},{5,7},{6,4},{7,5},{8,10},{9,11},{10,... | collective-permute-start | bytes 344072 | tf_op jit(solution)/shard_map/ppermute | solution.py:29
  340.4 18.8 %collective-permute-start.110 = (bf16[256,224]{1,0:T(8,128)(2,1)S(1)}, bf16[256,224]{1,0:T(8,128)(2,1)S(1)}, u32[]{:S(2)}, u32[]{:S(2)}) collective-permute-start(bf16[256,224]{1,0:T(8,128)(2,1)S(1)} %get-tuple-element.268), channel_id=1, source_target_pairs={{64,34},{65,35},{66,32},{67,33},{68,38},{69,39},{70,36},{71,37},{7... | collective-permute-start | bytes 344072 | tf_op jit(solution)/shard_map/ppermute | solution.py:29
  341.7 18.8 %collective-permute-start.109 = (bf16[256,224]{1,0:T(8,128)(2,1)S(1)}, bf16[256,224]{1,0:T(8,128)(2,1)S(1)}, u32[]{:S(2)}, u32[]{:S(2)}) collective-permute-start(bf16[256,224]{1,0:T(8,128)(2,1)S(1)} %get-tuple-element.268), channel_id=1, source_target_pairs={{64,36},{65,37},{66,38},{67,39},{68,32},{69,33},{70,34},{71,35},{7... | collective-permute-start | bytes 344072 | tf_op jit(solution)/shard_map/ppermute | solution.py:29
  343.0 17.5 %collective-permute-start.108 = (bf16[256,224]{1,0:T(8,128)(2,1)S(1)}, bf16[256,224]{1,0:T(8,128)(2,1)S(1)}, u32[]{:S(2)}, u32[]{:S(2)}) collective-permute-start(bf16[256,224]{1,0:T(8,128)(2,1)S(1)} %get-tuple-element.268), channel_id=1, source_target_pairs={{64,48},{65,49},{66,50},{67,51},{68,52},{69,53},{70,54},{71,55},{7... | collective-permute-start | bytes 344072 | tf_op jit(solution)/shard_map/ppermute | solution.py:29
  344.3 16.3 %collective-permute-start.107 = (bf16[256,224]{1,0:T(8,128)(2,1)S(1)}, bf16[256,224]{1,0:T(8,128)(2,1)S(1)}, u32[]{:S(2)}, u32[]{:S(2)}) collective-permute-start(bf16[256,224]{1,0:T(8,128)(2,1)S(1)} %get-tuple-element.268), channel_id=1, source_target_pairs={{64,40},{65,41},{66,42},{67,43},{68,44},{69,45},{70,46},{71,47},{7... | collective-permute-start | bytes 344072 | tf_op jit(solution)/shard_map/ppermute | solution.py:29
  345.6 15.0 %collective-permute-start.106 = (bf16[256,224]{1,0:T(8,128)(2,1)S(1)}, bf16[256,224]{1,0:T(8,128)(2,1)S(1)}, u32[]{:S(2)}, u32[]{:S(2)}) collective-permute-start(bf16[256,224]{1,0:T(8,128)(2,1)S(1)} %get-tuple-element.268), channel_id=1, source_target_pairs={{64,33},{65,32},{66,35},{67,34},{68,37},{69,36},{70,39},{71,38},{7... | collective-permute-start | bytes 344072 | tf_op jit(solution)/shard_map/ppermute | solution.py:29
  410.2 13.9 %collective-permute-start.132 = (bf16[256,224]{1,0:T(8,128)(2,1)S(1)}, bf16[256,224]{1,0:T(8,128)(2,1)S(1)}, u32[]{:S(2)}, u32[]{:S(2)}) collective-permute-start(bf16[256,224]{1,0:T(8,128)(2,1)S(1)} %get-tuple-element.290), channel_id=1, source_target_pairs={{64,34},{65,35},{66,32},{67,33},{68,38},{69,39},{70,36},{71,37},{7... | collective-permute-start | bytes 344072 | tf_op jit(solution)/shard_map/ppermute | solution.py:29
  411.5 14.6 %collective-permute-start.131 = (bf16[256,224]{1,0:T(8,128)(2,1)S(1)}, bf16[256,224]{1,0:T(8,128)(2,1)S(1)}, u32[]{:S(2)}, u32[]{:S(2)}) collective-permute-start(bf16[256,224]{1,0:T(8,128)(2,1)S(1)} %get-tuple-element.290), channel_id=1, source_target_pairs={{64,36},{65,37},{66,38},{67,39},{68,32},{69,33},{70,34},{71,35},{7... | collective-permute-start | bytes 344072 | tf_op jit(solution)/shard_map/ppermute | solution.py:29
  412.8 13.3 %collective-permute-start.130 = (bf16[256,224]{1,0:T(8,128)(2,1)S(1)}, bf16[256,224]{1,0:T(8,128)(2,1)S(1)}, u32[]{:S(2)}, u32[]{:S(2)}) collective-permute-start(bf16[256,224]{1,0:T(8,128)(2,1)S(1)} %get-tuple-element.290), channel_id=1, source_target_pairs={{64,48},{65,49},{66,50},{67,51},{68,52},{69,53},{70,54},{71,55},{7... | collective-permute-start | bytes 344072 | tf_op jit(solution)/shard_map/ppermute | solution.py:29
  462.9 13.7 %collective-permute-start.144 = (bf16[256,224]{1,0:T(8,128)(2,1)S(1)}, bf16[256,224]{1,0:T(8,128)(2,1)S(1)}, u32[]{:S(2)}, u32[]{:S(2)}) collective-permute-start(bf16[256,224]{1,0:T(8,128)(2,1)S(1)} %get-tuple-element.306), channel_id=1, source_target_pairs={{0,2},{1,3},{2,0},{3,1},{4,6},{5,7},{6,4},{7,5},{8,10},{9,11},{10,... | collective-permute-start | bytes 344072 | tf_op jit(solution)/shard_map/ppermute | solution.py:29
  478.1 14.1 %collective-permute-start.154 = (bf16[256,224]{1,0:T(8,128)(2,1)S(1)}, bf16[256,224]{1,0:T(8,128)(2,1)S(1)}, u32[]{:S(2)}, u32[]{:S(2)}) collective-permute-start(bf16[256,224]{1,0:T(8,128)(2,1)S(1)} %get-tuple-element.312), channel_id=1, source_target_pairs={{64,34},{65,35},{66,32},{67,33},{68,38},{69,39},{70,36},{71,37},{7... | collective-permute-start | bytes 344072 | tf_op jit(solution)/shard_map/ppermute | solution.py:29
  479.4 14.1 %collective-permute-start.153 = (bf16[256,224]{1,0:T(8,128)(2,1)S(1)}, bf16[256,224]{1,0:T(8,128)(2,1)S(1)}, u32[]{:S(2)}, u32[]{:S(2)}) collective-permute-start(bf16[256,224]{1,0:T(8,128)(2,1)S(1)} %get-tuple-element.312), channel_id=1, source_target_pairs={{64,36},{65,37},{66,38},{67,39},{68,32},{69,33},{70,34},{71,35},{7... | collective-permute-start | bytes 344072 | tf_op jit(solution)/shard_map/ppermute | solution.py:29
  (161 other events, 1440.8 us)
